TPU v7x, 32 devices: a whole 2x2x4 slice. The times are simulated.
32 devices in a mesh: lat: 8 (over z, x), lon: 4 (over y, core).
Axes of the slice: x: 2, y: 2, z: 4, core: 2. Of those that a mesh axis runs over, the one named last changes fastest.
Arguments:
- state: float32 [64, 1440, 256], P('lat', 'lon'), may hold values from -6 to 6
- filter_flag: int32 [64], P('lat'), may hold values from 0 to 1, as said below
- cutoff: int32 [64], P('lat'), may hold values from 2 to 179
Outputs:
- state_new: float32 [64, 1440, 256], P('lat', 'lon')
Inputs may be any that keep to these rules, and one draw needn't show every extreme that they name: `filter_flag`: row j is flagged exactly when j < S or j >= 32 + S, for one S between 8 and 24.
All inputs are finite; a program needn't handle non-finite values.
Results may differ from a plain program's by a relative error of at most 0.000057.
Values sent between devices are 32-bit elements; how exact they have to be, the bound alone decides.
No kernel may reach another device: no remote copies, remote signals or barrier semaphores. Data moves between devices by JAX's collectives and lax.ppermute only.
A program may use at most 64 MiB of HBM per device.

v0:
```python
import functools
import math

import jax
import jax.numpy as jnp
import numpy as np
from jax import lax
from jax.experimental import pallas as pl
from jax.experimental.pallas import tpu as pltpu
from jax.sharding import PartitionSpec as P

WIND_COEF = 0.03
VERT_COEF = 0.2
PRESS_COEF = 0.03
LANES = 128
VMEM_BYTES = 40 * 1024 * 1024
FIRST = 3
MERID = 2
ZONAL_SPEC = 4
F32 = jnp.float32
BF16 = jnp.bfloat16


def split_np(table):
    high = table.astype(np.float32).astype(jnp.bfloat16)
    low = (table - high.astype(np.float64)).astype(np.float32).astype(jnp.bfloat16)
    return high, low


def round_up(value, step):
    return -(-value // step) * step


@functools.lru_cache(maxsize=None)
def spectral_plan(nlon):
    quarter = nlon // 4
    points = np.arange(quarter)
    waves0 = np.arange(0, nlon // 2 + 1, 4)
    waves2 = np.arange(2, nlon // 2 + 1, 4)
    waves1 = np.arange(1, nlon // 2 + 1, 2)
    size0 = round_up(len(waves0), 16)
    size2 = round_up(len(waves2), 16)
    size1 = round_up(len(waves1), 8)

    def trig(waves, size):
        angle = 2.0 * np.pi * ((waves[:, None] * points[None, :]) % nlon) / nlon
        cos_t, sin_t = np.zeros((2, size, quarter))
        cos_t[: len(waves)] = np.cos(angle)
        sin_t[: len(waves)] = np.sin(angle)
        return cos_t, sin_t

    def padded(values, size):
        out = np.zeros(size)
        out[: len(values)] = values
        return out

    def weights(waves, size):
        ends = (waves == 0) | (2 * waves == nlon)
        return padded(np.where(ends, 1.0, 2.0) / nlon, size)

    cos0, sin0 = trig(waves0, size0)
    cos2, sin2 = trig(waves2, size2)
    cos1, sin1 = trig(waves1, size1)
    turn = padded(np.where(waves1 % 4 == 1, 1.0, -1.0), size1)[:, None]
    fwd0 = np.concatenate([cos0, sin0], 0)
    fwd2 = np.concatenate([cos2, sin2], 0)
    fwd1 = np.block([[cos1, -turn * sin1], [sin1, turn * cos1]])
    inv0 = (fwd0 * np.tile(weights(waves0, size0), 2)[:, None]).T
    inv2 = (fwd2 * np.tile(weights(waves2, size2), 2)[:, None]).T
    inv1 = (fwd1 * np.tile(weights(waves1, size1), 2)[:, None]).T
    forward = [part for table in (fwd0, fwd2, fwd1) for part in split_np(table)]
    inverse = [part for table in (inv0, inv2, inv1) for part in split_np(table)]

    def columns(waves, size):
        inv_wave = padded(1.0 / np.maximum(waves, 1), size)
        delta = padded(np.sin(2.0 * np.pi * waves / nlon), size)
        return np.concatenate([inv_wave, inv_wave]), np.concatenate([delta, -delta])

    per_wave = [columns(w, s) for w, s in ((waves0, size0), (waves2, size2), (waves1, size1))]
    mode = np.stack([np.concatenate([c[0] for c in per_wave]), np.concatenate([c[1] for c in per_wave])], 1)
    mode = np.pad(mode.astype(np.float32), ((0, 0), (0, LANES - 2)))
    return forward, inverse, mode, (size0, size2, size1)


def lane_ids(shape):
    return lax.broadcasted_iota(jnp.int32, shape, len(shape) - 1)


def select_groups(values, masks):
    out = values[0]
    for mask, value in zip(masks[1:], values[1:]):
        out = jnp.where(mask, value, out)
    return out


def group_masks(size, part):
    group = lane_ids((size, LANES)) // part
    return [group == g for g in range(LANES // part)]


def transpose_groups(tiles, masks, part, wanted):
    count = len(tiles)
    turned = []
    for shift in range(count):
        mixed = select_groups([tiles[(shift + g) % count] for g in range(count)], masks)
        turned.append(pltpu.roll(mixed, shift * part, 1) if shift else mixed)
    return [select_groups([turned[(h - g) % count] for h in range(count)], masks) for g in wanted]


def partner_order(blocks, me):
    odd, far = lax.rem(me, 2) == 1, me >= 2
    a, b, c, d = blocks
    a, b, c, d = jnp.where(odd, b, a), jnp.where(odd, a, b), jnp.where(odd, d, c), jnp.where(odd, c, d)
    return [jnp.where(far, c, a), jnp.where(far, d, b), jnp.where(far, a, c), jnp.where(far, b, d)]


def chunk_of(size):
    return next(c for c in (24, 40, 16, 8) if size % c == 0)


def cut_value(flag_ref, cut_ref, row, nlon):
    return jnp.where(flag_ref[row] == 1, cut_ref[row], nlon).astype(F32)


def row_cosine(row, count):
    return jnp.sin((row.astype(F32) + 0.5) * (math.pi / count))


def levels_table(levels):
    shape = (2 * levels, 2 * levels)
    source = lax.broadcasted_iota(jnp.int32, shape, 0)
    target = lax.broadcasted_iota(jnp.int32, shape, 1)
    step = source % levels - target % levels
    diff = jnp.where(step == 1, 1.0, jnp.where(step == -1, -1.0, 0.0))
    rim = (target % levels == 0) | (target % levels == levels - 1)
    twice = jnp.where(step == 0, jnp.where(rim, -1.0, -2.0), jnp.where(abs(step) == 2, 1.0, 0.0))
    from_press, to_press = source >= levels, target >= levels
    table = jnp.where(from_press, jnp.where(to_press, twice, diff), jnp.where(to_press, -10.0 * diff, 0.0))
    return table.astype(BF16)


def first_kernel(part, wind_ref, tile_ref, *refs):
    packs, (vert_ref, both_ref) = refs[:4], refs[4:]
    rows, width, _ = tile_ref.shape
    levels = LANES // 2
    nlat = rows * lax.axis_size("lat")
    me = lax.axis_index("lon")
    first = lax.axis_index("lat") * rows
    low = lane_ids((width, LANES)) < levels
    place = lax.broadcasted_iota(jnp.int32, (width, LANES), 0)
    gain = jnp.where(lane_ids((1, LANES)) < levels, -0.5 * VERT_COEF, 0.25 * PRESS_COEF * VERT_COEF)
    table = levels_table(levels)
    dot = functools.partial(jnp.dot, preferred_element_type=F32)
    for row in range(rows):
        tile = tile_ref[row]
        high = tile.astype(BF16)
        rest = (tile - high.astype(F32)).astype(BF16)
        mixed = tile + gain * (dot(high, table) + dot(rest, table))
        vert_ref[row] = mixed
        after = jnp.where(place == width - 1, 0.0, pltpu.roll(tile, width - 1, 0))
        before = jnp.where(place == 0, 0.0, pltpu.roll(tile, 1, 0))
        scale = WIND_COEF / (2.0 * row_cosine(jnp.full((1, LANES), first + row), nlat))
        zonal = wind_ref[row] - pltpu.roll((after - before) * scale, levels, 1)
        both_ref[row] = jnp.where(low, zonal, mixed)

    size = chunk_of(width)
    masks = group_masks(size, part)

    def pack(step, carry):
        start = pl.multiple_of(step * size, 8)
        lines = pl.ds(start, size)
        blocks = transpose_groups([both_ref[row, lines] for row in range(rows)], masks, part, range(8))
        for ref, value in zip(packs, partner_order(blocks[4:], me)):
            ref[lines] = value
        for ref, value in zip(packs, partner_order(blocks[:4], me)):
            ref[pl.ds(start + width, size)] = value
        return carry

    lax.fori_loop(0, width // size, pack, 0)
    line = lax.broadcasted_iota(jnp.int32, (8, LANES), 0)
    sides = []
    for row in range(rows):
        side = jnp.where(line == 0, tile_ref[row, 0:8], 0.0)
        sides.append(jnp.where(line == 7, tile_ref[row, width - 8 : width], side))
    blocks = transpose_groups(sides, group_masks(8, part), part, range(4, 8))
    for ref, value in zip(packs, partner_order(blocks, me)):
        ref[2 * width :] = value


def rim_kernel(flag_ref, cut_ref, wind_ref, tile_ref, _, north_ref, south_ref):
    rows, width, _ = tile_ref.shape
    levels = LANES // 2
    nlon = width * lax.axis_size("lon")
    low = lane_ids((width, LANES)) < levels
    half = 0.5 * WIND_COEF
    last = rows - 1
    rim = wind_ref[last] + half * tile_ref[last - 1]
    north_ref[:width] = jnp.where(low, pltpu.roll(rim, levels, 1), tile_ref[last])
    rim = wind_ref[0] - half * tile_ref[1]
    south_ref[:width] = jnp.where(low, pltpu.roll(rim, levels, 1), tile_ref[0])
    north_ref[width:] = jnp.full((8, LANES), cut_value(flag_ref, cut_ref, last, nlon), F32)
    south_ref[width:] = jnp.full((8, LANES), cut_value(flag_ref, cut_ref, 0, nlon), F32)


def merid_kernel(part, wind_ref, tile_ref, south_ref, north_ref, *refs):
    outs, (merid_ref, rim_ref) = refs[:4], refs[4:]
    rows, width, _ = tile_ref.shape
    levels = LANES // 2
    me = lax.axis_index("lon")
    half = 0.5 * WIND_COEF
    for row in range(rows):
        above = north_ref[:width] if row == rows - 1 else tile_ref[row + 1]
        below = south_ref[:width] if row == 0 else tile_ref[row - 1]
        merid_ref[row] = wind_ref[row] - half * (above - below)
    lines = rim_ref.shape[1] // 4
    rim_ref[0, :width] = south_ref[:width] - half * pltpu.roll(tile_ref[0], levels, 1)
    rim_ref[1, :width] = north_ref[:width] + half * pltpu.roll(tile_ref[rows - 1], levels, 1)
    rim_ref[:, width:] = jnp.zeros((2, 4 * lines - width, LANES), F32)

    size = chunk_of(width)
    masks = group_masks(size, part)

    def pack(step, carry):
        where = pl.ds(pl.multiple_of(step * size, 8), size)
        blocks = transpose_groups([merid_ref[row, where] for row in range(rows)], masks, part, range(4, 8))
        for ref, value in zip(outs, partner_order(blocks, me)):
            ref[where] = value
        return carry

    lax.fori_loop(0, width // size, pack, 0)
    size = chunk_of(lines)
    masks = group_masks(size, part)
    for at in range(0, lines, size):
        tiles = [rim_ref[g % 2, g // 2 * lines + at : g // 2 * lines + at + size] for g in range(8)]
        blocks = transpose_groups(tiles, masks, part, range(4))
        for ref, value in zip(outs, partner_order(blocks, me)):
            ref[width + at : width + at + size] = value


def dot3(table_high, table_low, value):
    high = value.astype(BF16)
    low = (value - high.astype(F32)).astype(BF16)
    width = value.shape[1]
    dot = functools.partial(jnp.dot, preferred_element_type=F32)
    both = dot(table_high[...], jnp.concatenate([high, low], 1))
    return both[:, :width] + both[:, width:] + dot(table_low[...], high)


def by_place(me, dif0, dif1):
    odd = lax.rem(me, 2) == 1
    sign = jnp.where(me >= 2, -1.0, 1.0).astype(F32)
    return jnp.where(odd, dif1, dif0) * sign, jnp.where(odd, dif0, dif1) * sign


def parity_sign(me):
    return jnp.where(lax.rem(me, 2) == 1, -1.0, 1.0).astype(F32)


def forward_dft(quarters, tables):
    me = lax.axis_index("lon")
    own, core, chip, far = quarters
    sum0, sum1 = own + chip, core + far
    dif0, dif1 = by_place(me, own - chip, core - far)
    return (
        dot3(tables[0], tables[1], sum0 + sum1),
        dot3(tables[2], tables[3], (sum0 - sum1) * parity_sign(me)),
        dot3(tables[4], tables[5], jnp.concatenate([dif0, dif1], 0)),
    )


def inverse_dft(parts, tables, outs):
    me = lax.axis_index("lon")
    even = dot3(tables[0], tables[1], parts[0])
    other = dot3(tables[2], tables[3], parts[1]) * parity_sign(me)
    both = dot3(tables[4], tables[5], parts[2])
    quarter = even.shape[0]
    dif0, dif1 = by_place(me, both[:quarter], both[quarter:])
    plus, minus = even + other, even - other
    outs[0][...] = plus + dif0
    outs[1][...] = minus + dif1
    outs[2][...] = plus - dif0
    outs[3][...] = minus - dif1


def lane_rows(pick, rows, part):
    group = lane_ids((1, LANES)) // part
    out = jnp.zeros((1, LANES), F32)
    for row in range(rows):
        out = jnp.where(group == row, pick(row), out)
    return out


def lane_cut(flag_ref, cut_ref, nlon, part):
    rows = flag_ref.shape[0]
    return lane_rows(lambda row: cut_value(flag_ref, cut_ref, row, nlon), rows, part)


def lane_cosine(shift, rows, part):
    row = lane_ids((1, LANES)) // part + lax.axis_index("lat") * rows + shift
    return row_cosine(row, rows * lax.axis_size("lat"))


def damping(cut, inv_wave):
    ratio = cut * inv_wave
    return jnp.minimum(1.0, ratio * ratio)


def zonal_spec_kernel(bounds, part, flag_ref, cut_ref, mode_ref, q0, q1, q2, q3, *refs):
    forward, inverse, outs, (press_ref, spec_ref) = refs[:6], refs[6:12], refs[12:16], refs[16:]
    rows = flag_ref.shape[0]
    width = outs[0].shape[0]
    me = lax.axis_index("lon")
    quarters = (q0, q1, q2, q3)
    scale = WIND_COEF / (2.0 * lane_cosine(0, rows, part))
    line = lax.broadcasted_iota(jnp.int32, (8, LANES), 0)
    sides = partner_order([q[2 * width :] for q in quarters], me)
    starts = [jnp.where(line == 0, scale * pltpu.roll(sides[(q + 3) % 4], 1, 0), 0.0) for q in range(4)]
    ends = [jnp.where(line == 7, scale * pltpu.roll(sides[(q + 1) % 4], 7, 0), 0.0) for q in range(4)]
    starts, ends = partner_order(starts, me), partner_order(ends, me)
    fields = []
    for q, start, end in zip(quarters, starts, ends):
        middle = q[width + 8 : 2 * width - 8]
        zonal = jnp.concatenate([q[width : width + 8] + start, middle, q[2 * width - 8 : 2 * width] - end], 0)
        fields.append(jnp.concatenate([q[:width], zonal], 1))
    damp = damping(lane_cut(flag_ref, cut_ref, 4 * width, part), mode_ref[:, 0:1])
    parts = []
    for (low, high), value in zip(bounds, forward_dft(fields, forward)):
        press_ref[low:high] = value[:, :LANES]
        parts.append(value[:, LANES:] * damp[low:high])
        spec_ref[low:high] = parts[-1]
    inverse_dft(parts, inverse, outs)


def merid_spec_kernel(bounds, part, flag_ref, cut_ref, mode_ref, south_ref, north_ref, q0, q1, q2, q3, *refs):
    forward, inverse, outs, (spec_ref, rim_ref) = refs[:6], refs[6:12], refs[12:16], refs[16:]
    width = outs[0].shape[0]
    fields = []
    for q in (q0, q1, q2, q3):
        value = q[width:]
        pieces = [pltpu.roll(value, LANES - 2 * part * g, 1) if g else value for g in range(4)]
        fields.append(jnp.concatenate([q[:width], jnp.concatenate(pieces, 0)[:width]], 1))
    group = lane_ids((1, LANES)) // part
    rim_cut = jnp.where(group == 0, south_ref[0:1], jnp.where(group == 1, north_ref[0:1], 0.0))
    inv_wave = mode_ref[:, 0:1]
    damp = damping(lane_cut(flag_ref, cut_ref, 4 * width, part), inv_wave)
    rim_damp = damping(rim_cut, inv_wave)
    parts = []
    for (low, high), value in zip(bounds, forward_dft(fields, forward)):
        rim_ref[low:high] = value[:, LANES:] * rim_damp[low:high]
        parts.append(value[:, :LANES] * damp[low:high])
        spec_ref[low:high] = parts[-1]
    inverse_dft(parts, inverse, outs)


def press_back_kernel(bounds, part, flag_ref, cut_ref, mode_ref, spec_ref, zonal_ref, merid_ref, rim_ref, *refs):
    inverse, outs = refs[:6], refs[6:10]
    rows = flag_ref.shape[0]
    nlon = 4 * inverse[0].shape[0]
    band = lax.axis_index("lat")
    mode = mode_ref[...]
    damp = damping(lane_cut(flag_ref, cut_ref, nlon, part), mode[:, 0:1])
    cosine = lane_cosine(0, rows, part)
    below = jnp.where(band == 0, 0.0, lane_cosine(-1, rows, part))
    above = jnp.where(band == lax.axis_size("lat") - 1, 0.0, lane_cosine(1, rows, part))
    half_inv = 0.5 / cosine
    group = lane_ids((1, LANES)) // part
    flux = merid_ref[...] * cosine
    rim = rim_ref[...]
    north = jnp.where(group == rows - 1, pltpu.roll(rim, (rows - 2) * part, 1) * above, pltpu.roll(flux, LANES - part, 1))
    south = jnp.where(group == 0, rim * below, pltpu.roll(flux, part, 1))
    div_y = (north - south) * half_inv
    zonal = zonal_ref[...]
    slope = mode[:, 1:2] / cosine
    parts = []
    for low, high in bounds:
        mid = (low + high) // 2
        swapped = jnp.concatenate([zonal[mid:high], zonal[low:mid]], 0)
        div = swapped * slope[low:high] + div_y[low:high]
        parts.append((spec_ref[low:high] - PRESS_COEF * div) * damp[low:high])
    inverse_dft(parts, inverse, outs)


def winds_out_kernel(part, *refs):
    blocks, out_ref = refs[:8], refs[8]
    rows, width, _ = out_ref.shape
    me = lax.axis_index("lon")
    size = chunk_of(width)
    masks = group_masks(size, part)

    def unpack(step, carry):
        lines = pl.ds(pl.multiple_of(step * size, 8), size)
        values = [ref[lines] for ref in blocks]
        values = partner_order(values[:4], me) + partner_order(values[4:], me)
        for row, value in enumerate(transpose_groups(values, masks, part, range(rows))):
            out_ref[row, lines] = value
        return carry

    lax.fori_loop(0, width // size, unpack, 0)


def press_out_kernel(part, _, tile_ref, *refs):
    blocks, out_ref = refs[:4], refs[4]
    rows, width, _ = out_ref.shape
    me = lax.axis_index("lon")
    size = chunk_of(width)
    masks = group_masks(size, part)
    low = lane_ids((size, LANES)) < LANES // 2

    def unpack(step, carry):
        lines = pl.ds(pl.multiple_of(step * size, 8), size)
        values = partner_order([ref[lines] for ref in blocks], me)
        for row, value in enumerate(transpose_groups(values + values, masks, part, range(rows))):
            out_ref[row, lines] = jnp.where(low, tile_ref[row, lines], value)
        return carry

    lax.fori_loop(0, width // size, unpack, 0)


def whole(shape):
    return pl.BlockSpec(shape, lambda step: (0,) * len(shape))


def tile_of(shape, index):
    return pl.BlockSpec((shape[0], shape[1], LANES), lambda step: (0, 0, index))


SMEM = pl.BlockSpec(memory_space=pltpu.SMEM)
ANY = pl.BlockSpec(memory_space=pl.ANY)


def call(kernel, out_shape, in_specs, out_specs, cost=1, grid=(1,), **more):
    return pl.pallas_call(
        kernel,
        grid=grid,
        out_shape=out_shape,
        in_specs=in_specs,
        out_specs=out_specs,
        compiler_params=pltpu.CompilerParams(vmem_limit_bytes=VMEM_BYTES),
        cost_estimate=pl.CostEstimate(flops=0, bytes_accessed=int(cost * 3.69e6), transcendentals=0),
        **more,
    )


def f32(*shape):
    return jax.ShapeDtypeStruct(shape, F32)


def exchange(blocks):
    pairs = [[(i, i ^ step) for i in range(4)] for step in range(4)]
    return [blocks[0]] + [lax.ppermute(blocks[step], "lon", pairs[step]) for step in range(1, 4)]


def packed_body(state, filter_flag, cutoff):
    rows, width, depth = state.shape
    levels = depth // 4
    bands = lax.axis_size("lat")
    nlon = 4 * width
    part = levels // 4
    forward, inverse, mode, sizes = spectral_plan(nlon)
    forward = [jnp.asarray(t) for t in forward]
    inverse = [jnp.asarray(t) for t in inverse]
    mode = jnp.asarray(mode)
    bounds, at = [], 0
    for size in sizes:
        bounds.append((at, at + 2 * size))
        at += 2 * size
    table_specs = [whole(t.shape) for t in forward] + [whole(t.shape) for t in inverse]
    block, spectrum = (width, LANES), (at, LANES)
    sided = (width + 8, LANES)
    rimmed = (width + round_up(-(-width // 4), 8), LANES)
    double = (2 * width + 8, LANES)
    full = (rows, width, LANES)
    low_tile, high_tile = tile_of(state.shape, 0), tile_of(state.shape, 1)

    *packs, vert = call(
        functools.partial(first_kernel, part),
        [f32(*double)] * 4 + [f32(*full)],
        [low_tile, high_tile],
        [whole(double)] * 4 + [whole(full)],
        cost=FIRST,
        scratch_shapes=[pltpu.VMEM(full, F32)],
    )(state, state)
    circle = exchange(packs)
    to_north, to_south = call(
        rim_kernel,
        [f32(*sided)] * 2,
        [SMEM] * 2 + [low_tile, high_tile, ANY],
        [whole(sided)] * 2,
    )(filter_flag, cutoff, state, state, vert)
    from_south = lax.ppermute(to_north, "lat", [(i, i + 1) for i in range(bands - 1)])
    from_north = lax.ppermute(to_south, "lat", [(i + 1, i) for i in range(bands - 1)])

    merid_packs = call(
        functools.partial(merid_kernel, part),
        [f32(*rimmed)] * 4,
        [low_tile, high_tile, whole(sided), whole(sided)],
        [whole(rimmed)] * 4,
        cost=MERID,
        scratch_shapes=[pltpu.VMEM(full, F32), pltpu.VMEM((2, 4 * (rimmed[0] - width), LANES), F32)],
    )(state, state, from_south, from_north)
    merid_circle = exchange(merid_packs)

    *zonal_parts, press_spec, zonal_spec = call(
        functools.partial(zonal_spec_kernel, bounds, part),
        [f32(*block)] * 4 + [f32(*spectrum)] * 2,
        [SMEM] * 2 + [whole(mode.shape)] + [whole(double)] * 4 + table_specs,
        [whole(block)] * 4 + [whole(spectrum)] * 2,
        cost=ZONAL_SPEC,
    )(filter_flag, cutoff, mode, *circle, *forward, *inverse)
    zonal_back = exchange(zonal_parts)

    last_lines = pl.BlockSpec((8, LANES), lambda step: (width // 8, 0))
    *merid_parts, merid_spec, rim_spec = call(
        functools.partial(merid_spec_kernel, bounds, part),
        [f32(*block)] * 4 + [f32(*spectrum)] * 2,
        [SMEM] * 2 + [whole(mode.shape), last_lines, last_lines] + [whole(rimmed)] * 4 + table_specs,
        [whole(block)] * 4 + [whole(spectrum)] * 2,
    )(filter_flag, cutoff, mode, from_south, from_north, *merid_circle, *forward, *inverse)
    merid_back = exchange(merid_parts)

    press_parts = call(
        functools.partial(press_back_kernel, bounds, part),
        [f32(*block)] * 4,
        [SMEM] * 2 + [whole(mode.shape)] + [whole(spectrum)] * 4 + table_specs[6:],
        [whole(block)] * 4,
    )(filter_flag, cutoff, mode, press_spec, zonal_spec, merid_spec, rim_spec, *inverse)
    press_back = exchange(press_parts)

    steps = next(s for s in (3, 5, 1) if width % (8 * s) == 0)
    piece = pl.BlockSpec((width // steps, LANES), lambda step: (step, 0))

    def slab(index):
        return pl.BlockSpec((rows, width // steps, LANES), lambda step: (0, step, index))

    out = call(
        functools.partial(winds_out_kernel, part),
        f32(*state.shape),
        [piece] * 8,
        slab(0),
        grid=(steps,),
    )(*zonal_back, *merid_back)
    return call(
        functools.partial(press_out_kernel, part),
        f32(*state.shape),
        [ANY, slab(0)] + [piece] * 4,
        slab(1),
        grid=(steps,),
        input_output_aliases={0: 0},
    )(out, vert, *press_back)


def padded_2(block, sides, width, periodic):
    for axis, dim in sides:
        count = lax.axis_size(axis)
        forward = [(i, i + 1) for i in range(count - 1)]
        if periodic:
            forward.append((count - 1, 0))
        backward = [(target, source) for source, target in forward]
        low = lax.ppermute(
            lax.slice_in_dim(block, block.shape[dim] - width, None, axis=dim), axis, forward
        )
        high = lax.ppermute(lax.slice_in_dim(block, 0, width, axis=dim), axis, backward)
        block = jnp.concatenate([low, block, high], axis=dim)
    return block


def dft_tables(width):
    points = jnp.arange(width, dtype=jnp.int32)
    waves = jnp.arange(width // 2 + 1, dtype=jnp.int32)
    phase = points[:, None] * waves[None, :] % width
    angle = phase.astype(jnp.float32) * (2.0 * math.pi / width)
    weights = jnp.where((waves == 0) | (waves * 2 == width), 1.0, 2.0).astype(jnp.float32) / width
    return (jnp.cos(angle), jnp.sin(angle), weights)


def rims(stack):
    wide = padded_2(stack, (("lon", 1),), 1, True)
    return padded_2(wide, (("lat", 0),), 1, False)


def level_diff(field):
    padded = jnp.pad(field, ((0, 0), (0, 0), (1, 1)))
    return 0.5 * (padded[:, :, 2:] - padded[:, :, :-2])


def damped(block, cut_vec, tables):
    cos_table, sin_table, weights = tables
    highest = lax.Precision.HIGHEST
    wave_vals = jnp.arange(cos_table.shape[1]).astype(jnp.float32)
    ratio = cut_vec[:, None] / jnp.maximum(wave_vals, 1.0)[None, :]
    damping = (jnp.minimum(1.0, ratio * ratio) * weights[None, :])[:, None, :]
    real_part = jnp.einsum("rnq,nk->rqk", block, cos_table, precision=highest)
    imag_part = jnp.einsum("rnq,nk->rqk", block, sin_table, precision=highest)
    restored = jnp.einsum("rqk,nk->rnq", real_part * damping, cos_table, precision=highest)
    return restored + jnp.einsum("rqk,nk->rnq", imag_part * damping, sin_table, precision=highest)


def circle_local(fields, cut_rows, tables):
    return damped(fields, cut_rows, tables)


def polar(fields, row_flag, cut_rows, tables, apply):
    smooth = apply(fields, cut_rows, tables)
    return jnp.where(row_flag[:, None, None], smooth, fields)


def plain_body(state, filter_flag, cutoff):
    rows, width, depth = state.shape
    levels = depth // 4
    zonal_wind = state[:, :, :levels]
    merid_wind = state[:, :, levels : 2 * levels]
    vert_wind = state[:, :, 2 * levels : 3 * levels]
    pressure = state[:, :, 3 * levels :]
    nlat = rows * lax.axis_size("lat")
    nlon = width * lax.axis_size("lon")
    offset = lax.axis_index("lat") * rows
    row_ids = (offset + jnp.arange(-1, rows + 1)).astype(jnp.float32)
    cos_ext = jnp.cos(-0.5 * math.pi + (row_ids + 0.5) * math.pi / nlat)
    cos_mid = cos_ext[1:-1][:, None, None]
    tables = dft_tables(nlon)
    row_flag = filter_flag == 1
    cut_rows = cutoff.astype(jnp.float32)
    padded = rims(pressure)
    grad_x = (padded[1:-1, 2:] - padded[1:-1, :-2]) / (2.0 * cos_mid)
    grad_y = 0.5 * (padded[2:, 1:-1] - padded[:-2, 1:-1])
    grad_z = level_diff(pressure)
    zonal_pre = zonal_wind - WIND_COEF * grad_x
    merid_pre = merid_wind - WIND_COEF * grad_y
    vert_new = vert_wind - VERT_COEF * grad_z
    div_z = level_diff(vert_new)
    outgoing = jnp.stack([zonal_pre, merid_pre, pressure, div_z], 3).reshape(
        rows, width, 4 * levels
    )
    circles = lax.all_to_all(outgoing, "lon", split_axis=2, concat_axis=1, tiled=True)
    part_levels = circles.shape[2] // 4
    circles = circles.reshape(rows, nlon, part_levels, 4)
    winds_c = jnp.concatenate([circles[:, :, :, 0], circles[:, :, :, 1]], 2)
    press_c = circles[:, :, :, 2]
    div_z_c = circles[:, :, :, 3]
    winds_c = polar(winds_c, row_flag, cut_rows, tables, circle_local)
    zonal_c = winds_c[:, :, :part_levels]
    merid_c = winds_c[:, :, part_levels:]
    div_x = (jnp.roll(zonal_c, -1, 1) - jnp.roll(zonal_c, 1, 1)) / (2.0 * cos_mid)
    flux = padded_2(merid_c * cos_mid, (("lat", 0),), 1, False)
    div_y = (flux[2:] - flux[:-2]) / (2.0 * cos_mid)
    press_mid = press_c - PRESS_COEF * (div_x + div_y + div_z_c)
    press_c = polar(press_mid, row_flag, cut_rows, tables, circle_local)
    back = jnp.stack([zonal_c, merid_c, press_c], 3).reshape(rows, nlon, 3 * part_levels)
    patches = lax.all_to_all(back, "lon", split_axis=1, concat_axis=2, tiled=True).reshape(
        rows, width, levels, 3
    )
    return jnp.concatenate(
        [patches[:, :, :, 0], patches[:, :, :, 1], vert_new, patches[:, :, :, 2]], 2
    )


def body(state, filter_flag, cutoff):
    rows, width, depth = state.shape
    levels = depth // 4
    lanes_fit = rows == 8 and 2 * levels == LANES and width % 8 == 0
    if lax.axis_size("lon") == 4 and lanes_fit:
        return packed_body(state, filter_flag, cutoff)
    return plain_body(state, filter_flag, cutoff)


def solution(mesh):
    return jax.shard_map(
        body,
        mesh=mesh,
        in_specs=(P("lat", "lon", None), P("lat"), P("lat")),
        out_specs=P("lat", "lon", None),
        check_vma=False,
    )
```

profile of v0, /device:TPU:17, one launch (start us, length us, event | category | flops | bytes accessed | tf_op | source)
XLA Modules:
  0.0 67.7 jit_solution(10750068323515296164)
XLA Ops:
  0.0 1.8 %copy-done = f32[8,360,256]{2,1,0:T(8,128)S(1)} copy-done((f32[8,360,256]{2,1,0:T(8,128)S(1)}, f32[8,360,256]{2,1,0:T(8,128)}, u32[]{:S(2)}) %copy-start) | copy-done | bytes 2949144
  1.8 2.8 %shard_map.154 = (f32[728,128]{1,0:T(8,128)S(1)}, f32[728,128]{1,0:T(8,128)S(1)}, f32[728,128]{1,0:T(8,128)S(1)}, f32[728,128]{1,0:T(8,128)S(1)}, f32[8,360,128]{2,1,0:T(8,128)S(1)}) custom-call(f32[8,360,256]{2,1,0:T(8,128)S(1)} %copy-done, f32[8,360,256]{2,1,0:T(8,128)S(1)} %copy-done), custom_call_target="tpu_custom_call" | custom-call | bytes 11070000 | tf_op jit(solution)/shard_map/pallas_call | solution.py:475
  6.2 3.1 %collective-permute-start.6 = (f32[368,128]{1,0:T(8,128)S(1)}, f32[368,128]{1,0:T(8,128)S(1)}, u32[]{:S(2)}, u32[]{:S(2)}) collective-permute-start(f32[368,128]{1,0:T(8,128)S(1)} %get-tuple-element.41), channel_id=1, source_target_pairs={{0,4},{4,8},{8,12},{12,16},{16,20},{20,24},{24,28},{1,5},{5,9},{9,... | collective-permute-start | bytes 565256 | tf_op jit(solution)/shard_map/ppermute | solution.py:490
  9.3 3.1 %collective-permute-start.7 = (f32[368,128]{1,0:T(8,128)S(1)}, f32[368,128]{1,0:T(8,128)S(1)}, u32[]{:S(2)}, u32[]{:S(2)}) collective-permute-start(f32[368,128]{1,0:T(8,128)S(1)} %get-tuple-element.42), channel_id=1, source_target_pairs={{4,0},{8,4},{12,8},{16,12},{20,16},{24,20},{28,24},{5,1},{9,5},{13... | collective-permute-start | bytes 565256 | tf_op jit(solution)/shard_map/ppermute | solution.py:491
  12.4 1.3 %collective-permute-start.1 = (f32[728,128]{1,0:T(8,128)S(1)}, f32[728,128]{1,0:T(8,128)S(1)}, u32[]{:S(2)}, u32[]{:S(2)}) collective-permute-start(f32[728,128]{1,0:T(8,128)S(1)} %get-tuple-element.34), channel_id=1, source_target_pairs={{0,2},{1,3},{2,0},{3,1},{4,6},{5,7},{6,4},{7,5},{8,10},{9,11},{10,... | collective-permute-start | bytes 1118216 | tf_op jit(solution)/shard_map/ppermute | solution.py:450
  13.8 1.1 %collective-permute-start.2 = (f32[728,128]{1,0:T(8,128)S(1)}, f32[728,128]{1,0:T(8,128)S(1)}, u32[]{:S(2)}, u32[]{:S(2)}) collective-permute-start(f32[728,128]{1,0:T(8,128)S(1)} %get-tuple-element.35), channel_id=1, source_target_pairs={{0,3},{1,2},{2,1},{3,0},{4,7},{5,6},{6,5},{7,4},{8,11},{9,10},{10,... | collective-permute-start | bytes 1118216 | tf_op jit(solution)/shard_map/ppermute | solution.py:450
  15.3 4.4 %collective-permute-done.7.north_ref = f32[368,128]{1,0:T(8,128)S(1)} collective-permute-done((f32[368,128]{1,0:T(8,128)S(1)}, f32[368,128]{1,0:T(8,128)S(1)}, u32[]{:S(2)}, u32[]{:S(2)}) %collective-permute-start.7) | collective-permute-done | bytes 188448 | tf_op jit(solution)/shard_map/ppermute | solution.py:491
  19.7 2.0 %shard_map.157 = (f32[456,128]{1,0:T(8,128)S(1)}, f32[456,128]{1,0:T(8,128)S(1)}, f32[456,128]{1,0:T(8,128)S(1)}, f32[456,128]{1,0:T(8,128)S(1)}) custom-call(f32[8,360,256]{2,1,0:T(8,128)S(1)} %copy-done, f32[8,360,256]{2,1,0:T(8,128)S(1)} %copy-done, f32[368,128]{1,0:T(8,128)S(1)} %collective-permute-done.6.south_ref, ...), custom_call_target="tpu_custom_call" | custom-call | bytes 7380000 | tf_op jit(solution)/shard_map/pallas_call | solution.py:493
  22.2 1.3 %collective-permute-start.9 = (f32[456,128]{1,0:T(8,128)S(1)}, f32[456,128]{1,0:T(8,128)S(1)}, u32[]{:S(2)}, u32[]{:S(2)}) collective-permute-start(f32[456,128]{1,0:T(8,128)S(1)} %get-tuple-element.45), channel_id=1, source_target_pairs={{0,2},{1,3},{2,0},{3,1},{4,6},{5,7},{6,4},{7,5},{8,10},{9,11},{10,... | collective-permute-start | bytes 700424 | tf_op jit(solution)/shard_map/ppermute | solution.py:450
  23.9 8.0 %collective-permute-done.2.q3 = f32[728,128]{1,0:T(8,128)S(1)} collective-permute-done((f32[728,128]{1,0:T(8,128)S(1)}, f32[728,128]{1,0:T(8,128)S(1)}, u32[]{:S(2)}, u32[]{:S(2)}) %collective-permute-start.2) | collective-permute-done | bytes 372768 | tf_op jit(solution)/shard_map/ppermute | solution.py:450
  32.0 4.1 %shard_map.155 = (f32[360,128]{1,0:T(8,128)S(1)}, f32[360,128]{1,0:T(8,128)S(1)}, f32[360,128]{1,0:T(8,128)S(1)}, f32[360,128]{1,0:T(8,128)S(1)}, f32[1488,128]{1,0:T(8,128)S(1)}, /*index=5*/f32[1488,128]{1,0:T(8,128)S(1)}) custom-call(s32[8]{0:T(128)S(1)} %copy-done.14, s32[8]{0:T(128)S(1)} %copy-done.15, f32[1488,128]{1,0:T(8,128)S(1)} %copy-done.3, ...), custom_call_target="tpu_custom_call" | custom-call | bytes 14760000 | tf_op jit(solution)/shard_map/pallas_call | solution.py:503
  36.2 1.3 %collective-permute-start.4 = (f32[360,128]{1,0:T(8,128)S(1)}, f32[360,128]{1,0:T(8,128)S(1)}, u32[]{:S(2)}, u32[]{:S(2)}) collective-permute-start(f32[360,128]{1,0:T(8,128)S(1)} %get-tuple-element.38), channel_id=1, source_target_pairs={{0,2},{1,3},{2,0},{3,1},{4,6},{5,7},{6,4},{7,5},{8,10},{9,11},{10,... | collective-permute-start | bytes 552968 | tf_op jit(solution)/shard_map/ppermute | solution.py:450
  38.3 3.6 %collective-permute-done.10.q3 = f32[456,128]{1,0:T(8,128)S(1)} collective-permute-done((f32[456,128]{1,0:T(8,128)S(1)}, f32[456,128]{1,0:T(8,128)S(1)}, u32[]{:S(2)}, u32[]{:S(2)}) %collective-permute-start.10) | collective-permute-done | bytes 233504 | tf_op jit(solution)/shard_map/ppermute | solution.py:450
  41.9 4.1 %shard_map.158 = (f32[360,128]{1,0:T(8,128)S(1)}, f32[360,128]{1,0:T(8,128)S(1)}, f32[360,128]{1,0:T(8,128)S(1)}, f32[360,128]{1,0:T(8,128)S(1)}, f32[1488,128]{1,0:T(8,128)S(1)}, /*index=5*/f32[1488,128]{1,0:T(8,128)S(1)}) custom-call(s32[8]{0:T(128)S(1)} %copy-done.14, s32[8]{0:T(128)S(1)} %copy-done.15, f32[1488,128]{1,0:T(8,128)S(1)} %copy-done.3, ...), custom_call_target="tpu_custom_call" | custom-call | bytes 3690000 | tf_op jit(solution)/shard_map/pallas_call | solution.py:513
  46.1 1.3 %collective-permute-start.12 = (f32[360,128]{1,0:T(8,128)S(1)}, f32[360,128]{1,0:T(8,128)S(1)}, u32[]{:S(2)}, u32[]{:S(2)}) collective-permute-start(f32[360,128]{1,0:T(8,128)S(1)} %get-tuple-element.49), channel_id=1, source_target_pairs={{0,2},{1,3},{2,0},{3,1},{4,6},{5,7},{6,4},{7,5},{8,10},{9,11},{10,... | collective-permute-start | bytes 552968 | tf_op jit(solution)/shard_map/ppermute | solution.py:450
  47.4 2.2 %shard_map.160 = (f32[360,128]{1,0:T(8,128)S(1)}, f32[360,128]{1,0:T(8,128)S(1)}, f32[360,128]{1,0:T(8,128)S(1)}, f32[360,128]{1,0:T(8,128)S(1)}) custom-call(s32[8]{0:T(128)S(1)} %copy-done.14, s32[8]{0:T(128)S(1)} %copy-done.15, f32[1488,128]{1,0:T(8,128)S(1)} %copy-done.3, f32[1488,128]{1,0:T(8,128)S(1)} %get-tuple-element.51.spec_ref, ...), custom_call_target="tpu_custom_call" | custom-call | bytes 3690000 | tf_op jit(solution)/shard_map/pallas_call | solution.py:521
  49.6 0.9 %collective-permute-start.13 = (f32[360,128]{1,0:T(8,128)S(1)}, f32[360,128]{1,0:T(8,128)S(1)}, u32[]{:S(2)}, u32[]{:S(2)}) collective-permute-start(f32[360,128]{1,0:T(8,128)S(1)} %get-tuple-element.50), channel_id=1, source_target_pairs={{0,3},{1,2},{2,1},{3,0},{4,7},{5,6},{6,5},{7,4},{8,11},{9,10},{10,... | collective-permute-start | bytes 552968 | tf_op jit(solution)/shard_map/ppermute | solution.py:450
  50.5 1.3 %collective-permute-start.15 = (f32[360,128]{1,0:T(8,128)S(1)}, f32[360,128]{1,0:T(8,128)S(1)}, u32[]{:S(2)}, u32[]{:S(2)}) collective-permute-start(f32[360,128]{1,0:T(8,128)S(1)} %get-tuple-element.57), channel_id=1, source_target_pairs={{0,2},{1,3},{2,0},{3,1},{4,6},{5,7},{6,4},{7,5},{8,10},{9,11},{10,... | collective-permute-start | bytes 552968 | tf_op jit(solution)/shard_map/ppermute | solution.py:450
  51.9 0.8 %collective-permute-start.16 = (f32[360,128]{1,0:T(8,128)S(1)}, f32[360,128]{1,0:T(8,128)S(1)}, u32[]{:S(2)}, u32[]{:S(2)}) collective-permute-start(f32[360,128]{1,0:T(8,128)S(1)} %get-tuple-element.58), channel_id=1, source_target_pairs={{0,3},{1,2},{2,1},{3,0},{4,7},{5,6},{6,5},{7,4},{8,11},{9,10},{10,... | collective-permute-start | bytes 552968 | tf_op jit(solution)/shard_map/ppermute | solution.py:450
  52.7 4.2 %collective-permute-done.13.refs_7_ = f32[360,128]{1,0:T(8,128)S(1)} collective-permute-done((f32[360,128]{1,0:T(8,128)S(1)}, f32[360,128]{1,0:T(8,128)S(1)}, u32[]{:S(2)}, u32[]{:S(2)}) %collective-permute-start.13) | collective-permute-done | bytes 184352 | tf_op jit(solution)/shard_map/ppermute | solution.py:450
  56.9 2.8 %shard_map.159._ = f32[8,360,256]{2,1,0:T(8,128)} custom-call(f32[360,128]{1,0:T(8,128)S(1)} %get-tuple-element.36.refs_0_, f32[360,128]{1,0:T(8,128)S(1)} %collective-permute-done.3.refs_1_, f32[360,128]{1,0:T(8,128)S(1)} %collective-permute-done.4.refs_2_, f32[360,128]{1,0:T(8,128)S(1)} %collective-permute-done.5.refs_3_, ...), custom_call_target="tpu_custom_call" | custom-call | bytes 3690000 | tf_op jit(solution)/shard_map/pallas_call | solution.py:535
  59.7 1.2 %collective-permute-done.15.refs_2_ = f32[360,128]{1,0:T(8,128)S(1)} collective-permute-done((f32[360,128]{1,0:T(8,128)S(1)}, f32[360,128]{1,0:T(8,128)S(1)}, u32[]{:S(2)}, u32[]{:S(2)}) %collective-permute-start.15) | collective-permute-done | bytes 184352 | tf_op jit(solution)/shard_map/ppermute | solution.py:450
  60.9 3.9 %collective-permute-done.16.refs_3_ = f32[360,128]{1,0:T(8,128)S(1)} collective-permute-done((f32[360,128]{1,0:T(8,128)S(1)}, f32[360,128]{1,0:T(8,128)S(1)}, u32[]{:S(2)}, u32[]{:S(2)}) %collective-permute-start.16) | collective-permute-done | bytes 184352 | tf_op jit(solution)/shard_map/ppermute | solution.py:450
  64.8 2.8 %shard_map.161 = f32[8,360,256]{2,1,0:T(8,128)} custom-call(f32[8,360,256]{2,1,0:T(8,128)} %shard_map.159._, f32[8,360,128]{2,1,0:T(8,128)S(1)} %get-tuple-element.40._.tile_ref, f32[360,128]{1,0:T(8,128)S(1)} %get-tuple-element.55.refs_0_, f32[360,128]{1,0:T(8,128)S(1)} %collective-permute-done.14.refs_1_, ...), custom_call_target="tpu_custom_call", output_to_operand_aliasing={{}: (0, {})} | custom-call | bytes 3690000 | tf_op jit(solution)/shard_map/pallas_call | solution.py:542
  (50 shorter events, 4.0 us)
Async XLA Ops:
  4.7 18.8 %collective-permute-start = (f32[728,128]{1,0:T(8,128)S(1)}, f32[728,128]{1,0:T(8,128)S(1)}, u32[]{:S(2)}, u32[]{:S(2)}) collective-permute-start(f32[728,128]{1,0:T(8,128)S(1)} %get-tuple-element.33), channel_id=1, source_target_pairs={{0,1},{1,0},{2,3},{3,2},{4,5},{5,4},{6,7},{7,6},{8,9},{9,8},{10,11... | collective-permute-start | bytes 1118216 | tf_op jit(solution)/shard_map/ppermute | solution.py:450
  5.4 26.5 %copy-start.9 = (bf16[360,384]{1,0:T(8,128)(2,1)S(1)}, bf16[360,384]{1,0:T(8,128)(2,1)}, u32[]{:S(2)}) copy-start(bf16[360,384]{1,0:T(8,128)(2,1)} %constant.32.clone.refs_6_.refs_0_) | copy-start | bytes 829444
  5.4 26.5 %copy-start.10 = (bf16[384,360]{1,0:T(8,128)(2,1)S(1)}, bf16[384,360]{1,0:T(8,128)(2,1)}, u32[]{:S(2)}) copy-start(bf16[384,360]{1,0:T(8,128)(2,1)} %constant.29.clone.refs_3_) | copy-start | bytes 829444
  5.4 26.5 %copy-start.11 = (bf16[384,360]{1,0:T(8,128)(2,1)S(1)}, bf16[384,360]{1,0:T(8,128)(2,1)}, u32[]{:S(2)}) copy-start(bf16[384,360]{1,0:T(8,128)(2,1)} %constant.28.clone.refs_2_) | copy-start | bytes 829444
  5.5 26.5 %copy-start.12 = (bf16[384,360]{1,0:T(8,128)(2,1)S(1)}, bf16[384,360]{1,0:T(8,128)(2,1)}, u32[]{:S(2)}) copy-start(bf16[384,360]{1,0:T(8,128)(2,1)} %constant.27.clone.refs_1_) | copy-start | bytes 829444
  5.5 26.5 %copy-start.13 = (bf16[384,360]{1,0:T(8,128)(2,1)S(1)}, bf16[384,360]{1,0:T(8,128)(2,1)}, u32[]{:S(2)}) copy-start(bf16[384,360]{1,0:T(8,128)(2,1)} %constant.26.clone.refs_0_) | copy-start | bytes 829444
  6.2 9.1 %collective-permute-start.6 = (f32[368,128]{1,0:T(8,128)S(1)}, f32[368,128]{1,0:T(8,128)S(1)}, u32[]{:S(2)}, u32[]{:S(2)}) collective-permute-start(f32[368,128]{1,0:T(8,128)S(1)} %get-tuple-element.41), channel_id=1, source_target_pairs={{0,4},{4,8},{8,12},{12,16},{16,20},{20,24},{24,28},{1,5},{5,9},{9,... | collective-permute-start | bytes 565256 | tf_op jit(solution)/shard_map/ppermute | solution.py:490
  9.3 10.4 %collective-permute-start.7 = (f32[368,128]{1,0:T(8,128)S(1)}, f32[368,128]{1,0:T(8,128)S(1)}, u32[]{:S(2)}, u32[]{:S(2)}) collective-permute-start(f32[368,128]{1,0:T(8,128)S(1)} %get-tuple-element.42), channel_id=1, source_target_pairs={{4,0},{8,4},{12,8},{16,12},{20,16},{24,20},{28,24},{5,1},{9,5},{13... | collective-permute-start | bytes 565256 | tf_op jit(solution)/shard_map/ppermute | solution.py:491
  12.4 11.5 %collective-permute-start.1 = (f32[728,128]{1,0:T(8,128)S(1)}, f32[728,128]{1,0:T(8,128)S(1)}, u32[]{:S(2)}, u32[]{:S(2)}) collective-permute-start(f32[728,128]{1,0:T(8,128)S(1)} %get-tuple-element.34), channel_id=1, source_target_pairs={{0,2},{1,3},{2,0},{3,1},{4,6},{5,7},{6,4},{7,5},{8,10},{9,11},{10,... | collective-permute-start | bytes 1118216 | tf_op jit(solution)/shard_map/ppermute | solution.py:450
  13.7 18.3 %copy-start.5 = (bf16[720,720]{1,0:T(8,128)(2,1)S(1)}, bf16[720,720]{1,0:T(8,128)(2,1)}, u32[]{:S(2)}) copy-start(bf16[720,720]{1,0:T(8,128)(2,1)} %constant.30.clone.refs_4_) | copy-start | bytes 3110404
  13.7 18.3 %copy-start.6 = (bf16[360,384]{1,0:T(8,128)(2,1)S(1)}, bf16[360,384]{1,0:T(8,128)(2,1)}, u32[]{:S(2)}) copy-start(bf16[360,384]{1,0:T(8,128)(2,1)} %constant.35.clone.refs_9_.refs_3_) | copy-start | bytes 829444
  13.8 18.1 %collective-permute-start.2 = (f32[728,128]{1,0:T(8,128)S(1)}, f32[728,128]{1,0:T(8,128)S(1)}, u32[]{:S(2)}, u32[]{:S(2)}) collective-permute-start(f32[728,128]{1,0:T(8,128)S(1)} %get-tuple-element.35), channel_id=1, source_target_pairs={{0,3},{1,2},{2,1},{3,0},{4,7},{5,6},{6,5},{7,4},{8,11},{9,10},{10,... | collective-permute-start | bytes 1118216 | tf_op jit(solution)/shard_map/ppermute | solution.py:450
  21.6 15.9 %collective-permute-start.8 = (f32[456,128]{1,0:T(8,128)S(1)}, f32[456,128]{1,0:T(8,128)S(1)}, u32[]{:S(2)}, u32[]{:S(2)}) collective-permute-start(f32[456,128]{1,0:T(8,128)S(1)} %get-tuple-element.44), channel_id=1, source_target_pairs={{0,1},{1,0},{2,3},{3,2},{4,5},{5,4},{6,7},{7,6},{8,9},{9,8},{10,11... | collective-permute-start | bytes 700424 | tf_op jit(solution)/shard_map/ppermute | solution.py:450
  22.2 16.2 %collective-permute-start.9 = (f32[456,128]{1,0:T(8,128)S(1)}, f32[456,128]{1,0:T(8,128)S(1)}, u32[]{:S(2)}, u32[]{:S(2)}) collective-permute-start(f32[456,128]{1,0:T(8,128)S(1)} %get-tuple-element.45), channel_id=1, source_target_pairs={{0,2},{1,3},{2,0},{3,1},{4,6},{5,7},{6,4},{7,5},{8,10},{9,11},{10,... | collective-permute-start | bytes 700424 | tf_op jit(solution)/shard_map/ppermute | solution.py:450
  23.4 18.5 %collective-permute-start.10 = (f32[456,128]{1,0:T(8,128)S(1)}, f32[456,128]{1,0:T(8,128)S(1)}, u32[]{:S(2)}, u32[]{:S(2)}) collective-permute-start(f32[456,128]{1,0:T(8,128)S(1)} %get-tuple-element.46), channel_id=1, source_target_pairs={{0,3},{1,2},{2,1},{3,0},{4,7},{5,6},{6,5},{7,4},{8,11},{9,10},{10,... | collective-permute-start | bytes 700424 | tf_op jit(solution)/shard_map/ppermute | solution.py:450
  36.1 13.5 %collective-permute-start.3 = (f32[360,128]{1,0:T(8,128)S(1)}, f32[360,128]{1,0:T(8,128)S(1)}, u32[]{:S(2)}, u32[]{:S(2)}) collective-permute-start(f32[360,128]{1,0:T(8,128)S(1)} %get-tuple-element.37), channel_id=1, source_target_pairs={{0,1},{1,0},{2,3},{3,2},{4,5},{5,4},{6,7},{7,6},{8,9},{9,8},{10,11... | collective-permute-start | bytes 552968 | tf_op jit(solution)/shard_map/ppermute | solution.py:450
  36.2 14.3 %collective-permute-start.4 = (f32[360,128]{1,0:T(8,128)S(1)}, f32[360,128]{1,0:T(8,128)S(1)}, u32[]{:S(2)}, u32[]{:S(2)}) collective-permute-start(f32[360,128]{1,0:T(8,128)S(1)} %get-tuple-element.38), channel_id=1, source_target_pairs={{0,2},{1,3},{2,0},{3,1},{4,6},{5,7},{6,4},{7,5},{8,10},{9,11},{10,... | collective-permute-start | bytes 552968 | tf_op jit(solution)/shard_map/ppermute | solution.py:450
  37.5 13.0 %collective-permute-start.5 = (f32[360,128]{1,0:T(8,128)S(1)}, f32[360,128]{1,0:T(8,128)S(1)}, u32[]{:S(2)}, u32[]{:S(2)}) collective-permute-start(f32[360,128]{1,0:T(8,128)S(1)} %get-tuple-element.39), channel_id=1, source_target_pairs={{0,3},{1,2},{2,1},{3,0},{4,7},{5,6},{6,5},{7,4},{8,11},{9,10},{10,... | collective-permute-start | bytes 552968 | tf_op jit(solution)/shard_map/ppermute | solution.py:450
  46.0 5.8 %collective-permute-start.11 = (f32[360,128]{1,0:T(8,128)S(1)}, f32[360,128]{1,0:T(8,128)S(1)}, u32[]{:S(2)}, u32[]{:S(2)}) collective-permute-start(f32[360,128]{1,0:T(8,128)S(1)} %get-tuple-element.48), channel_id=1, source_target_pairs={{0,1},{1,0},{2,3},{3,2},{4,5},{5,4},{6,7},{7,6},{8,9},{9,8},{10,11... | collective-permute-start | bytes 552968 | tf_op jit(solution)/shard_map/ppermute | solution.py:450
  46.1 6.6 %collective-permute-start.12 = (f32[360,128]{1,0:T(8,128)S(1)}, f32[360,128]{1,0:T(8,128)S(1)}, u32[]{:S(2)}, u32[]{:S(2)}) collective-permute-start(f32[360,128]{1,0:T(8,128)S(1)} %get-tuple-element.49), channel_id=1, source_target_pairs={{0,2},{1,3},{2,0},{3,1},{4,6},{5,7},{6,4},{7,5},{8,10},{9,11},{10,... | collective-permute-start | bytes 552968 | tf_op jit(solution)/shard_map/ppermute | solution.py:450
  49.6 7.3 %collective-permute-start.13 = (f32[360,128]{1,0:T(8,128)S(1)}, f32[360,128]{1,0:T(8,128)S(1)}, u32[]{:S(2)}, u32[]{:S(2)}) collective-permute-start(f32[360,128]{1,0:T(8,128)S(1)} %get-tuple-element.50), channel_id=1, source_target_pairs={{0,3},{1,2},{2,1},{3,0},{4,7},{5,6},{6,5},{7,4},{8,11},{9,10},{10,... | collective-permute-start | bytes 552968 | tf_op jit(solution)/shard_map/ppermute | solution.py:450
  50.5 9.1 %collective-permute-start.14 = (f32[360,128]{1,0:T(8,128)S(1)}, f32[360,128]{1,0:T(8,128)S(1)}, u32[]{:S(2)}, u32[]{:S(2)}) collective-permute-start(f32[360,128]{1,0:T(8,128)S(1)} %get-tuple-element.56), channel_id=1, source_target_pairs={{0,1},{1,0},{2,3},{3,2},{4,5},{5,4},{6,7},{7,6},{8,9},{9,8},{10,11... | collective-permute-start | bytes 552968 | tf_op jit(solution)/shard_map/ppermute | solution.py:450
  50.5 10.3 %collective-permute-start.15 = (f32[360,128]{1,0:T(8,128)S(1)}, f32[360,128]{1,0:T(8,128)S(1)}, u32[]{:S(2)}, u32[]{:S(2)}) collective-permute-start(f32[360,128]{1,0:T(8,128)S(1)} %get-tuple-element.57), channel_id=1, source_target_pairs={{0,2},{1,3},{2,0},{3,1},{4,6},{5,7},{6,4},{7,5},{8,10},{9,11},{10,... | collective-permute-start | bytes 552968 | tf_op jit(solution)/shard_map/ppermute | solution.py:450
  51.9 13.0 %collective-permute-start.16 = (f32[360,128]{1,0:T(8,128)S(1)}, f32[360,128]{1,0:T(8,128)S(1)}, u32[]{:S(2)}, u32[]{:S(2)}) collective-permute-start(f32[360,128]{1,0:T(8,128)S(1)} %get-tuple-element.58), channel_id=1, source_target_pairs={{0,3},{1,2},{2,1},{3,0},{4,7},{5,6},{6,5},{7,4},{8,11},{9,10},{10,... | collective-permute-start | bytes 552968 | tf_op jit(solution)/shard_map/ppermute | solution.py:450
  (9 other events, 118.6 us)
where the time goes:
time: 67.8 us; the launch traced here: 67.7 us
  waiting for transfers between devices  25.8 us (38%)
  Pallas kernels  21.5 us (32%)
  starting transfers between devices  18.1 us (27%)
  local copies, waits for them, and re-layouts  1.91 us (3%)
    ppermute x15, waiting for transfers between devices, exchange(): lax.ppermute(blocks[step], 'lon', pairs[step])  21 us
    ppermute x15, starting transfers between devices, exchange(): lax.ppermute(blocks[step], 'lon', pairs[step])  12 us
    ppermute x1, waiting for transfers between devices, packed_body(): lax.ppermute(to_south, 'lat', [(i + 1, i) for i in range(bands - 1)])  4.39 us
    pallas_call x1, Pallas kernels, packed_body(): call(functools.partial(zonal_spec_kernel, bounds, part), [f32(*block)] *...  4.1 us
    pallas_call x1, Pallas kernels, packed_body(): call(functools.partial(merid_spec_kernel, bounds, part), [f32(*block)] *...  4.1 us
    ppermute x1, starting transfers between devices, packed_body(): lax.ppermute(to_north, 'lat', [(i, i + 1) for i in range(bands - 1)])  3.12 us
    ppermute x1, starting transfers between devices, packed_body(): lax.ppermute(to_south, 'lat', [(i + 1, i) for i in range(bands - 1)])  3.06 us
    pallas_call x1, Pallas kernels, packed_body(): call(functools.partial(first_kernel, part), [f32(*double)] * 4 + [f32(*fu...  2.84 us
  transfers between devices with their start and end apart: 17, of which 7 were waited for; matrix products, arithmetic and copies ran while one was open for 0% of the time, Pallas kernels for 23%

commit v1 on v0

--- a/solution.py
+++ b/solution.py
@@ -14,9 +14,6 @@
 PRESS_COEF = 0.03
 LANES = 128
 VMEM_BYTES = 40 * 1024 * 1024
-FIRST = 3
-MERID = 2
-ZONAL_SPEC = 4
 F32 = jnp.float32
 BF16 = jnp.bfloat16
 
@@ -139,15 +136,104 @@
     return table.astype(BF16)
 
 
-def first_kernel(part, wind_ref, tile_ref, *refs):
-    packs, (vert_ref, both_ref) = refs[:4], refs[4:]
+def each_chunk(size, step, work, **loop):
+    def turn(index, carry):
+        work(pl.multiple_of(index * step, 8))
+        return carry
+
+    lax.fori_loop(0, size // step, turn, 0, **loop)
+
+
+def put(refs, start, values):
+    for ref, value in zip(refs, values):
+        ref[pl.ds(start, value.shape[0])] = value
+
+
+def merid_row(wind_ref, tile_ref, row, lines):
+    half = 0.5 * WIND_COEF
+    value = wind_ref[row, lines]
+    if row < tile_ref.shape[0] - 1:
+        value = value - half * tile_ref[row + 1, lines]
+    return value + half * tile_ref[row - 1, lines] if row else value
+
+
+def zonal_kernel(part, wind_ref, tile_ref, *refs):
+    packs, zonal_ref = refs[:4], refs[4]
     rows, width, _ = tile_ref.shape
+    last = rows - 1
     levels = LANES // 2
     nlat = rows * lax.axis_size("lat")
     me = lax.axis_index("lon")
     first = lax.axis_index("lat") * rows
-    low = lane_ids((width, LANES)) < levels
     place = lax.broadcasted_iota(jnp.int32, (width, LANES), 0)
+    for row in range(rows):
+        tile = tile_ref[row]
+        after = jnp.where(place == width - 1, 0.0, pltpu.roll(tile, width - 1, 0))
+        before = jnp.where(place == 0, 0.0, pltpu.roll(tile, 1, 0))
+        scale = WIND_COEF / (2.0 * row_cosine(jnp.full((1, LANES), first + row), nlat))
+        zonal_ref[row] = wind_ref[row] - pltpu.roll((after - before) * scale, levels, 1)
+
+    size = chunk_of(width)
+    masks = group_masks(size, part)
+
+    def pack(start):
+        lines = pl.ds(start, size)
+        blocks = transpose_groups([zonal_ref[row, lines] for row in range(rows)], masks, part, range(4))
+        put(packs, start, partner_order(blocks, me))
+
+    each_chunk(width, size, pack)
+    line = lax.broadcasted_iota(jnp.int32, (8, LANES), 0)
+    sides = []
+    for row in range(rows):
+        side = jnp.where(line == 0, tile_ref[row, 0:8], 0.0)
+        sides.append(jnp.where(line == 7, tile_ref[row, width - 8 : width], side))
+    masks8 = group_masks(8, part)
+    put(packs, width, partner_order(transpose_groups(sides, masks8, part, range(4, 8)), me))
+
+    head = rim_lines(width)
+
+    def pack_rim(start):
+        tiles = []
+        for begin in (start, jnp.minimum(start + head, width - 8)):
+            lines = pl.ds(pl.multiple_of(begin, 8), 8)
+            for row in (0, last):
+                tiles += [merid_row(wind_ref, tile_ref, row, lines), tile_ref[row, lines]]
+        put(packs, width + 8 + start, partner_order(transpose_groups(tiles, masks8, part, range(4, 8)), me))
+
+    each_chunk(head, 8, pack_rim, unroll=True)
+
+
+def rim_lines(width):
+    return round_up(-(-width // 2), 8)
+
+
+def fold_lines(width):
+    return round_up(-(-width * 3 // 4), 8)
+
+
+def press_kernel(part, wind_ref, tile_ref, *refs):
+    packs, vert_ref = refs[:4], refs[4]
+    rows, width, _ = tile_ref.shape
+    levels = LANES // 2
+    me = lax.axis_index("lon")
+    masks8 = group_masks(8, part)
+    head = fold_lines(width)
+    tail = width - head
+
+    def pack_merid(start, pair, fold=None):
+        lines = pl.ds(start, 8)
+        folded = pl.ds(start - pair * tail + head if fold is None else fold, 8)
+        tiles = [merid_row(wind_ref, tile_ref, row, lines) for row in range(1, rows - 1)]
+        one = merid_row(wind_ref, tile_ref, 2 * pair + 1, folded)
+        two = merid_row(wind_ref, tile_ref, 2 * pair + 2, folded)
+        blocks = transpose_groups([one] + tiles + [two], masks8, part, range(4, 8))
+        put(packs, start, partner_order(blocks, me))
+
+    for pair in range(3):
+        each_chunk(tail, 8, lambda start: pack_merid(pl.multiple_of(start + pair * tail, 8), pair), unroll=True)
+    for start in range(3 * tail, head, 8):
+        pack_merid(start, 2, start)
+
     gain = jnp.where(lane_ids((1, LANES)) < levels, -0.5 * VERT_COEF, 0.25 * PRESS_COEF * VERT_COEF)
     table = levels_table(levels)
     dot = functools.partial(jnp.dot, preferred_element_type=F32)
@@ -155,86 +241,91 @@
         tile = tile_ref[row]
         high = tile.astype(BF16)
         rest = (tile - high.astype(F32)).astype(BF16)
-        mixed = tile + gain * (dot(high, table) + dot(rest, table))
-        vert_ref[row] = mixed
-        after = jnp.where(place == width - 1, 0.0, pltpu.roll(tile, width - 1, 0))
-        before = jnp.where(place == 0, 0.0, pltpu.roll(tile, 1, 0))
-        scale = WIND_COEF / (2.0 * row_cosine(jnp.full((1, LANES), first + row), nlat))
-        zonal = wind_ref[row] - pltpu.roll((after - before) * scale, levels, 1)
-        both_ref[row] = jnp.where(low, zonal, mixed)
+        vert_ref[row] = tile + gain * (dot(high, table) + dot(rest, table))
 
     size = chunk_of(width)
     masks = group_masks(size, part)
 
-    def pack(step, carry):
-        start = pl.multiple_of(step * size, 8)
+    def pack(start):
         lines = pl.ds(start, size)
-        blocks = transpose_groups([both_ref[row, lines] for row in range(rows)], masks, part, range(8))
-        for ref, value in zip(packs, partner_order(blocks[4:], me)):
-            ref[lines] = value
-        for ref, value in zip(packs, partner_order(blocks[:4], me)):
-            ref[pl.ds(start + width, size)] = value
-        return carry
-
-    lax.fori_loop(0, width // size, pack, 0)
-    line = lax.broadcasted_iota(jnp.int32, (8, LANES), 0)
-    sides = []
-    for row in range(rows):
-        side = jnp.where(line == 0, tile_ref[row, 0:8], 0.0)
-        sides.append(jnp.where(line == 7, tile_ref[row, width - 8 : width], side))
-    blocks = transpose_groups(sides, group_masks(8, part), part, range(4, 8))
-    for ref, value in zip(packs, partner_order(blocks, me)):
-        ref[2 * width :] = value
-
-
-def rim_kernel(flag_ref, cut_ref, wind_ref, tile_ref, _, north_ref, south_ref):
-    rows, width, _ = tile_ref.shape
-    levels = LANES // 2
-    nlon = width * lax.axis_size("lon")
-    low = lane_ids((width, LANES)) < levels
+        blocks = transpose_groups([vert_ref[row, lines] for row in range(rows)], masks, part, range(4, 8))
+        put(packs, pl.multiple_of(start + head, 8), partner_order(blocks, me))
+
+    each_chunk(width, size, pack)
+
+
+def turn_groups(value, groups, part):
+    shift = groups * part % LANES
+    return pltpu.roll(value, shift, 1) if shift else value
+
+
+def rim_kernel(part, skip, flag_ref, cut_ref, *refs):
+    blocks, north_ref, south_ref = refs[:4], refs[4], refs[5]
+    lines = blocks[0].shape[0] - skip
+    first = lane_ids((lines, LANES)) // part % 4 < 2
+    for half in range(2):
+        one, two = blocks[2 * half][skip:], blocks[2 * half + 1][skip:]
+        where = slice(half * lines, half * lines + lines)
+        south_ref[where] = jnp.where(first, one, turn_groups(two, 2, part))
+        north_ref[where] = jnp.where(first, turn_groups(two, -2, part), one)
+    last = flag_ref.shape[0] - 1
+    nlon = (skip - 8) * 4
+    north_ref[2 * lines :] = jnp.full((8, LANES), cut_value(flag_ref, cut_ref, last, nlon), F32)
+    south_ref[2 * lines :] = jnp.full((8, LANES), cut_value(flag_ref, cut_ref, 0, nlon), F32)
+
+
+def edge_spec_kernel(bounds, part, skip, flag_ref, cut_ref, mode_ref, south_ref, north_ref, *refs):
+    blocks, forward, spec_ref = refs[:4], refs[4:10], refs[10]
+    lines = blocks[0].shape[0] - skip
+    width = skip - 8
     half = 0.5 * WIND_COEF
-    last = rows - 1
-    rim = wind_ref[last] + half * tile_ref[last - 1]
-    north_ref[:width] = jnp.where(low, pltpu.roll(rim, levels, 1), tile_ref[last])
-    rim = wind_ref[0] - half * tile_ref[1]
-    south_ref[:width] = jnp.where(low, pltpu.roll(rim, levels, 1), tile_ref[0])
-    north_ref[width:] = jnp.full((8, LANES), cut_value(flag_ref, cut_ref, last, nlon), F32)
-    south_ref[width:] = jnp.full((8, LANES), cut_value(flag_ref, cut_ref, 0, nlon), F32)
-
-
-def merid_kernel(part, wind_ref, tile_ref, south_ref, north_ref, *refs):
-    outs, (merid_ref, rim_ref) = refs[:4], refs[4:]
-    rows, width, _ = tile_ref.shape
-    levels = LANES // 2
-    me = lax.axis_index("lon")
-    half = 0.5 * WIND_COEF
-    for row in range(rows):
-        above = north_ref[:width] if row == rows - 1 else tile_ref[row + 1]
-        below = south_ref[:width] if row == 0 else tile_ref[row - 1]
-        merid_ref[row] = wind_ref[row] - half * (above - below)
-    lines = rim_ref.shape[1] // 4
-    rim_ref[0, :width] = south_ref[:width] - half * pltpu.roll(tile_ref[0], levels, 1)
-    rim_ref[1, :width] = north_ref[:width] + half * pltpu.roll(tile_ref[rows - 1], levels, 1)
-    rim_ref[:, width:] = jnp.zeros((2, 4 * lines - width, LANES), F32)
-
-    size = chunk_of(width)
-    masks = group_masks(size, part)
-
-    def pack(step, carry):
-        where = pl.ds(pl.multiple_of(step * size, 8), size)
-        blocks = transpose_groups([merid_ref[row, where] for row in range(rows)], masks, part, range(4, 8))
-        for ref, value in zip(outs, partner_order(blocks, me)):
-            ref[where] = value
-        return carry
-
-    lax.fori_loop(0, width // size, pack, 0)
-    size = chunk_of(lines)
-    masks = group_masks(size, part)
-    for at in range(0, lines, size):
-        tiles = [rim_ref[g % 2, g // 2 * lines + at : g // 2 * lines + at + size] for g in range(8)]
-        blocks = transpose_groups(tiles, masks, part, range(4))
-        for ref, value in zip(outs, partner_order(blocks, me)):
-            ref[width + at : width + at + size] = value
+    item = lane_ids((lines, LANES)) // part % 4
+    fields = []
+    for quarter, block in enumerate(blocks):
+        where = slice(quarter // 2 * lines, quarter // 2 * lines + lines)
+        own, south, north = block[skip:], south_ref[where], north_ref[where]
+        at = 0 if quarter % 2 else 2
+        merid_s, press_s = turn_groups(south, 1 - at, part), turn_groups(south, -1 - at, part)
+        merid_n, press_n = turn_groups(north, 1 + at, part), turn_groups(north, at - 1, part)
+        inner = own + half * jnp.where(item == 0, press_s, -press_n)
+        outer = jnp.where(item == 1, merid_s - half * own, merid_n + half * own)
+        value = jnp.where(item % 2 == 0, inner, outer)
+        fields.append(jnp.concatenate([value, turn_groups(value, -4, part)], 0)[:width])
+    rows = flag_ref.shape[0]
+    group = lane_ids((1, LANES)) // part
+    cut = jnp.where(group == 0, cut_value(flag_ref, cut_ref, 0, 4 * width), cut_value(flag_ref, cut_ref, rows - 1, 4 * width))
+    cut = jnp.where(group == 1, south_ref[2 * lines : 2 * lines + 1], cut)
+    cut = jnp.where(group == 3, north_ref[2 * lines : 2 * lines + 1], cut)
+    damp = damping(cut, mode_ref[:, 0:1])
+    for (low, high), value in zip(bounds, forward_dft(fields, forward)):
+        spec_ref[low:high] = value * damp[low:high]
+
+
+def merid_spec_kernel(bounds, part, flag_ref, cut_ref, mode_ref, edge_ref, _, *refs):
+    blocks, forward, inverse, outs, spec_ref = refs[:4], refs[4:10], refs[10:16], refs[16:20], refs[20]
+    rows = flag_ref.shape[0]
+    width = outs[0].shape[0]
+    head = fold_lines(width)
+    tail = width - head
+    group = lane_ids((tail, LANES)) // part
+    fields = []
+    for block in blocks:
+        out = None
+        for pair in range(3):
+            value = block[pair * tail : pair * tail + tail]
+            one, two = turn_groups(value, 2 * pair + 1, part), turn_groups(value, 2 * pair + 3, part)
+            both = jnp.where(group == 2 * pair + 1, one, two)
+            out = both if pair == 0 else jnp.where(group > 2 * pair, both, out)
+        fields.append(jnp.concatenate([block[:head], out], 0))
+    damp = damping(lane_cut(flag_ref, cut_ref, 4 * width, part), mode_ref[:, 0:1])
+    group = lane_ids((1, LANES)) // part
+    parts = []
+    for (low, high), value in zip(bounds, forward_dft(fields, forward)):
+        edge = edge_ref[low:high]
+        value = jnp.where(group == 0, edge, value * damp[low:high])
+        parts.append(jnp.where(group == rows - 1, turn_groups(edge, rows - 3, part), value))
+        spec_ref[low:high] = parts[-1]
+    inverse_dft(parts, inverse, outs)
 
 
 def dot3(table_high, table_low, value):
@@ -306,54 +397,31 @@
 
 
 def zonal_spec_kernel(bounds, part, flag_ref, cut_ref, mode_ref, q0, q1, q2, q3, *refs):
-    forward, inverse, outs, (press_ref, spec_ref) = refs[:6], refs[6:12], refs[12:16], refs[16:]
+    forward, inverse, outs, spec_ref = refs[:6], refs[6:12], refs[12:16], refs[16]
     rows = flag_ref.shape[0]
     width = outs[0].shape[0]
     me = lax.axis_index("lon")
     quarters = (q0, q1, q2, q3)
     scale = WIND_COEF / (2.0 * lane_cosine(0, rows, part))
     line = lax.broadcasted_iota(jnp.int32, (8, LANES), 0)
-    sides = partner_order([q[2 * width :] for q in quarters], me)
+    sides = partner_order([q[width : width + 8] for q in quarters], me)
     starts = [jnp.where(line == 0, scale * pltpu.roll(sides[(q + 3) % 4], 1, 0), 0.0) for q in range(4)]
     ends = [jnp.where(line == 7, scale * pltpu.roll(sides[(q + 1) % 4], 7, 0), 0.0) for q in range(4)]
     starts, ends = partner_order(starts, me), partner_order(ends, me)
-    fields = []
-    for q, start, end in zip(quarters, starts, ends):
-        middle = q[width + 8 : 2 * width - 8]
-        zonal = jnp.concatenate([q[width : width + 8] + start, middle, q[2 * width - 8 : 2 * width] - end], 0)
-        fields.append(jnp.concatenate([q[:width], zonal], 1))
+    fields = [
+        jnp.concatenate([q[0:8] + start, q[8 : width - 8], q[width - 8 : width] - end], 0)
+        for q, start, end in zip(quarters, starts, ends)
+    ]
     damp = damping(lane_cut(flag_ref, cut_ref, 4 * width, part), mode_ref[:, 0:1])
-    parts = []
-    for (low, high), value in zip(bounds, forward_dft(fields, forward)):
-        press_ref[low:high] = value[:, :LANES]
-        parts.append(value[:, LANES:] * damp[low:high])
-        spec_ref[low:high] = parts[-1]
+    parts = [value * damp[b[0] : b[1]] for b, value in zip(bounds, forward_dft(fields, forward))]
+    for (low, high), value in zip(bounds, parts):
+        spec_ref[low:high] = value
     inverse_dft(parts, inverse, outs)
 
 
-def merid_spec_kernel(bounds, part, flag_ref, cut_ref, mode_ref, south_ref, north_ref, q0, q1, q2, q3, *refs):
-    forward, inverse, outs, (spec_ref, rim_ref) = refs[:6], refs[6:12], refs[12:16], refs[16:]
-    width = outs[0].shape[0]
-    fields = []
-    for q in (q0, q1, q2, q3):
-        value = q[width:]
-        pieces = [pltpu.roll(value, LANES - 2 * part * g, 1) if g else value for g in range(4)]
-        fields.append(jnp.concatenate([q[:width], jnp.concatenate(pieces, 0)[:width]], 1))
-    group = lane_ids((1, LANES)) // part
-    rim_cut = jnp.where(group == 0, south_ref[0:1], jnp.where(group == 1, north_ref[0:1], 0.0))
-    inv_wave = mode_ref[:, 0:1]
-    damp = damping(lane_cut(flag_ref, cut_ref, 4 * width, part), inv_wave)
-    rim_damp = damping(rim_cut, inv_wave)
-    parts = []
-    for (low, high), value in zip(bounds, forward_dft(fields, forward)):
-        rim_ref[low:high] = value[:, LANES:] * rim_damp[low:high]
-        parts.append(value[:, :LANES] * damp[low:high])
-        spec_ref[low:high] = parts[-1]
-    inverse_dft(parts, inverse, outs)
-
-
-def press_back_kernel(bounds, part, flag_ref, cut_ref, mode_ref, spec_ref, zonal_ref, merid_ref, rim_ref, *refs):
-    inverse, outs = refs[:6], refs[6:10]
+def press_back_kernel(bounds, part, flag_ref, cut_ref, mode_ref, zonal_ref, merid_ref, edge_ref, *refs):
+    quarters, forward, inverse, outs = refs[:4], refs[4:10], refs[10:16], refs[16:]
+    skip = quarters[0].shape[0] - outs[0].shape[0]
     rows = flag_ref.shape[0]
     nlon = 4 * inverse[0].shape[0]
     band = lax.axis_index("lat")
@@ -365,18 +433,18 @@
     half_inv = 0.5 / cosine
     group = lane_ids((1, LANES)) // part
     flux = merid_ref[...] * cosine
-    rim = rim_ref[...]
-    north = jnp.where(group == rows - 1, pltpu.roll(rim, (rows - 2) * part, 1) * above, pltpu.roll(flux, LANES - part, 1))
-    south = jnp.where(group == 0, rim * below, pltpu.roll(flux, part, 1))
+    edge = edge_ref[...]
+    north = jnp.where(group == rows - 1, turn_groups(edge, rows - 4, part) * above, turn_groups(flux, -1, part))
+    south = jnp.where(group == 0, turn_groups(edge, -1, part) * below, turn_groups(flux, 1, part))
     div_y = (north - south) * half_inv
     zonal = zonal_ref[...]
     slope = mode[:, 1:2] / cosine
     parts = []
-    for low, high in bounds:
+    for (low, high), press in zip(bounds, forward_dft([q[skip:] for q in quarters], forward)):
         mid = (low + high) // 2
         swapped = jnp.concatenate([zonal[mid:high], zonal[low:mid]], 0)
         div = swapped * slope[low:high] + div_y[low:high]
-        parts.append((spec_ref[low:high] - PRESS_COEF * div) * damp[low:high])
+        parts.append((press - PRESS_COEF * div) * damp[low:high])
     inverse_dft(parts, inverse, outs)
 
 
@@ -428,7 +496,7 @@
 ANY = pl.BlockSpec(memory_space=pl.ANY)
 
 
-def call(kernel, out_shape, in_specs, out_specs, cost=1, grid=(1,), **more):
+def call(kernel, out_shape, in_specs, out_specs, cost=2, grid=(1,), **more):
     return pl.pallas_call(
         kernel,
         grid=grid,
@@ -465,65 +533,67 @@
         bounds.append((at, at + 2 * size))
         at += 2 * size
     table_specs = [whole(t.shape) for t in forward] + [whole(t.shape) for t in inverse]
-    block, spectrum = (width, LANES), (at, LANES)
-    sided = (width + 8, LANES)
-    rimmed = (width + round_up(-(-width // 4), 8), LANES)
-    double = (2 * width + 8, LANES)
-    full = (rows, width, LANES)
+    block, spectrum, full = (width, LANES), (at, LANES), (rows, width, LANES)
+    skip = width + 8
+    first = (skip + rim_lines(width), LANES)
+    second = (fold_lines(width) + width, LANES)
+    rims = (2 * rim_lines(width) + 8, LANES)
     low_tile, high_tile = tile_of(state.shape, 0), tile_of(state.shape, 1)
 
+    first_circle = exchange(
+        call(
+            functools.partial(zonal_kernel, part),
+            [f32(*first)] * 4,
+            [low_tile, high_tile],
+            [whole(first)] * 4,
+            scratch_shapes=[pltpu.VMEM(full, F32)],
+        )(state, state)
+    )
     *packs, vert = call(
-        functools.partial(first_kernel, part),
-        [f32(*double)] * 4 + [f32(*full)],
+        functools.partial(press_kernel, part),
+        [f32(*second)] * 4 + [f32(*full)],
         [low_tile, high_tile],
-        [whole(double)] * 4 + [whole(full)],
-        cost=FIRST,
-        scratch_shapes=[pltpu.VMEM(full, F32)],
+        [whole(second)] * 4 + [whole(full)],
     )(state, state)
-    circle = exchange(packs)
+    second_circle = exchange(packs)
+
     to_north, to_south = call(
-        rim_kernel,
-        [f32(*sided)] * 2,
-        [SMEM] * 2 + [low_tile, high_tile, ANY],
-        [whole(sided)] * 2,
-    )(filter_flag, cutoff, state, state, vert)
+        functools.partial(rim_kernel, part, skip),
+        [f32(*rims)] * 2,
+        [SMEM] * 2 + [whole(first)] * 4,
+        [whole(rims)] * 2,
+    )(filter_flag, cutoff, *first_circle)
     from_south = lax.ppermute(to_north, "lat", [(i, i + 1) for i in range(bands - 1)])
     from_north = lax.ppermute(to_south, "lat", [(i + 1, i) for i in range(bands - 1)])
 
-    merid_packs = call(
-        functools.partial(merid_kernel, part),
-        [f32(*rimmed)] * 4,
-        [low_tile, high_tile, whole(sided), whole(sided)],
-        [whole(rimmed)] * 4,
-        cost=MERID,
-        scratch_shapes=[pltpu.VMEM(full, F32), pltpu.VMEM((2, 4 * (rimmed[0] - width), LANES), F32)],
-    )(state, state, from_south, from_north)
-    merid_circle = exchange(merid_packs)
-
-    *zonal_parts, press_spec, zonal_spec = call(
+    *zonal_parts, zonal_spec = call(
         functools.partial(zonal_spec_kernel, bounds, part),
-        [f32(*block)] * 4 + [f32(*spectrum)] * 2,
-        [SMEM] * 2 + [whole(mode.shape)] + [whole(double)] * 4 + table_specs,
-        [whole(block)] * 4 + [whole(spectrum)] * 2,
-        cost=ZONAL_SPEC,
-    )(filter_flag, cutoff, mode, *circle, *forward, *inverse)
+        [f32(*block)] * 4 + [f32(*spectrum)],
+        [SMEM] * 2 + [whole(mode.shape)] + [whole(first)] * 4 + table_specs,
+        [whole(block)] * 4 + [whole(spectrum)],
+    )(filter_flag, cutoff, mode, *first_circle, *forward, *inverse)
     zonal_back = exchange(zonal_parts)
-
-    last_lines = pl.BlockSpec((8, LANES), lambda step: (width // 8, 0))
-    *merid_parts, merid_spec, rim_spec = call(
+    edge_spec = call(
+        functools.partial(edge_spec_kernel, bounds, part, skip),
+        f32(*spectrum),
+        [SMEM] * 2 + [whole(mode.shape)] + [whole(rims)] * 2 + [whole(first)] * 4 + table_specs[:6],
+        whole(spectrum),
+    )(filter_flag, cutoff, mode, from_south, from_north, *first_circle, *forward)
+
+    *merid_parts, merid_spec = call(
         functools.partial(merid_spec_kernel, bounds, part),
-        [f32(*block)] * 4 + [f32(*spectrum)] * 2,
-        [SMEM] * 2 + [whole(mode.shape), last_lines, last_lines] + [whole(rimmed)] * 4 + table_specs,
-        [whole(block)] * 4 + [whole(spectrum)] * 2,
-    )(filter_flag, cutoff, mode, from_south, from_north, *merid_circle, *forward, *inverse)
+        [f32(*block)] * 4 + [f32(*spectrum)],
+        [SMEM] * 2 + [whole(mode.shape), whole(spectrum), ANY] + [whole(second)] * 4 + table_specs,
+        [whole(block)] * 4 + [whole(spectrum)],
+    )(filter_flag, cutoff, mode, edge_spec, zonal_spec, *second_circle, *forward, *inverse)
     merid_back = exchange(merid_parts)
 
     press_parts = call(
         functools.partial(press_back_kernel, bounds, part),
         [f32(*block)] * 4,
-        [SMEM] * 2 + [whole(mode.shape)] + [whole(spectrum)] * 4 + table_specs[6:],
+        [SMEM] * 2 + [whole(mode.shape)] + [whole(spectrum)] * 3 + [whole(second)] * 4 + table_specs,
         [whole(block)] * 4,
-    )(filter_flag, cutoff, mode, press_spec, zonal_spec, merid_spec, rim_spec, *inverse)
+    )(filter_flag, cutoff, mode, zonal_spec, merid_spec, edge_spec, *second_circle, *forward, *inverse)
     press_back = exchange(press_parts)
 
     steps = next(s for s in (3, 5, 1) if width % (8 * s) == 0)

time: 67.8 us -> 64.2 us (0.947)
  waiting for transfers between devices: 25.8 us -> 21.3 us
    ppermute x15, waiting for transfers between devices: 21 us -> 17.6 us  [exchange(): lax.ppermute(blocks[step], 'lon', pairs[step])]
    pallas_call x3 -> x4, Pallas kernels: 5.5 us -> 7.99 us  [the longest x1 2.68 us: packed_body(): call(functools.partial(press_kernel, part), [f32(*second)] * 4 + [f32(*fu...]
    pallas_call x1, Pallas kernels: 4.1 us -> 2.77 us  [packed_body(): call(functools.partial(zonal_spec_kernel, bounds, part), [f32(*block)] *...]
    pallas_call x1, Pallas kernels: 4.1 us -> 2.97 us  [packed_body(): call(functools.partial(merid_spec_kernel, bounds, part), [f32(*block)] *...]
    ppermute x1, waiting for transfers between devices: 4.39 us -> 3.58 us  [packed_body(): lax.ppermute(to_south, 'lat', [(i + 1, i) for i in range(bands - 1)])]
  transfers between devices with their start and end apart: 17 -> 17, of which waited for: 7 -> 7; matrix products, arithmetic and copies ran while one was open for 0% -> 0% of each run, Pallas kernels for 23% -> 26%
where the time goes in v1:
time: 64.2 us; the launch traced here: 64 us
  Pallas kernels  22.1 us (34%)
  waiting for transfers between devices  21.3 us (33%)
  starting transfers between devices  18.4 us (29%)
  local copies, waits for them, and re-layouts  1.9 us (3%)
    ppermute x15, waiting for transfers between devices, exchange(): lax.ppermute(blocks[step], 'lon', pairs[step])  17.6 us
    ppermute x15, starting transfers between devices, exchange(): lax.ppermute(blocks[step], 'lon', pairs[step])  12 us
    ppermute x1, waiting for transfers between devices, packed_body(): lax.ppermute(to_south, 'lat', [(i + 1, i) for i in range(bands - 1)])  3.58 us
    ppermute x1, starting transfers between devices, packed_body(): lax.ppermute(to_south, 'lat', [(i + 1, i) for i in range(bands - 1)])  3.24 us
    ppermute x1, starting transfers between devices, packed_body(): lax.ppermute(to_north, 'lat', [(i, i + 1) for i in range(bands - 1)])  3.12 us
    pallas_call x1, Pallas kernels, packed_body(): call(functools.partial(merid_spec_kernel, bounds, part), [f32(*block)] *...  2.97 us
    pallas_call x1, Pallas kernels, packed_body(): call(functools.partial(press_out_kernel, part), f32(*state.shape), [ANY,...  2.83 us
    pallas_call x1, Pallas kernels, packed_body(): call(functools.partial(press_back_kernel, bounds, part), [f32(*block)] *...  2.82 us
  transfers between devices with their start and end apart: 17, of which 7 were waited for; matrix products, arithmetic and copies ran while one was open for 0% of the time, Pallas kernels for 26%

profile of v1, /device:TPU:17, one launch (start us, length us, event | category | flops | bytes accessed | tf_op | source)
XLA Modules:
  0.0 64.0 jit_solution(15515952178047867261)
XLA Ops:
  0.0 1.8 %copy-done = f32[8,360,256]{2,1,0:T(8,128)S(1)} copy-done((f32[8,360,256]{2,1,0:T(8,128)S(1)}, f32[8,360,256]{2,1,0:T(8,128)}, u32[]{:S(2)}) %copy-start) | copy-done | bytes 2949144
  1.8 2.5 %shard_map.154 = (f32[552,128]{1,0:T(8,128)S(1)}, f32[552,128]{1,0:T(8,128)S(1)}, f32[552,128]{1,0:T(8,128)S(1)}, f32[552,128]{1,0:T(8,128)S(1)}) custom-call(f32[8,360,256]{2,1,0:T(8,128)S(1)} %copy-done, f32[8,360,256]{2,1,0:T(8,128)S(1)} %copy-done), custom_call_target="tpu_custom_call" | custom-call | bytes 7380000 | tf_op jit(solution)/shard_map/pallas_call | solution.py:544
  5.1 1.3 %collective-permute-start.1 = (f32[552,128]{1,0:T(8,128)S(1)}, f32[552,128]{1,0:T(8,128)S(1)}, u32[]{:S(2)}, u32[]{:S(2)}) collective-permute-start(f32[552,128]{1,0:T(8,128)S(1)} %get-tuple-element.32), channel_id=1, source_target_pairs={{0,2},{1,3},{2,0},{3,1},{4,6},{5,7},{6,4},{7,5},{8,10},{9,11},{10,... | collective-permute-start | bytes 847880 | tf_op jit(solution)/shard_map/ppermute | solution.py:518
  7.0 2.7 %shard_map.158 = (f32[632,128]{1,0:T(8,128)S(1)}, f32[632,128]{1,0:T(8,128)S(1)}, f32[632,128]{1,0:T(8,128)S(1)}, f32[632,128]{1,0:T(8,128)S(1)}, f32[8,360,128]{2,1,0:T(8,128)S(1)}) custom-call(f32[8,360,256]{2,1,0:T(8,128)S(1)} %copy-done, f32[8,360,256]{2,1,0:T(8,128)S(1)} %copy-done), custom_call_target="tpu_custom_call" | custom-call | bytes 7380000 | tf_op jit(solution)/shard_map/pallas_call | solution.py:552
  9.9 1.2 %collective-permute-start.9 = (f32[632,128]{1,0:T(8,128)S(1)}, f32[632,128]{1,0:T(8,128)S(1)}, u32[]{:S(2)}, u32[]{:S(2)}) collective-permute-start(f32[632,128]{1,0:T(8,128)S(1)} %get-tuple-element.43), channel_id=1, source_target_pairs={{0,2},{1,3},{2,0},{3,1},{4,6},{5,7},{6,4},{7,5},{8,10},{9,11},{10,... | collective-permute-start | bytes 970760 | tf_op jit(solution)/shard_map/ppermute | solution.py:518
  11.9 1.6 %collective-permute-done.1.q2.refs_2_ = f32[552,128]{1,0:T(8,128)S(1)} collective-permute-done((f32[552,128]{1,0:T(8,128)S(1)}, f32[552,128]{1,0:T(8,128)S(1)}, u32[]{:S(2)}, u32[]{:S(2)}) %collective-permute-start.1) | collective-permute-done | bytes 282656 | tf_op jit(solution)/shard_map/ppermute | solution.py:518
  13.5 6.7 %collective-permute-done.2.q3.refs_3_ = f32[552,128]{1,0:T(8,128)S(1)} collective-permute-done((f32[552,128]{1,0:T(8,128)S(1)}, f32[552,128]{1,0:T(8,128)S(1)}, u32[]{:S(2)}, u32[]{:S(2)}) %collective-permute-start.2) | collective-permute-done | bytes 282656 | tf_op jit(solution)/shard_map/ppermute | solution.py:518
  20.8 3.1 %collective-permute-start.6 = (f32[376,128]{1,0:T(8,128)S(1)}, f32[376,128]{1,0:T(8,128)S(1)}, u32[]{:S(2)}, u32[]{:S(2)}) collective-permute-start(f32[376,128]{1,0:T(8,128)S(1)} %get-tuple-element.38), channel_id=1, source_target_pairs={{0,4},{4,8},{8,12},{12,16},{16,20},{20,24},{24,28},{1,5},{5,9},{9,... | collective-permute-start | bytes 577544 | tf_op jit(solution)/shard_map/ppermute | solution.py:566
  24.0 3.2 %collective-permute-start.7 = (f32[376,128]{1,0:T(8,128)S(1)}, f32[376,128]{1,0:T(8,128)S(1)}, u32[]{:S(2)}, u32[]{:S(2)}) collective-permute-start(f32[376,128]{1,0:T(8,128)S(1)} %get-tuple-element.39), channel_id=1, source_target_pairs={{4,0},{8,4},{12,8},{16,12},{20,16},{24,20},{28,24},{5,1},{9,5},{13... | collective-permute-start | bytes 577544 | tf_op jit(solution)/shard_map/ppermute | solution.py:567
  27.4 2.8 %shard_map.155 = (f32[360,128]{1,0:T(8,128)S(1)}, f32[360,128]{1,0:T(8,128)S(1)}, f32[360,128]{1,0:T(8,128)S(1)}, f32[360,128]{1,0:T(8,128)S(1)}, f32[1488,128]{1,0:T(8,128)S(1)}) custom-call(s32[8]{0:T(128)S(1)} %copy-done.14, s32[8]{0:T(128)S(1)} %copy-done.15, f32[1488,128]{1,0:T(8,128)S(1)} %copy-done.3, f32[552,128]{1,0:T(8,128)S(1)} %get-tuple-element.30.q0.refs_0_, ...), custom_call_target="tpu_custom_call" | custom-call | bytes 7380000 | tf_op jit(solution)/shard_map/pallas_call | solution.py:569
  31.0 3.6 %collective-permute-done.7.north_ref = f32[376,128]{1,0:T(8,128)S(1)} collective-permute-done((f32[376,128]{1,0:T(8,128)S(1)}, f32[376,128]{1,0:T(8,128)S(1)}, u32[]{:S(2)}, u32[]{:S(2)}) %collective-permute-start.7) | collective-permute-done | bytes 192544 | tf_op jit(solution)/shard_map/ppermute | solution.py:567
  34.5 1.2 %collective-permute-start.4 = (f32[360,128]{1,0:T(8,128)S(1)}, f32[360,128]{1,0:T(8,128)S(1)}, u32[]{:S(2)}, u32[]{:S(2)}) collective-permute-start(f32[360,128]{1,0:T(8,128)S(1)} %get-tuple-element.36), channel_id=1, source_target_pairs={{0,2},{1,3},{2,0},{3,1},{4,6},{5,7},{6,4},{7,5},{8,10},{9,11},{10,... | collective-permute-start | bytes 552968 | tf_op jit(solution)/shard_map/ppermute | solution.py:518
  35.8 2.1 %shard_map.157.edge_ref = f32[1488,128]{1,0:T(8,128)S(1)} custom-call(s32[8]{0:T(128)S(1)} %copy-done.14, s32[8]{0:T(128)S(1)} %copy-done.15, f32[1488,128]{1,0:T(8,128)S(1)} %copy-done.3, f32[376,128]{1,0:T(8,128)S(1)} %collective-permute-done.6.south_ref, f32[376,128]{1,0:T(8,128)S(1)} %collective-permute-done.7.north_ref, ...), custom_call_target="tpu_custom_call" | custom-call | bytes 7380000 | tf_op jit(solution)/shard_map/pallas_call | solution.py:576
  37.9 0.9 %collective-permute-start.5 = (f32[360,128]{1,0:T(8,128)S(1)}, f32[360,128]{1,0:T(8,128)S(1)}, u32[]{:S(2)}, u32[]{:S(2)}) collective-permute-start(f32[360,128]{1,0:T(8,128)S(1)} %get-tuple-element.37), channel_id=1, source_target_pairs={{0,3},{1,2},{2,1},{3,0},{4,7},{5,6},{6,5},{7,4},{8,11},{9,10},{10,... | collective-permute-start | bytes 552968 | tf_op jit(solution)/shard_map/ppermute | solution.py:518
  38.8 3.0 %shard_map.159 = (f32[360,128]{1,0:T(8,128)S(1)}, f32[360,128]{1,0:T(8,128)S(1)}, f32[360,128]{1,0:T(8,128)S(1)}, f32[360,128]{1,0:T(8,128)S(1)}, f32[1488,128]{1,0:T(8,128)S(1)}) custom-call(s32[8]{0:T(128)S(1)} %copy-done.14, s32[8]{0:T(128)S(1)} %copy-done.15, f32[1488,128]{1,0:T(8,128)S(1)} %copy-done.3, f32[1488,128]{1,0:T(8,128)S(1)} %shard_map.157.edge_ref, ...), custom_call_target="tpu_custom_call" | custom-call | bytes 7380000 | tf_op jit(solution)/shard_map/pallas_call | solution.py:583
  41.8 1.3 %collective-permute-start.12 = (f32[360,128]{1,0:T(8,128)S(1)}, f32[360,128]{1,0:T(8,128)S(1)}, u32[]{:S(2)}, u32[]{:S(2)}) collective-permute-start(f32[360,128]{1,0:T(8,128)S(1)} %get-tuple-element.47), channel_id=1, source_target_pairs={{0,2},{1,3},{2,0},{3,1},{4,6},{5,7},{6,4},{7,5},{8,10},{9,11},{10,... | collective-permute-start | bytes 552968 | tf_op jit(solution)/shard_map/ppermute | solution.py:518
  43.1 2.8 %shard_map.161 = (f32[360,128]{1,0:T(8,128)S(1)}, f32[360,128]{1,0:T(8,128)S(1)}, f32[360,128]{1,0:T(8,128)S(1)}, f32[360,128]{1,0:T(8,128)S(1)}) custom-call(s32[8]{0:T(128)S(1)} %copy-done.14, s32[8]{0:T(128)S(1)} %copy-done.15, f32[1488,128]{1,0:T(8,128)S(1)} %copy-done.3, f32[1488,128]{1,0:T(8,128)S(1)} %get-tuple-element.40._.zonal_ref, ...), custom_call_target="tpu_custom_call" | custom-call | bytes 7380000 | tf_op jit(solution)/shard_map/pallas_call | solution.py:591
  46.0 0.9 %collective-permute-start.13 = (f32[360,128]{1,0:T(8,128)S(1)}, f32[360,128]{1,0:T(8,128)S(1)}, u32[]{:S(2)}, u32[]{:S(2)}) collective-permute-start(f32[360,128]{1,0:T(8,128)S(1)} %get-tuple-element.48), channel_id=1, source_target_pairs={{0,3},{1,2},{2,1},{3,0},{4,7},{5,6},{6,5},{7,4},{8,11},{9,10},{10,... | collective-permute-start | bytes 552968 | tf_op jit(solution)/shard_map/ppermute | solution.py:518
  46.9 1.3 %collective-permute-start.15 = (f32[360,128]{1,0:T(8,128)S(1)}, f32[360,128]{1,0:T(8,128)S(1)}, u32[]{:S(2)}, u32[]{:S(2)}) collective-permute-start(f32[360,128]{1,0:T(8,128)S(1)} %get-tuple-element.53), channel_id=1, source_target_pairs={{0,2},{1,3},{2,0},{3,1},{4,6},{5,7},{6,4},{7,5},{8,10},{9,11},{10,... | collective-permute-start | bytes 552968 | tf_op jit(solution)/shard_map/ppermute | solution.py:518
  49.0 4.2 %collective-permute-done.13.refs_7_ = f32[360,128]{1,0:T(8,128)S(1)} collective-permute-done((f32[360,128]{1,0:T(8,128)S(1)}, f32[360,128]{1,0:T(8,128)S(1)}, u32[]{:S(2)}, u32[]{:S(2)}) %collective-permute-start.13) | collective-permute-done | bytes 184352 | tf_op jit(solution)/shard_map/ppermute | solution.py:518
  53.3 2.8 %shard_map.160._ = f32[8,360,256]{2,1,0:T(8,128)} custom-call(f32[360,128]{1,0:T(8,128)S(1)} %get-tuple-element.34.refs_0_, f32[360,128]{1,0:T(8,128)S(1)} %collective-permute-done.3.refs_1_, f32[360,128]{1,0:T(8,128)S(1)} %collective-permute-done.4.refs_2_, f32[360,128]{1,0:T(8,128)S(1)} %collective-permute-done.5.refs_3_, ...), custom_call_target="tpu_custom_call" | custom-call | bytes 7380000 | tf_op jit(solution)/shard_map/pallas_call | solution.py:605
  56.0 1.2 %collective-permute-done.15.refs_2_ = f32[360,128]{1,0:T(8,128)S(1)} collective-permute-done((f32[360,128]{1,0:T(8,128)S(1)}, f32[360,128]{1,0:T(8,128)S(1)}, u32[]{:S(2)}, u32[]{:S(2)}) %collective-permute-start.15) | collective-permute-done | bytes 184352 | tf_op jit(solution)/shard_map/ppermute | solution.py:518
  57.2 3.9 %collective-permute-done.16.refs_3_ = f32[360,128]{1,0:T(8,128)S(1)} collective-permute-done((f32[360,128]{1,0:T(8,128)S(1)}, f32[360,128]{1,0:T(8,128)S(1)}, u32[]{:S(2)}, u32[]{:S(2)}) %collective-permute-start.16) | collective-permute-done | bytes 184352 | tf_op jit(solution)/shard_map/ppermute | solution.py:518
  61.2 2.8 %shard_map.162 = f32[8,360,256]{2,1,0:T(8,128)} custom-call(f32[8,360,256]{2,1,0:T(8,128)} %shard_map.160._, f32[8,360,128]{2,1,0:T(8,128)S(1)} %get-tuple-element.49.tile_ref, f32[360,128]{1,0:T(8,128)S(1)} %get-tuple-element.51.refs_0_, f32[360,128]{1,0:T(8,128)S(1)} %collective-permute-done.14.refs_1_, ...), custom_call_target="tpu_custom_call", output_to_operand_aliasing={{}: (0, {})} | custom-call | bytes 7380000 | tf_op jit(solution)/shard_map/pallas_call | solution.py:612
  (51 shorter events, 4.8 us)
Async XLA Ops:
  1.8 25.4 %copy-start.12 = (bf16[360,384]{1,0:T(8,128)(2,1)S(1)}, bf16[360,384]{1,0:T(8,128)(2,1)}, u32[]{:S(2)}) copy-start(bf16[360,384]{1,0:T(8,128)(2,1)} %constant.33.clone.refs_7_.refs_11_) | copy-start | bytes 829444
  1.8 25.4 %copy-start.13 = (bf16[360,384]{1,0:T(8,128)(2,1)S(1)}, bf16[360,384]{1,0:T(8,128)(2,1)}, u32[]{:S(2)}) copy-start(bf16[360,384]{1,0:T(8,128)(2,1)} %constant.32.clone.refs_6_.refs_10_) | copy-start | bytes 829444
  4.4 6.8 %collective-permute-start = (f32[552,128]{1,0:T(8,128)S(1)}, f32[552,128]{1,0:T(8,128)S(1)}, u32[]{:S(2)}, u32[]{:S(2)}) collective-permute-start(f32[552,128]{1,0:T(8,128)S(1)} %get-tuple-element.31), channel_id=1, source_target_pairs={{0,1},{1,0},{2,3},{3,2},{4,5},{5,4},{6,7},{7,6},{8,9},{9,8},{10,11... | collective-permute-start | bytes 847880 | tf_op jit(solution)/shard_map/ppermute | solution.py:518
  5.1 8.3 %collective-permute-start.1 = (f32[552,128]{1,0:T(8,128)S(1)}, f32[552,128]{1,0:T(8,128)S(1)}, u32[]{:S(2)}, u32[]{:S(2)}) collective-permute-start(f32[552,128]{1,0:T(8,128)S(1)} %get-tuple-element.32), channel_id=1, source_target_pairs={{0,2},{1,3},{2,0},{3,1},{4,6},{5,7},{6,4},{7,5},{8,10},{9,11},{10,... | collective-permute-start | bytes 847880 | tf_op jit(solution)/shard_map/ppermute | solution.py:518
  6.4 20.9 %copy-start.7 = (bf16[384,360]{1,0:T(8,128)(2,1)S(1)}, bf16[384,360]{1,0:T(8,128)(2,1)}, u32[]{:S(2)}) copy-start(bf16[384,360]{1,0:T(8,128)(2,1)} %constant.28.clone.refs_2_.refs_6_) | copy-start | bytes 829444
  6.4 20.9 %copy-start.8 = (bf16[384,360]{1,0:T(8,128)(2,1)S(1)}, bf16[384,360]{1,0:T(8,128)(2,1)}, u32[]{:S(2)}) copy-start(bf16[384,360]{1,0:T(8,128)(2,1)} %constant.27.clone.refs_1_.refs_5_) | copy-start | bytes 829444
  6.4 20.9 %copy-start.9 = (bf16[384,360]{1,0:T(8,128)(2,1)S(1)}, bf16[384,360]{1,0:T(8,128)(2,1)}, u32[]{:S(2)}) copy-start(bf16[384,360]{1,0:T(8,128)(2,1)} %constant.26.clone.refs_0_.refs_4_) | copy-start | bytes 829444
  6.4 20.9 %copy-start.10 = (bf16[360,384]{1,0:T(8,128)(2,1)S(1)}, bf16[360,384]{1,0:T(8,128)(2,1)}, u32[]{:S(2)}) copy-start(bf16[360,384]{1,0:T(8,128)(2,1)} %constant.35.clone.refs_9_.refs_13_) | copy-start | bytes 829444
  6.4 20.9 %copy-start.11 = (bf16[360,384]{1,0:T(8,128)(2,1)S(1)}, bf16[360,384]{1,0:T(8,128)(2,1)}, u32[]{:S(2)}) copy-start(bf16[360,384]{1,0:T(8,128)(2,1)} %constant.34.clone.refs_8_.refs_12_) | copy-start | bytes 829444
  6.5 13.7 %collective-permute-start.2 = (f32[552,128]{1,0:T(8,128)S(1)}, f32[552,128]{1,0:T(8,128)S(1)}, u32[]{:S(2)}, u32[]{:S(2)}) collective-permute-start(f32[552,128]{1,0:T(8,128)S(1)} %get-tuple-element.33), channel_id=1, source_target_pairs={{0,3},{1,2},{2,1},{3,0},{4,7},{5,6},{6,5},{7,4},{8,11},{9,10},{10,... | collective-permute-start | bytes 847880 | tf_op jit(solution)/shard_map/ppermute | solution.py:518
  9.7 28.2 %collective-permute-start.8 = (f32[632,128]{1,0:T(8,128)S(1)}, f32[632,128]{1,0:T(8,128)S(1)}, u32[]{:S(2)}, u32[]{:S(2)}) collective-permute-start(f32[632,128]{1,0:T(8,128)S(1)} %get-tuple-element.42), channel_id=1, source_target_pairs={{0,1},{1,0},{2,3},{3,2},{4,5},{5,4},{6,7},{7,6},{8,9},{9,8},{10,11... | collective-permute-start | bytes 970760 | tf_op jit(solution)/shard_map/ppermute | solution.py:518
  9.9 28.8 %collective-permute-start.9 = (f32[632,128]{1,0:T(8,128)S(1)}, f32[632,128]{1,0:T(8,128)S(1)}, u32[]{:S(2)}, u32[]{:S(2)}) collective-permute-start(f32[632,128]{1,0:T(8,128)S(1)} %get-tuple-element.43), channel_id=1, source_target_pairs={{0,2},{1,3},{2,0},{3,1},{4,6},{5,7},{6,4},{7,5},{8,10},{9,11},{10,... | collective-permute-start | bytes 970760 | tf_op jit(solution)/shard_map/ppermute | solution.py:518
  11.2 27.6 %collective-permute-start.10 = (f32[632,128]{1,0:T(8,128)S(1)}, f32[632,128]{1,0:T(8,128)S(1)}, u32[]{:S(2)}, u32[]{:S(2)}) collective-permute-start(f32[632,128]{1,0:T(8,128)S(1)} %get-tuple-element.44), channel_id=1, source_target_pairs={{0,3},{1,2},{2,1},{3,0},{4,7},{5,6},{6,5},{7,4},{8,11},{9,10},{10,... | collective-permute-start | bytes 970760 | tf_op jit(solution)/shard_map/ppermute | solution.py:518
  20.8 9.4 %collective-permute-start.6 = (f32[376,128]{1,0:T(8,128)S(1)}, f32[376,128]{1,0:T(8,128)S(1)}, u32[]{:S(2)}, u32[]{:S(2)}) collective-permute-start(f32[376,128]{1,0:T(8,128)S(1)} %get-tuple-element.38), channel_id=1, source_target_pairs={{0,4},{4,8},{8,12},{12,16},{16,20},{20,24},{24,28},{1,5},{5,9},{9,... | collective-permute-start | bytes 577544 | tf_op jit(solution)/shard_map/ppermute | solution.py:566
  24.0 10.6 %collective-permute-start.7 = (f32[376,128]{1,0:T(8,128)S(1)}, f32[376,128]{1,0:T(8,128)S(1)}, u32[]{:S(2)}, u32[]{:S(2)}) collective-permute-start(f32[376,128]{1,0:T(8,128)S(1)} %get-tuple-element.39), channel_id=1, source_target_pairs={{4,0},{8,4},{12,8},{16,12},{20,16},{24,20},{28,24},{5,1},{9,5},{13... | collective-permute-start | bytes 577544 | tf_op jit(solution)/shard_map/ppermute | solution.py:567
  30.2 15.7 %collective-permute-start.3 = (f32[360,128]{1,0:T(8,128)S(1)}, f32[360,128]{1,0:T(8,128)S(1)}, u32[]{:S(2)}, u32[]{:S(2)}) collective-permute-start(f32[360,128]{1,0:T(8,128)S(1)} %get-tuple-element.35), channel_id=1, source_target_pairs={{0,1},{1,0},{2,3},{3,2},{4,5},{5,4},{6,7},{7,6},{8,9},{9,8},{10,11... | collective-permute-start | bytes 552968 | tf_op jit(solution)/shard_map/ppermute | solution.py:518
  34.5 12.3 %collective-permute-start.4 = (f32[360,128]{1,0:T(8,128)S(1)}, f32[360,128]{1,0:T(8,128)S(1)}, u32[]{:S(2)}, u32[]{:S(2)}) collective-permute-start(f32[360,128]{1,0:T(8,128)S(1)} %get-tuple-element.36), channel_id=1, source_target_pairs={{0,2},{1,3},{2,0},{3,1},{4,6},{5,7},{6,4},{7,5},{8,10},{9,11},{10,... | collective-permute-start | bytes 552968 | tf_op jit(solution)/shard_map/ppermute | solution.py:518
  37.9 9.0 %collective-permute-start.5 = (f32[360,128]{1,0:T(8,128)S(1)}, f32[360,128]{1,0:T(8,128)S(1)}, u32[]{:S(2)}, u32[]{:S(2)}) collective-permute-start(f32[360,128]{1,0:T(8,128)S(1)} %get-tuple-element.37), channel_id=1, source_target_pairs={{0,3},{1,2},{2,1},{3,0},{4,7},{5,6},{6,5},{7,4},{8,11},{9,10},{10,... | collective-permute-start | bytes 552968 | tf_op jit(solution)/shard_map/ppermute | solution.py:518
  41.7 6.4 %collective-permute-start.11 = (f32[360,128]{1,0:T(8,128)S(1)}, f32[360,128]{1,0:T(8,128)S(1)}, u32[]{:S(2)}, u32[]{:S(2)}) collective-permute-start(f32[360,128]{1,0:T(8,128)S(1)} %get-tuple-element.46), channel_id=1, source_target_pairs={{0,1},{1,0},{2,3},{3,2},{4,5},{5,4},{6,7},{7,6},{8,9},{9,8},{10,11... | collective-permute-start | bytes 552968 | tf_op jit(solution)/shard_map/ppermute | solution.py:518
  41.8 7.2 %collective-permute-start.12 = (f32[360,128]{1,0:T(8,128)S(1)}, f32[360,128]{1,0:T(8,128)S(1)}, u32[]{:S(2)}, u32[]{:S(2)}) collective-permute-start(f32[360,128]{1,0:T(8,128)S(1)} %get-tuple-element.47), channel_id=1, source_target_pairs={{0,2},{1,3},{2,0},{3,1},{4,6},{5,7},{6,4},{7,5},{8,10},{9,11},{10,... | collective-permute-start | bytes 552968 | tf_op jit(solution)/shard_map/ppermute | solution.py:518
  46.0 7.3 %collective-permute-start.13 = (f32[360,128]{1,0:T(8,128)S(1)}, f32[360,128]{1,0:T(8,128)S(1)}, u32[]{:S(2)}, u32[]{:S(2)}) collective-permute-start(f32[360,128]{1,0:T(8,128)S(1)} %get-tuple-element.48), channel_id=1, source_target_pairs={{0,3},{1,2},{2,1},{3,0},{4,7},{5,6},{6,5},{7,4},{8,11},{9,10},{10,... | collective-permute-start | bytes 552968 | tf_op jit(solution)/shard_map/ppermute | solution.py:518
  46.9 9.2 %collective-permute-start.14 = (f32[360,128]{1,0:T(8,128)S(1)}, f32[360,128]{1,0:T(8,128)S(1)}, u32[]{:S(2)}, u32[]{:S(2)}) collective-permute-start(f32[360,128]{1,0:T(8,128)S(1)} %get-tuple-element.52), channel_id=1, source_target_pairs={{0,1},{1,0},{2,3},{3,2},{4,5},{5,4},{6,7},{7,6},{8,9},{9,8},{10,11... | collective-permute-start | bytes 552968 | tf_op jit(solution)/shard_map/ppermute | solution.py:518
  46.9 10.3 %collective-permute-start.15 = (f32[360,128]{1,0:T(8,128)S(1)}, f32[360,128]{1,0:T(8,128)S(1)}, u32[]{:S(2)}, u32[]{:S(2)}) collective-permute-start(f32[360,128]{1,0:T(8,128)S(1)} %get-tuple-element.53), channel_id=1, source_target_pairs={{0,2},{1,3},{2,0},{3,1},{4,6},{5,7},{6,4},{7,5},{8,10},{9,11},{10,... | collective-permute-start | bytes 552968 | tf_op jit(solution)/shard_map/ppermute | solution.py:518
  48.2 13.0 %collective-permute-start.16 = (f32[360,128]{1,0:T(8,128)S(1)}, f32[360,128]{1,0:T(8,128)S(1)}, u32[]{:S(2)}, u32[]{:S(2)}) collective-permute-start(f32[360,128]{1,0:T(8,128)S(1)} %get-tuple-element.54), channel_id=1, source_target_pairs={{0,3},{1,2},{2,1},{3,0},{4,7},{5,6},{6,5},{7,4},{8,11},{9,10},{10,... | collective-permute-start | bytes 552968 | tf_op jit(solution)/shard_map/ppermute | solution.py:518
  (9 other events, 149.2 us)

commit v2 on v1

--- a/solution.py
+++ b/solution.py
@@ -84,9 +84,10 @@
 
 
 def select_groups(values, masks):
-    out = values[0]
-    for mask, value in zip(masks[1:], values[1:]):
-        out = jnp.where(mask, value, out)
+    out = None
+    for mask, value in zip(masks, values):
+        if value is not None:
+            out = value if out is None else jnp.where(mask, value, out)
     return out
 
 
@@ -99,9 +100,21 @@
     count = len(tiles)
     turned = []
     for shift in range(count):
-        mixed = select_groups([tiles[(shift + g) % count] for g in range(count)], masks)
+        mixed = select_groups([tiles[(shift + g) % count] if g in wanted else None for g in range(count)], masks)
         turned.append(pltpu.roll(mixed, shift * part, 1) if shift else mixed)
     return [select_groups([turned[(h - g) % count] for h in range(count)], masks) for g in wanted]
+
+
+def gather_groups(blocks, masks, part):
+    count = len(masks)
+    turned = []
+    for shift in range(count):
+        mixed = [None] * count
+        for g, block in enumerate(blocks):
+            mixed[(4 + g - shift) % count] = block
+        mixed = select_groups(mixed, masks)
+        turned.append(pltpu.roll(mixed, shift * part, 1) if shift else mixed)
+    return [select_groups([None] * 4 + [turned[(4 + g - row) % count] for g in range(4)], masks) for row in range(count)]
 
 
 def partner_order(blocks, me):
@@ -136,12 +149,12 @@
     return table.astype(BF16)
 
 
-def each_chunk(size, step, work, **loop):
+def each_chunk(size, step, work):
     def turn(index, carry):
         work(pl.multiple_of(index * step, 8))
         return carry
 
-    lax.fori_loop(0, size // step, turn, 0, **loop)
+    lax.fori_loop(0, size // step, turn, 0, unroll=True)
 
 
 def put(refs, start, values):
@@ -200,7 +213,7 @@
                 tiles += [merid_row(wind_ref, tile_ref, row, lines), tile_ref[row, lines]]
         put(packs, width + 8 + start, partner_order(transpose_groups(tiles, masks8, part, range(4, 8)), me))
 
-    each_chunk(head, 8, pack_rim, unroll=True)
+    each_chunk(head, 8, pack_rim)
 
 
 def rim_lines(width):
@@ -230,7 +243,7 @@
         put(packs, start, partner_order(blocks, me))
 
     for pair in range(3):
-        each_chunk(tail, 8, lambda start: pack_merid(pl.multiple_of(start + pair * tail, 8), pair), unroll=True)
+        each_chunk(tail, 8, lambda start: pack_merid(pl.multiple_of(start + pair * tail, 8), pair))
     for start in range(3 * tail, head, 8):
         pack_merid(start, 2, start)
 
@@ -396,7 +409,7 @@
     return jnp.minimum(1.0, ratio * ratio)
 
 
-def zonal_spec_kernel(bounds, part, flag_ref, cut_ref, mode_ref, q0, q1, q2, q3, *refs):
+def zonal_spec_kernel(bounds, part, flag_ref, cut_ref, mode_ref, _, q0, q1, q2, q3, *refs):
     forward, inverse, outs, spec_ref = refs[:6], refs[6:12], refs[12:16], refs[16]
     rows = flag_ref.shape[0]
     width = outs[0].shape[0]
@@ -455,33 +468,40 @@
     size = chunk_of(width)
     masks = group_masks(size, part)
 
-    def unpack(step, carry):
-        lines = pl.ds(pl.multiple_of(step * size, 8), size)
+    def unpack(start):
+        lines = pl.ds(start, size)
         values = [ref[lines] for ref in blocks]
         values = partner_order(values[:4], me) + partner_order(values[4:], me)
         for row, value in enumerate(transpose_groups(values, masks, part, range(rows))):
             out_ref[row, lines] = value
-        return carry
-
-    lax.fori_loop(0, width // size, unpack, 0)
+
+    each_chunk(width, size, unpack)
 
 
 def press_out_kernel(part, _, tile_ref, *refs):
-    blocks, out_ref = refs[:4], refs[4]
-    rows, width, _ = out_ref.shape
+    blocks, out_hbm, tile_out, sems = refs[:4], refs[4], refs[5], refs[6]
+    rows, width, _ = tile_ref.shape
     me = lax.axis_index("lon")
     size = chunk_of(width)
     masks = group_masks(size, part)
     low = lane_ids((size, LANES)) < LANES // 2
-
-    def unpack(step, carry):
-        lines = pl.ds(pl.multiple_of(step * size, 8), size)
-        values = partner_order([ref[lines] for ref in blocks], me)
-        for row, value in enumerate(transpose_groups(values + values, masks, part, range(rows))):
-            out_ref[row, lines] = jnp.where(low, tile_ref[row, lines], value)
-        return carry
-
-    lax.fori_loop(0, width // size, unpack, 0)
+    count = sems.shape[0]
+    copies = []
+    for piece in range(count):
+        begin, end = piece * width // count, (piece + 1) * width // count
+
+        def unpack(start):
+            lines = pl.ds(start + begin, size)
+            values = partner_order([ref[lines] for ref in blocks], me)
+            for row, value in enumerate(gather_groups(values, masks, part)):
+                tile_out[row, lines] = jnp.where(low, tile_ref[row, lines], value)
+
+        each_chunk(end - begin, size, unpack)
+        copy = pltpu.make_async_copy(tile_out.at[:, begin:end], out_hbm.at[:, begin:end, LANES:], sems.at[piece])
+        copy.start()
+        copies.append(copy)
+    for copy in copies:
+        copy.wait()
 
 
 def whole(shape):
@@ -515,7 +535,8 @@
 
 def exchange(blocks):
     pairs = [[(i, i ^ step) for i in range(4)] for step in range(4)]
-    return [blocks[0]] + [lax.ppermute(blocks[step], "lon", pairs[step]) for step in range(1, 4)]
+    chip, far, core = (lax.ppermute(blocks[step], "lon", pairs[step]) for step in (2, 3, 1))
+    return [blocks[0], core, chip, far]
 
 
 def packed_body(state, filter_flag, cutoff):
@@ -569,9 +590,9 @@
     *zonal_parts, zonal_spec = call(
         functools.partial(zonal_spec_kernel, bounds, part),
         [f32(*block)] * 4 + [f32(*spectrum)],
-        [SMEM] * 2 + [whole(mode.shape)] + [whole(first)] * 4 + table_specs,
+        [SMEM] * 2 + [whole(mode.shape), ANY] + [whole(first)] * 4 + table_specs,
         [whole(block)] * 4 + [whole(spectrum)],
-    )(filter_flag, cutoff, mode, *first_circle, *forward, *inverse)
+    )(filter_flag, cutoff, mode, second_circle[1], *first_circle, *forward, *inverse)
     zonal_back = exchange(zonal_parts)
     edge_spec = call(
         functools.partial(edge_spec_kernel, bounds, part, skip),
@@ -596,25 +617,19 @@
     )(filter_flag, cutoff, mode, zonal_spec, merid_spec, edge_spec, *second_circle, *forward, *inverse)
     press_back = exchange(press_parts)
 
-    steps = next(s for s in (3, 5, 1) if width % (8 * s) == 0)
-    piece = pl.BlockSpec((width // steps, LANES), lambda step: (step, 0))
-
-    def slab(index):
-        return pl.BlockSpec((rows, width // steps, LANES), lambda step: (0, step, index))
-
     out = call(
         functools.partial(winds_out_kernel, part),
         f32(*state.shape),
-        [piece] * 8,
-        slab(0),
-        grid=(steps,),
+        [whole(block)] * 8,
+        low_tile,
     )(*zonal_back, *merid_back)
+    pieces = next(n for n in (3, 5, 1) if width % (n * chunk_of(width)) == 0)
     return call(
         functools.partial(press_out_kernel, part),
         f32(*state.shape),
-        [ANY, slab(0)] + [piece] * 4,
-        slab(1),
-        grid=(steps,),
+        [ANY, whole(full)] + [whole(block)] * 4,
+        ANY,
+        scratch_shapes=[pltpu.VMEM(full, F32), pltpu.SemaphoreType.DMA((pieces,))],
         input_output_aliases={0: 0},
     )(out, vert, *press_back)
 

time: 64.2 us -> 60.1 us (0.936)
  Pallas kernels: 22.1 us -> 17.4 us
    pallas_call x1, Pallas kernels: 2.83 us -> 1.38 us  [packed_body(): call(functools.partial(press_out_kernel, part), f32(*state.shape), [ANY,...]
    pallas_call x1, Pallas kernels: 2.55 us -> 1.23 us  [packed_body(): call(functools.partial(zonal_kernel, part), [f32(*first)] * 4, [low_tile,...]
    pallas_call x1, Pallas kernels: 2.68 us -> 1.49 us  [packed_body(): call(functools.partial(press_kernel, part), [f32(*second)] * 4 + [f32(*fu...]
    ppermute x15, waiting for transfers between devices: 17.6 us -> 18.8 us  [exchange(): lax.ppermute(blocks[step], 'lon', pairs[step])]
    pallas_call x1, Pallas kernels: 2.76 us -> 1.92 us  [packed_body(): call(functools.partial(winds_out_kernel, part), f32(*state.shape), [whole...]
    ppermute x1, waiting for transfers between devices: 3.58 us -> 2.76 us  [packed_body(): lax.ppermute(to_south, 'lat', [(i + 1, i) for i in range(bands - 1)])]
  transfers between devices with their start and end apart: 17 -> 17, of which waited for: 7 -> 6; matrix products, arithmetic and copies ran while one was open for 0% -> 0% of each run, Pallas kernels for 26% -> 25%
where the time goes in v2:
time: 60.1 us; the launch traced here: 60 us
  waiting for transfers between devices  21.5 us (36%)
  starting transfers between devices  18.7 us (31%)
  Pallas kernels  17.4 us (29%)
  local copies, waits for them, and re-layouts  1.9 us (3%)
    ppermute x15, waiting for transfers between devices, exchange(): lax.ppermute(blocks[step], 'lon', pairs[step])  18.8 us
    ppermute x15, starting transfers between devices, exchange(): lax.ppermute(blocks[step], 'lon', pairs[step])  12.3 us
    ppermute x1, starting transfers between devices, packed_body(): lax.ppermute(to_south, 'lat', [(i + 1, i) for i in range(bands - 1)])  3.24 us
    ppermute x1, starting transfers between devices, packed_body(): lax.ppermute(to_north, 'lat', [(i, i + 1) for i in range(bands - 1)])  3.12 us
    pallas_call x1, Pallas kernels, packed_body(): call(functools.partial(merid_spec_kernel, bounds, part), [f32(*block)] *...  3.02 us
    pallas_call x1, Pallas kernels, packed_body(): call(functools.partial(press_back_kernel, bounds, part), [f32(*block)] *...  2.85 us
    ppermute x1, waiting for transfers between devices, packed_body(): lax.ppermute(to_south, 'lat', [(i + 1, i) for i in range(bands - 1)])  2.76 us
    pallas_call x1, Pallas kernels, packed_body(): call(functools.partial(zonal_spec_kernel, bounds, part), [f32(*block)] *...  2.76 us
  transfers between devices with their start and end apart: 17, of which 6 were waited for; matrix products, arithmetic and copies ran while one was open for 0% of the time, Pallas kernels for 25%

profile of v2, /device:TPU:17, one launch (start us, length us, event | category | flops | bytes accessed | tf_op | source)
XLA Modules:
  0.0 60.0 jit_solution(13986121508731703310)
XLA Ops:
  0.0 1.8 %copy-done = f32[8,360,256]{2,1,0:T(8,128)S(1)} copy-done((f32[8,360,256]{2,1,0:T(8,128)S(1)}, f32[8,360,256]{2,1,0:T(8,128)}, u32[]{:S(2)}) %copy-start) | copy-done | bytes 2949144
  1.8 1.2 %shard_map.155 = (f32[552,128]{1,0:T(8,128)S(1)}, f32[552,128]{1,0:T(8,128)S(1)}, f32[552,128]{1,0:T(8,128)S(1)}, f32[552,128]{1,0:T(8,128)S(1)}) custom-call(f32[8,360,256]{2,1,0:T(8,128)S(1)} %copy-done, f32[8,360,256]{2,1,0:T(8,128)S(1)} %copy-done), custom_call_target="tpu_custom_call" | custom-call | bytes 7380000 | tf_op jit(solution)/shard_map/pallas_call | solution.py:565
  3.8 1.3 %collective-permute-start.2 = (f32[552,128]{1,0:T(8,128)S(1)}, f32[552,128]{1,0:T(8,128)S(1)}, u32[]{:S(2)}, u32[]{:S(2)}) collective-permute-start(f32[552,128]{1,0:T(8,128)S(1)} %get-tuple-element.33), channel_id=1, source_target_pairs={{0,2},{1,3},{2,0},{3,1},{4,6},{5,7},{6,4},{7,5},{8,10},{9,11},{10,... | collective-permute-start | bytes 847880 | tf_op jit(solution)/shard_map/ppermute | solution.py:538
  5.7 1.5 %shard_map.154 = (f32[632,128]{1,0:T(8,128)S(1)}, f32[632,128]{1,0:T(8,128)S(1)}, f32[632,128]{1,0:T(8,128)S(1)}, f32[632,128]{1,0:T(8,128)S(1)}, f32[8,360,128]{2,1,0:T(8,128)S(1)}) custom-call(f32[8,360,256]{2,1,0:T(8,128)S(1)} %copy-done, f32[8,360,256]{2,1,0:T(8,128)S(1)} %copy-done), custom_call_target="tpu_custom_call" | custom-call | bytes 7380000 | tf_op jit(solution)/shard_map/pallas_call | solution.py:573
  7.4 1.2 %collective-permute-start.9 = (f32[632,128]{1,0:T(8,128)S(1)}, f32[632,128]{1,0:T(8,128)S(1)}, u32[]{:S(2)}, u32[]{:S(2)}) collective-permute-start(f32[632,128]{1,0:T(8,128)S(1)} %get-tuple-element.43), channel_id=1, source_target_pairs={{0,2},{1,3},{2,0},{3,1},{4,6},{5,7},{6,4},{7,5},{8,10},{9,11},{10,... | collective-permute-start | bytes 970760 | tf_op jit(solution)/shard_map/ppermute | solution.py:538
  8.6 0.8 %collective-permute-start.10 = (f32[632,128]{1,0:T(8,128)S(1)}, f32[632,128]{1,0:T(8,128)S(1)}, u32[]{:S(2)}, u32[]{:S(2)}) collective-permute-start(f32[632,128]{1,0:T(8,128)S(1)} %get-tuple-element.44), channel_id=1, source_target_pairs={{0,3},{1,2},{2,1},{3,0},{4,7},{5,6},{6,5},{7,4},{8,11},{9,10},{10,... | collective-permute-start | bytes 970760 | tf_op jit(solution)/shard_map/ppermute | solution.py:538
  9.4 2.8 %collective-permute-done.2.q2.refs_2_ = f32[552,128]{1,0:T(8,128)S(1)} collective-permute-done((f32[552,128]{1,0:T(8,128)S(1)}, f32[552,128]{1,0:T(8,128)S(1)}, u32[]{:S(2)}, u32[]{:S(2)}) %collective-permute-start.2) | collective-permute-done | bytes 282656 | tf_op jit(solution)/shard_map/ppermute | solution.py:538
  12.1 6.7 %collective-permute-done.3.q3.refs_3_ = f32[552,128]{1,0:T(8,128)S(1)} collective-permute-done((f32[552,128]{1,0:T(8,128)S(1)}, f32[552,128]{1,0:T(8,128)S(1)}, u32[]{:S(2)}, u32[]{:S(2)}) %collective-permute-start.3) | collective-permute-done | bytes 282656 | tf_op jit(solution)/shard_map/ppermute | solution.py:538
  19.5 3.1 %collective-permute-start.7 = (f32[376,128]{1,0:T(8,128)S(1)}, f32[376,128]{1,0:T(8,128)S(1)}, u32[]{:S(2)}, u32[]{:S(2)}) collective-permute-start(f32[376,128]{1,0:T(8,128)S(1)} %get-tuple-element.39), channel_id=1, source_target_pairs={{0,4},{4,8},{8,12},{12,16},{16,20},{20,24},{24,28},{1,5},{5,9},{9,... | collective-permute-start | bytes 577544 | tf_op jit(solution)/shard_map/ppermute | solution.py:587
  22.6 3.2 %collective-permute-start.8 = (f32[376,128]{1,0:T(8,128)S(1)}, f32[376,128]{1,0:T(8,128)S(1)}, u32[]{:S(2)}, u32[]{:S(2)}) collective-permute-start(f32[376,128]{1,0:T(8,128)S(1)} %get-tuple-element.40), channel_id=1, source_target_pairs={{4,0},{8,4},{12,8},{16,12},{20,16},{24,20},{28,24},{5,1},{9,5},{13... | collective-permute-start | bytes 577544 | tf_op jit(solution)/shard_map/ppermute | solution.py:588
  26.0 2.8 %shard_map.156 = (f32[360,128]{1,0:T(8,128)S(1)}, f32[360,128]{1,0:T(8,128)S(1)}, f32[360,128]{1,0:T(8,128)S(1)}, f32[360,128]{1,0:T(8,128)S(1)}, f32[1488,128]{1,0:T(8,128)S(1)}) custom-call(s32[8]{0:T(128)S(1)} %copy-done.14, s32[8]{0:T(128)S(1)} %copy-done.15, f32[1488,128]{1,0:T(8,128)S(1)} %copy-done.3, f32[632,128]{1,0:T(8,128)S(1)} %collective-permute-done._.refs_1_, ...), custom_call_target="tpu_custom_call" | custom-call | bytes 7380000 | tf_op jit(solution)/shard_map/pallas_call | solution.py:590
  29.2 1.2 %collective-permute-start.5 = (f32[360,128]{1,0:T(8,128)S(1)}, f32[360,128]{1,0:T(8,128)S(1)}, u32[]{:S(2)}, u32[]{:S(2)}) collective-permute-start(f32[360,128]{1,0:T(8,128)S(1)} %get-tuple-element.37), channel_id=1, source_target_pairs={{0,2},{1,3},{2,0},{3,1},{4,6},{5,7},{6,4},{7,5},{8,10},{9,11},{10,... | collective-permute-start | bytes 552968 | tf_op jit(solution)/shard_map/ppermute | solution.py:538
  30.5 2.8 %collective-permute-done.8.north_ref = f32[376,128]{1,0:T(8,128)S(1)} collective-permute-done((f32[376,128]{1,0:T(8,128)S(1)}, f32[376,128]{1,0:T(8,128)S(1)}, u32[]{:S(2)}, u32[]{:S(2)}) %collective-permute-start.8) | collective-permute-done | bytes 192544 | tf_op jit(solution)/shard_map/ppermute | solution.py:588
  33.2 1.6 %collective-permute-start.6 = (f32[360,128]{1,0:T(8,128)S(1)}, f32[360,128]{1,0:T(8,128)S(1)}, u32[]{:S(2)}, u32[]{:S(2)}) collective-permute-start(f32[360,128]{1,0:T(8,128)S(1)} %get-tuple-element.38), channel_id=1, source_target_pairs={{0,3},{1,2},{2,1},{3,0},{4,7},{5,6},{6,5},{7,4},{8,11},{9,10},{10,... | collective-permute-start | bytes 552968 | tf_op jit(solution)/shard_map/ppermute | solution.py:538
  34.8 2.1 %shard_map.158.edge_ref = f32[1488,128]{1,0:T(8,128)S(1)} custom-call(s32[8]{0:T(128)S(1)} %copy-done.14, s32[8]{0:T(128)S(1)} %copy-done.15, f32[1488,128]{1,0:T(8,128)S(1)} %copy-done.3, f32[376,128]{1,0:T(8,128)S(1)} %collective-permute-done.7.south_ref, f32[376,128]{1,0:T(8,128)S(1)} %collective-permute-done.8.north_ref, ...), custom_call_target="tpu_custom_call" | custom-call | bytes 7380000 | tf_op jit(solution)/shard_map/pallas_call | solution.py:597
  36.9 3.0 %shard_map.159 = (f32[360,128]{1,0:T(8,128)S(1)}, f32[360,128]{1,0:T(8,128)S(1)}, f32[360,128]{1,0:T(8,128)S(1)}, f32[360,128]{1,0:T(8,128)S(1)}, f32[1488,128]{1,0:T(8,128)S(1)}) custom-call(s32[8]{0:T(128)S(1)} %copy-done.14, s32[8]{0:T(128)S(1)} %copy-done.15, f32[1488,128]{1,0:T(8,128)S(1)} %copy-done.3, f32[1488,128]{1,0:T(8,128)S(1)} %shard_map.158.edge_ref, ...), custom_call_target="tpu_custom_call" | custom-call | bytes 7380000 | tf_op jit(solution)/shard_map/pallas_call | solution.py:604
  40.3 2.9 %shard_map.161 = (f32[360,128]{1,0:T(8,128)S(1)}, f32[360,128]{1,0:T(8,128)S(1)}, f32[360,128]{1,0:T(8,128)S(1)}, f32[360,128]{1,0:T(8,128)S(1)}) custom-call(s32[8]{0:T(128)S(1)} %copy-done.14, s32[8]{0:T(128)S(1)} %copy-done.15, f32[1488,128]{1,0:T(8,128)S(1)} %copy-done.3, f32[1488,128]{1,0:T(8,128)S(1)} %get-tuple-element.41._.zonal_ref, ...), custom_call_target="tpu_custom_call" | custom-call | bytes 7380000 | tf_op jit(solution)/shard_map/pallas_call | solution.py:612
  43.1 1.9 %collective-permute-start.13 = (f32[360,128]{1,0:T(8,128)S(1)}, f32[360,128]{1,0:T(8,128)S(1)}, u32[]{:S(2)}, u32[]{:S(2)}) collective-permute-start(f32[360,128]{1,0:T(8,128)S(1)} %get-tuple-element.48), channel_id=1, source_target_pairs={{0,3},{1,2},{2,1},{3,0},{4,7},{5,6},{6,5},{7,4},{8,11},{9,10},{10,... | collective-permute-start | bytes 552968 | tf_op jit(solution)/shard_map/ppermute | solution.py:538
  45.3 1.8 %collective-permute-start.16 = (f32[360,128]{1,0:T(8,128)S(1)}, f32[360,128]{1,0:T(8,128)S(1)}, u32[]{:S(2)}, u32[]{:S(2)}) collective-permute-start(f32[360,128]{1,0:T(8,128)S(1)} %get-tuple-element.54), channel_id=1, source_target_pairs={{0,3},{1,2},{2,1},{3,0},{4,7},{5,6},{6,5},{7,4},{8,11},{9,10},{10,... | collective-permute-start | bytes 552968 | tf_op jit(solution)/shard_map/ppermute | solution.py:538
  47.2 3.3 %collective-permute-done.13.refs_7_ = f32[360,128]{1,0:T(8,128)S(1)} collective-permute-done((f32[360,128]{1,0:T(8,128)S(1)}, f32[360,128]{1,0:T(8,128)S(1)}, u32[]{:S(2)}, u32[]{:S(2)}) %collective-permute-start.13) | collective-permute-done | bytes 184352 | tf_op jit(solution)/shard_map/ppermute | solution.py:538
  50.5 1.9 %shard_map.160._ = f32[8,360,256]{2,1,0:T(8,128)} custom-call(f32[360,128]{1,0:T(8,128)S(1)} %get-tuple-element.35.refs_0_, f32[360,128]{1,0:T(8,128)S(1)} %collective-permute-done.4.refs_1_, f32[360,128]{1,0:T(8,128)S(1)} %collective-permute-done.5.refs_2_, f32[360,128]{1,0:T(8,128)S(1)} %collective-permute-done.6.refs_3_, ...), custom_call_target="tpu_custom_call" | custom-call | bytes 7380000 | tf_op jit(solution)/shard_map/pallas_call | solution.py:620
  52.4 2.0 %collective-permute-done.15.refs_2_ = f32[360,128]{1,0:T(8,128)S(1)} collective-permute-done((f32[360,128]{1,0:T(8,128)S(1)}, f32[360,128]{1,0:T(8,128)S(1)}, u32[]{:S(2)}, u32[]{:S(2)}) %collective-permute-start.15) | collective-permute-done | bytes 184352 | tf_op jit(solution)/shard_map/ppermute | solution.py:538
  54.5 3.9 %collective-permute-done.16.refs_3_ = f32[360,128]{1,0:T(8,128)S(1)} collective-permute-done((f32[360,128]{1,0:T(8,128)S(1)}, f32[360,128]{1,0:T(8,128)S(1)}, u32[]{:S(2)}, u32[]{:S(2)}) %collective-permute-start.16) | collective-permute-done | bytes 184352 | tf_op jit(solution)/shard_map/ppermute | solution.py:538
  58.4 1.4 %shard_map.162 = f32[8,360,256]{2,1,0:T(8,128)} custom-call(f32[8,360,256]{2,1,0:T(8,128)} %shard_map.160._, f32[8,360,128]{2,1,0:T(8,128)S(1)} %get-tuple-element.49.tile_ref, f32[360,128]{1,0:T(8,128)S(1)} %get-tuple-element.51.refs_0_, f32[360,128]{1,0:T(8,128)S(1)} %collective-permute-done.14.refs_1_, ...), custom_call_target="tpu_custom_call", output_to_operand_aliasing={{}: (0, {})} | custom-call | bytes 7380000 | tf_op jit(solution)/shard_map/pallas_call | solution.py:627
  (51 shorter events, 3.4 us)
Async XLA Ops:
  1.8 24.1 %copy-start.12 = (bf16[360,384]{1,0:T(8,128)(2,1)S(1)}, bf16[360,384]{1,0:T(8,128)(2,1)}, u32[]{:S(2)}) copy-start(bf16[360,384]{1,0:T(8,128)(2,1)} %constant.33.clone.refs_7_.refs_11_) | copy-start | bytes 829444
  1.8 24.1 %copy-start.13 = (bf16[360,384]{1,0:T(8,128)(2,1)S(1)}, bf16[360,384]{1,0:T(8,128)(2,1)}, u32[]{:S(2)}) copy-start(bf16[360,384]{1,0:T(8,128)(2,1)} %constant.32.clone.refs_6_.refs_10_) | copy-start | bytes 829444
  3.1 5.6 %collective-permute-start.1 = (f32[552,128]{1,0:T(8,128)S(1)}, f32[552,128]{1,0:T(8,128)S(1)}, u32[]{:S(2)}, u32[]{:S(2)}) collective-permute-start(f32[552,128]{1,0:T(8,128)S(1)} %get-tuple-element.32), channel_id=1, source_target_pairs={{0,1},{1,0},{2,3},{3,2},{4,5},{5,4},{6,7},{7,6},{8,9},{9,8},{10,11... | collective-permute-start | bytes 847880 | tf_op jit(solution)/shard_map/ppermute | solution.py:538
  3.8 8.3 %collective-permute-start.2 = (f32[552,128]{1,0:T(8,128)S(1)}, f32[552,128]{1,0:T(8,128)S(1)}, u32[]{:S(2)}, u32[]{:S(2)}) collective-permute-start(f32[552,128]{1,0:T(8,128)S(1)} %get-tuple-element.33), channel_id=1, source_target_pairs={{0,2},{1,3},{2,0},{3,1},{4,6},{5,7},{6,4},{7,5},{8,10},{9,11},{10,... | collective-permute-start | bytes 847880 | tf_op jit(solution)/shard_map/ppermute | solution.py:538
  5.1 20.9 %copy-start.7 = (bf16[384,360]{1,0:T(8,128)(2,1)S(1)}, bf16[384,360]{1,0:T(8,128)(2,1)}, u32[]{:S(2)}) copy-start(bf16[384,360]{1,0:T(8,128)(2,1)} %constant.28.clone.refs_2_.refs_6_) | copy-start | bytes 829444
  5.1 20.9 %copy-start.8 = (bf16[384,360]{1,0:T(8,128)(2,1)S(1)}, bf16[384,360]{1,0:T(8,128)(2,1)}, u32[]{:S(2)}) copy-start(bf16[384,360]{1,0:T(8,128)(2,1)} %constant.27.clone.refs_1_.refs_5_) | copy-start | bytes 829444
  5.1 20.9 %copy-start.9 = (bf16[384,360]{1,0:T(8,128)(2,1)S(1)}, bf16[384,360]{1,0:T(8,128)(2,1)}, u32[]{:S(2)}) copy-start(bf16[384,360]{1,0:T(8,128)(2,1)} %constant.26.clone.refs_0_.refs_4_) | copy-start | bytes 829444
  5.1 20.9 %copy-start.10 = (bf16[360,384]{1,0:T(8,128)(2,1)S(1)}, bf16[360,384]{1,0:T(8,128)(2,1)}, u32[]{:S(2)}) copy-start(bf16[360,384]{1,0:T(8,128)(2,1)} %constant.35.clone.refs_9_.refs_13_) | copy-start | bytes 829444
  5.1 20.9 %copy-start.11 = (bf16[360,384]{1,0:T(8,128)(2,1)S(1)}, bf16[360,384]{1,0:T(8,128)(2,1)}, u32[]{:S(2)}) copy-start(bf16[360,384]{1,0:T(8,128)(2,1)} %constant.34.clone.refs_8_.refs_12_) | copy-start | bytes 829444
  5.1 13.7 %collective-permute-start.3 = (f32[552,128]{1,0:T(8,128)S(1)}, f32[552,128]{1,0:T(8,128)S(1)}, u32[]{:S(2)}, u32[]{:S(2)}) collective-permute-start(f32[552,128]{1,0:T(8,128)S(1)} %get-tuple-element.34), channel_id=1, source_target_pairs={{0,3},{1,2},{2,1},{3,0},{4,7},{5,6},{6,5},{7,4},{8,11},{9,10},{10,... | collective-permute-start | bytes 847880 | tf_op jit(solution)/shard_map/ppermute | solution.py:538
  7.2 18.7 %collective-permute-start = (f32[632,128]{1,0:T(8,128)S(1)}, f32[632,128]{1,0:T(8,128)S(1)}, u32[]{:S(2)}, u32[]{:S(2)}) collective-permute-start(f32[632,128]{1,0:T(8,128)S(1)} %get-tuple-element.30), channel_id=1, source_target_pairs={{0,1},{1,0},{2,3},{3,2},{4,5},{5,4},{6,7},{7,6},{8,9},{9,8},{10,11... | collective-permute-start | bytes 970760 | tf_op jit(solution)/shard_map/ppermute | solution.py:538
  7.4 29.5 %collective-permute-start.9 = (f32[632,128]{1,0:T(8,128)S(1)}, f32[632,128]{1,0:T(8,128)S(1)}, u32[]{:S(2)}, u32[]{:S(2)}) collective-permute-start(f32[632,128]{1,0:T(8,128)S(1)} %get-tuple-element.43), channel_id=1, source_target_pairs={{0,2},{1,3},{2,0},{3,1},{4,6},{5,7},{6,4},{7,5},{8,10},{9,11},{10,... | collective-permute-start | bytes 970760 | tf_op jit(solution)/shard_map/ppermute | solution.py:538
  8.6 28.2 %collective-permute-start.10 = (f32[632,128]{1,0:T(8,128)S(1)}, f32[632,128]{1,0:T(8,128)S(1)}, u32[]{:S(2)}, u32[]{:S(2)}) collective-permute-start(f32[632,128]{1,0:T(8,128)S(1)} %get-tuple-element.44), channel_id=1, source_target_pairs={{0,3},{1,2},{2,1},{3,0},{4,7},{5,6},{6,5},{7,4},{8,11},{9,10},{10,... | collective-permute-start | bytes 970760 | tf_op jit(solution)/shard_map/ppermute | solution.py:538
  19.5 9.7 %collective-permute-start.7 = (f32[376,128]{1,0:T(8,128)S(1)}, f32[376,128]{1,0:T(8,128)S(1)}, u32[]{:S(2)}, u32[]{:S(2)}) collective-permute-start(f32[376,128]{1,0:T(8,128)S(1)} %get-tuple-element.39), channel_id=1, source_target_pairs={{0,4},{4,8},{8,12},{12,16},{16,20},{20,24},{24,28},{1,5},{5,9},{9,... | collective-permute-start | bytes 577544 | tf_op jit(solution)/shard_map/ppermute | solution.py:587
  22.6 10.6 %collective-permute-start.8 = (f32[376,128]{1,0:T(8,128)S(1)}, f32[376,128]{1,0:T(8,128)S(1)}, u32[]{:S(2)}, u32[]{:S(2)}) collective-permute-start(f32[376,128]{1,0:T(8,128)S(1)} %get-tuple-element.40), channel_id=1, source_target_pairs={{4,0},{8,4},{12,8},{16,12},{20,16},{24,20},{28,24},{5,1},{9,5},{13... | collective-permute-start | bytes 577544 | tf_op jit(solution)/shard_map/ppermute | solution.py:588
  28.8 14.3 %collective-permute-start.4 = (f32[360,128]{1,0:T(8,128)S(1)}, f32[360,128]{1,0:T(8,128)S(1)}, u32[]{:S(2)}, u32[]{:S(2)}) collective-permute-start(f32[360,128]{1,0:T(8,128)S(1)} %get-tuple-element.36), channel_id=1, source_target_pairs={{0,1},{1,0},{2,3},{3,2},{4,5},{5,4},{6,7},{7,6},{8,9},{9,8},{10,11... | collective-permute-start | bytes 552968 | tf_op jit(solution)/shard_map/ppermute | solution.py:538
  29.2 15.8 %collective-permute-start.5 = (f32[360,128]{1,0:T(8,128)S(1)}, f32[360,128]{1,0:T(8,128)S(1)}, u32[]{:S(2)}, u32[]{:S(2)}) collective-permute-start(f32[360,128]{1,0:T(8,128)S(1)} %get-tuple-element.37), channel_id=1, source_target_pairs={{0,2},{1,3},{2,0},{3,1},{4,6},{5,7},{6,4},{7,5},{8,10},{9,11},{10,... | collective-permute-start | bytes 552968 | tf_op jit(solution)/shard_map/ppermute | solution.py:538
  33.2 11.8 %collective-permute-start.6 = (f32[360,128]{1,0:T(8,128)S(1)}, f32[360,128]{1,0:T(8,128)S(1)}, u32[]{:S(2)}, u32[]{:S(2)}) collective-permute-start(f32[360,128]{1,0:T(8,128)S(1)} %get-tuple-element.38), channel_id=1, source_target_pairs={{0,3},{1,2},{2,1},{3,0},{4,7},{5,6},{6,5},{7,4},{8,11},{9,10},{10,... | collective-permute-start | bytes 552968 | tf_op jit(solution)/shard_map/ppermute | solution.py:538
  39.9 5.4 %collective-permute-start.11 = (f32[360,128]{1,0:T(8,128)S(1)}, f32[360,128]{1,0:T(8,128)S(1)}, u32[]{:S(2)}, u32[]{:S(2)}) collective-permute-start(f32[360,128]{1,0:T(8,128)S(1)} %get-tuple-element.46), channel_id=1, source_target_pairs={{0,1},{1,0},{2,3},{3,2},{4,5},{5,4},{6,7},{7,6},{8,9},{9,8},{10,11... | collective-permute-start | bytes 552968 | tf_op jit(solution)/shard_map/ppermute | solution.py:538
  40.0 7.2 %collective-permute-start.12 = (f32[360,128]{1,0:T(8,128)S(1)}, f32[360,128]{1,0:T(8,128)S(1)}, u32[]{:S(2)}, u32[]{:S(2)}) collective-permute-start(f32[360,128]{1,0:T(8,128)S(1)} %get-tuple-element.47), channel_id=1, source_target_pairs={{0,2},{1,3},{2,0},{3,1},{4,6},{5,7},{6,4},{7,5},{8,10},{9,11},{10,... | collective-permute-start | bytes 552968 | tf_op jit(solution)/shard_map/ppermute | solution.py:538
  43.1 7.4 %collective-permute-start.13 = (f32[360,128]{1,0:T(8,128)S(1)}, f32[360,128]{1,0:T(8,128)S(1)}, u32[]{:S(2)}, u32[]{:S(2)}) collective-permute-start(f32[360,128]{1,0:T(8,128)S(1)} %get-tuple-element.48), channel_id=1, source_target_pairs={{0,3},{1,2},{2,1},{3,0},{4,7},{5,6},{6,5},{7,4},{8,11},{9,10},{10,... | collective-permute-start | bytes 552968 | tf_op jit(solution)/shard_map/ppermute | solution.py:538
  45.0 7.4 %collective-permute-start.14 = (f32[360,128]{1,0:T(8,128)S(1)}, f32[360,128]{1,0:T(8,128)S(1)}, u32[]{:S(2)}, u32[]{:S(2)}) collective-permute-start(f32[360,128]{1,0:T(8,128)S(1)} %get-tuple-element.52), channel_id=1, source_target_pairs={{0,1},{1,0},{2,3},{3,2},{4,5},{5,4},{6,7},{7,6},{8,9},{9,8},{10,11... | collective-permute-start | bytes 552968 | tf_op jit(solution)/shard_map/ppermute | solution.py:538
  45.1 9.4 %collective-permute-start.15 = (f32[360,128]{1,0:T(8,128)S(1)}, f32[360,128]{1,0:T(8,128)S(1)}, u32[]{:S(2)}, u32[]{:S(2)}) collective-permute-start(f32[360,128]{1,0:T(8,128)S(1)} %get-tuple-element.53), channel_id=1, source_target_pairs={{0,2},{1,3},{2,0},{3,1},{4,6},{5,7},{6,4},{7,5},{8,10},{9,11},{10,... | collective-permute-start | bytes 552968 | tf_op jit(solution)/shard_map/ppermute | solution.py:538
  45.3 13.1 %collective-permute-start.16 = (f32[360,128]{1,0:T(8,128)S(1)}, f32[360,128]{1,0:T(8,128)S(1)}, u32[]{:S(2)}, u32[]{:S(2)}) collective-permute-start(f32[360,128]{1,0:T(8,128)S(1)} %get-tuple-element.54), channel_id=1, source_target_pairs={{0,3},{1,2},{2,1},{3,0},{4,7},{5,6},{6,5},{7,4},{8,11},{9,10},{10,... | collective-permute-start | bytes 552968 | tf_op jit(solution)/shard_map/ppermute | solution.py:538
  (9 other events, 150.4 us)

commit v3 on v2

--- a/solution.py
+++ b/solution.py
@@ -155,6 +155,11 @@
         return carry
 
     lax.fori_loop(0, size // step, turn, 0, unroll=True)
+
+
+def natural(refs):
+    own, chip, far, core = refs
+    return [own, core, chip, far]
 
 
 def put(refs, start, values):
@@ -273,7 +278,7 @@
 
 
 def rim_kernel(part, skip, flag_ref, cut_ref, *refs):
-    blocks, north_ref, south_ref = refs[:4], refs[4], refs[5]
+    blocks, north_ref, south_ref = natural(refs[:4]), refs[4], refs[5]
     lines = blocks[0].shape[0] - skip
     first = lane_ids((lines, LANES)) // part % 4 < 2
     for half in range(2):
@@ -288,7 +293,7 @@
 
 
 def edge_spec_kernel(bounds, part, skip, flag_ref, cut_ref, mode_ref, south_ref, north_ref, *refs):
-    blocks, forward, spec_ref = refs[:4], refs[4:10], refs[10]
+    blocks, forward, spec_ref = natural(refs[:4]), refs[4:10], refs[10]
     lines = blocks[0].shape[0] - skip
     width = skip - 8
     half = 0.5 * WIND_COEF
@@ -315,7 +320,7 @@
 
 
 def merid_spec_kernel(bounds, part, flag_ref, cut_ref, mode_ref, edge_ref, _, *refs):
-    blocks, forward, inverse, outs, spec_ref = refs[:4], refs[4:10], refs[10:16], refs[16:20], refs[20]
+    blocks, forward, inverse, outs, spec_ref = natural(refs[:4]), refs[4:10], refs[10:16], refs[16:20], refs[20]
     rows = flag_ref.shape[0]
     width = outs[0].shape[0]
     head = fold_lines(width)
@@ -409,7 +414,7 @@
     return jnp.minimum(1.0, ratio * ratio)
 
 
-def zonal_spec_kernel(bounds, part, flag_ref, cut_ref, mode_ref, _, q0, q1, q2, q3, *refs):
+def zonal_spec_kernel(bounds, part, flag_ref, cut_ref, mode_ref, _, q0, q2, q3, q1, *refs):
     forward, inverse, outs, spec_ref = refs[:6], refs[6:12], refs[12:16], refs[16]
     rows = flag_ref.shape[0]
     width = outs[0].shape[0]
@@ -433,7 +438,7 @@
 
 
 def press_back_kernel(bounds, part, flag_ref, cut_ref, mode_ref, zonal_ref, merid_ref, edge_ref, *refs):
-    quarters, forward, inverse, outs = refs[:4], refs[4:10], refs[10:16], refs[16:]
+    quarters, forward, inverse, outs = natural(refs[:4]), refs[4:10], refs[10:16], refs[16:]
     skip = quarters[0].shape[0] - outs[0].shape[0]
     rows = flag_ref.shape[0]
     nlon = 4 * inverse[0].shape[0]
@@ -462,7 +467,7 @@
 
 
 def winds_out_kernel(part, *refs):
-    blocks, out_ref = refs[:8], refs[8]
+    blocks, out_ref = natural(refs[:4]) + natural(refs[4:8]), refs[8]
     rows, width, _ = out_ref.shape
     me = lax.axis_index("lon")
     size = chunk_of(width)
@@ -479,7 +484,7 @@
 
 
 def press_out_kernel(part, _, tile_ref, *refs):
-    blocks, out_hbm, tile_out, sems = refs[:4], refs[4], refs[5], refs[6]
+    blocks, out_hbm, tile_out, sems = natural(refs[:4]), refs[4], refs[5], refs[6]
     rows, width, _ = tile_ref.shape
     me = lax.axis_index("lon")
     size = chunk_of(width)
@@ -535,8 +540,7 @@
 
 def exchange(blocks):
     pairs = [[(i, i ^ step) for i in range(4)] for step in range(4)]
-    chip, far, core = (lax.ppermute(blocks[step], "lon", pairs[step]) for step in (2, 3, 1))
-    return [blocks[0], core, chip, far]
+    return [blocks[0]] + [lax.ppermute(blocks[step], "lon", pairs[step]) for step in (2, 3, 1)]
 
 
 def packed_body(state, filter_flag, cutoff):
@@ -592,7 +596,7 @@
         [f32(*block)] * 4 + [f32(*spectrum)],
         [SMEM] * 2 + [whole(mode.shape), ANY] + [whole(first)] * 4 + table_specs,
         [whole(block)] * 4 + [whole(spectrum)],
-    )(filter_flag, cutoff, mode, second_circle[1], *first_circle, *forward, *inverse)
+    )(filter_flag, cutoff, mode, second_circle[3], *first_circle, *forward, *inverse)
     zonal_back = exchange(zonal_parts)
     edge_spec = call(
         functools.partial(edge_spec_kernel, bounds, part, skip),

time: 60.1 us -> 58.8 us (0.978)
  waiting for transfers between devices: 21.5 us -> 17.3 us
  starting transfers between devices: 18.7 us -> 21.5 us
    ppermute x15, waiting for transfers between devices: 18.8 us -> 14.9 us  [exchange(): lax.ppermute(blocks[step], 'lon', pairs[step])]
    ppermute x15, starting transfers between devices: 12.3 us -> 15.2 us  [exchange(): lax.ppermute(blocks[step], 'lon', pairs[step])]
where the time goes in v3:
time: 58.8 us; the launch traced here: 58.6 us
  starting transfers between devices  21.5 us (37%)
  Pallas kernels  17.4 us (30%)
  waiting for transfers between devices  17.3 us (29%)
  local copies, waits for them, and re-layouts  1.92 us (3%)
    ppermute x15, starting transfers between devices, exchange(): lax.ppermute(blocks[step], 'lon', pairs[step])  15.2 us
    ppermute x15, waiting for transfers between devices, exchange(): lax.ppermute(blocks[step], 'lon', pairs[step])  14.9 us
    ppermute x1, starting transfers between devices, packed_body(): lax.ppermute(to_south, 'lat', [(i + 1, i) for i in range(bands - 1)])  3.24 us
    ppermute x1, starting transfers between devices, packed_body(): lax.ppermute(to_north, 'lat', [(i, i + 1) for i in range(bands - 1)])  3.12 us
    pallas_call x1, Pallas kernels, packed_body(): call(functools.partial(merid_spec_kernel, bounds, part), [f32(*block)] *...  3.02 us
    pallas_call x1, Pallas kernels, packed_body(): call(functools.partial(press_back_kernel, bounds, part), [f32(*block)] *...  2.85 us
    pallas_call x1, Pallas kernels, packed_body(): call(functools.partial(zonal_spec_kernel, bounds, part), [f32(*block)] *...  2.76 us
    ppermute x1, waiting for transfers between devices, packed_body(): lax.ppermute(to_south, 'lat', [(i + 1, i) for i in range(bands - 1)])  2.43 us
  transfers between devices with their start and end apart: 17, of which 6 were waited for; matrix products, arithmetic and copies ran while one was open for 0% of the time, Pallas kernels for 25%

profile of v3, /device:TPU:17, one launch (start us, length us, event | category | flops | bytes accessed | tf_op | source)
XLA Modules:
  0.0 58.6 jit_solution(6340315813331838470)
XLA Ops:
  0.0 1.8 %copy-done = f32[8,360,256]{2,1,0:T(8,128)S(1)} copy-done((f32[8,360,256]{2,1,0:T(8,128)S(1)}, f32[8,360,256]{2,1,0:T(8,128)}, u32[]{:S(2)}) %copy-start) | copy-done | bytes 2949144
  1.8 1.2 %shard_map.155 = (f32[552,128]{1,0:T(8,128)S(1)}, f32[552,128]{1,0:T(8,128)S(1)}, f32[552,128]{1,0:T(8,128)S(1)}, f32[552,128]{1,0:T(8,128)S(1)}) custom-call(f32[8,360,256]{2,1,0:T(8,128)S(1)} %copy-done, f32[8,360,256]{2,1,0:T(8,128)S(1)} %copy-done), custom_call_target="tpu_custom_call" | custom-call | bytes 7380000 | tf_op jit(solution)/shard_map/pallas_call | solution.py:569
  3.1 1.3 %collective-permute-start.1 = (f32[552,128]{1,0:T(8,128)S(1)}, f32[552,128]{1,0:T(8,128)S(1)}, u32[]{:S(2)}, u32[]{:S(2)}) collective-permute-start(f32[552,128]{1,0:T(8,128)S(1)} %get-tuple-element.32), channel_id=1, source_target_pairs={{0,2},{1,3},{2,0},{3,1},{4,6},{5,7},{6,4},{7,5},{8,10},{9,11},{10,... | collective-permute-start | bytes 847880 | tf_op jit(solution)/shard_map/ppermute | solution.py:543
  4.4 1.1 %collective-permute-start.2 = (f32[552,128]{1,0:T(8,128)S(1)}, f32[552,128]{1,0:T(8,128)S(1)}, u32[]{:S(2)}, u32[]{:S(2)}) collective-permute-start(f32[552,128]{1,0:T(8,128)S(1)} %get-tuple-element.33), channel_id=1, source_target_pairs={{0,3},{1,2},{2,1},{3,0},{4,7},{5,6},{6,5},{7,4},{8,11},{9,10},{10,... | collective-permute-start | bytes 847880 | tf_op jit(solution)/shard_map/ppermute | solution.py:543
  5.6 1.5 %shard_map.154 = (f32[632,128]{1,0:T(8,128)S(1)}, f32[632,128]{1,0:T(8,128)S(1)}, f32[632,128]{1,0:T(8,128)S(1)}, f32[632,128]{1,0:T(8,128)S(1)}, f32[8,360,128]{2,1,0:T(8,128)S(1)}) custom-call(f32[8,360,256]{2,1,0:T(8,128)S(1)} %copy-done, f32[8,360,256]{2,1,0:T(8,128)S(1)} %copy-done), custom_call_target="tpu_custom_call" | custom-call | bytes 7380000 | tf_op jit(solution)/shard_map/pallas_call | solution.py:577
  7.7 1.3 %collective-permute-start.9 = (f32[632,128]{1,0:T(8,128)S(1)}, f32[632,128]{1,0:T(8,128)S(1)}, u32[]{:S(2)}, u32[]{:S(2)}) collective-permute-start(f32[632,128]{1,0:T(8,128)S(1)} %get-tuple-element.43), channel_id=1, source_target_pairs={{0,2},{1,3},{2,0},{3,1},{4,6},{5,7},{6,4},{7,5},{8,10},{9,11},{10,... | collective-permute-start | bytes 970760 | tf_op jit(solution)/shard_map/ppermute | solution.py:543
  8.9 1.8 %collective-permute-done.1.q2.refs_1_ = f32[552,128]{1,0:T(8,128)S(1)} collective-permute-done((f32[552,128]{1,0:T(8,128)S(1)}, f32[552,128]{1,0:T(8,128)S(1)}, u32[]{:S(2)}, u32[]{:S(2)}) %collective-permute-start.1) | collective-permute-done | bytes 282656 | tf_op jit(solution)/shard_map/ppermute | solution.py:543
  10.8 3.8 %collective-permute-start.10 = (f32[632,128]{1,0:T(8,128)S(1)}, f32[632,128]{1,0:T(8,128)S(1)}, u32[]{:S(2)}, u32[]{:S(2)}) collective-permute-start(f32[632,128]{1,0:T(8,128)S(1)} %get-tuple-element.44), channel_id=1, source_target_pairs={{0,3},{1,2},{2,1},{3,0},{4,7},{5,6},{6,5},{7,4},{8,11},{9,10},{10,... | collective-permute-start | bytes 970760 | tf_op jit(solution)/shard_map/ppermute | solution.py:543
  14.6 4.2 %collective-permute-done.2.q3.refs_2_ = f32[552,128]{1,0:T(8,128)S(1)} collective-permute-done((f32[552,128]{1,0:T(8,128)S(1)}, f32[552,128]{1,0:T(8,128)S(1)}, u32[]{:S(2)}, u32[]{:S(2)}) %collective-permute-start.2) | collective-permute-done | bytes 282656 | tf_op jit(solution)/shard_map/ppermute | solution.py:543
  19.5 3.1 %collective-permute-start.7 = (f32[376,128]{1,0:T(8,128)S(1)}, f32[376,128]{1,0:T(8,128)S(1)}, u32[]{:S(2)}, u32[]{:S(2)}) collective-permute-start(f32[376,128]{1,0:T(8,128)S(1)} %get-tuple-element.39), channel_id=1, source_target_pairs={{0,4},{4,8},{8,12},{12,16},{16,20},{20,24},{24,28},{1,5},{5,9},{9,... | collective-permute-start | bytes 577544 | tf_op jit(solution)/shard_map/ppermute | solution.py:591
  22.7 3.2 %collective-permute-start.8 = (f32[376,128]{1,0:T(8,128)S(1)}, f32[376,128]{1,0:T(8,128)S(1)}, u32[]{:S(2)}, u32[]{:S(2)}) collective-permute-start(f32[376,128]{1,0:T(8,128)S(1)} %get-tuple-element.40), channel_id=1, source_target_pairs={{4,0},{8,4},{12,8},{16,12},{20,16},{24,20},{28,24},{5,1},{9,5},{13... | collective-permute-start | bytes 577544 | tf_op jit(solution)/shard_map/ppermute | solution.py:592
  26.1 2.8 %shard_map.156 = (f32[360,128]{1,0:T(8,128)S(1)}, f32[360,128]{1,0:T(8,128)S(1)}, f32[360,128]{1,0:T(8,128)S(1)}, f32[360,128]{1,0:T(8,128)S(1)}, f32[1488,128]{1,0:T(8,128)S(1)}) custom-call(s32[8]{0:T(128)S(1)} %copy-done.14, s32[8]{0:T(128)S(1)} %copy-done.15, f32[1488,128]{1,0:T(8,128)S(1)} %copy-done.3, f32[632,128]{1,0:T(8,128)S(1)} %collective-permute-done._.refs_3_, ...), custom_call_target="tpu_custom_call" | custom-call | bytes 7380000 | tf_op jit(solution)/shard_map/pallas_call | solution.py:594
  28.8 1.3 %collective-permute-start.4 = (f32[360,128]{1,0:T(8,128)S(1)}, f32[360,128]{1,0:T(8,128)S(1)}, u32[]{:S(2)}, u32[]{:S(2)}) collective-permute-start(f32[360,128]{1,0:T(8,128)S(1)} %get-tuple-element.36), channel_id=1, source_target_pairs={{0,2},{1,3},{2,0},{3,1},{4,6},{5,7},{6,4},{7,5},{8,10},{9,11},{10,... | collective-permute-start | bytes 552968 | tf_op jit(solution)/shard_map/ppermute | solution.py:543
  30.8 2.4 %collective-permute-done.8.north_ref = f32[376,128]{1,0:T(8,128)S(1)} collective-permute-done((f32[376,128]{1,0:T(8,128)S(1)}, f32[376,128]{1,0:T(8,128)S(1)}, u32[]{:S(2)}, u32[]{:S(2)}) %collective-permute-start.8) | collective-permute-done | bytes 192544 | tf_op jit(solution)/shard_map/ppermute | solution.py:592
  33.7 2.1 %shard_map.158.edge_ref = f32[1488,128]{1,0:T(8,128)S(1)} custom-call(s32[8]{0:T(128)S(1)} %copy-done.14, s32[8]{0:T(128)S(1)} %copy-done.15, f32[1488,128]{1,0:T(8,128)S(1)} %copy-done.3, f32[376,128]{1,0:T(8,128)S(1)} %collective-permute-done.7.south_ref, f32[376,128]{1,0:T(8,128)S(1)} %collective-permute-done.8.north_ref, ...), custom_call_target="tpu_custom_call" | custom-call | bytes 7380000 | tf_op jit(solution)/shard_map/pallas_call | solution.py:601
  35.8 3.0 %shard_map.159 = (f32[360,128]{1,0:T(8,128)S(1)}, f32[360,128]{1,0:T(8,128)S(1)}, f32[360,128]{1,0:T(8,128)S(1)}, f32[360,128]{1,0:T(8,128)S(1)}, f32[1488,128]{1,0:T(8,128)S(1)}) custom-call(s32[8]{0:T(128)S(1)} %copy-done.14, s32[8]{0:T(128)S(1)} %copy-done.15, f32[1488,128]{1,0:T(8,128)S(1)} %copy-done.3, f32[1488,128]{1,0:T(8,128)S(1)} %shard_map.158.edge_ref, ...), custom_call_target="tpu_custom_call" | custom-call | bytes 7380000 | tf_op jit(solution)/shard_map/pallas_call | solution.py:608
  39.2 1.3 %collective-permute-start.12 = (f32[360,128]{1,0:T(8,128)S(1)}, f32[360,128]{1,0:T(8,128)S(1)}, u32[]{:S(2)}, u32[]{:S(2)}) collective-permute-start(f32[360,128]{1,0:T(8,128)S(1)} %get-tuple-element.47), channel_id=1, source_target_pairs={{0,3},{1,2},{2,1},{3,0},{4,7},{5,6},{6,5},{7,4},{8,11},{9,10},{10,... | collective-permute-start | bytes 552968 | tf_op jit(solution)/shard_map/ppermute | solution.py:543
  40.6 2.9 %shard_map.161 = (f32[360,128]{1,0:T(8,128)S(1)}, f32[360,128]{1,0:T(8,128)S(1)}, f32[360,128]{1,0:T(8,128)S(1)}, f32[360,128]{1,0:T(8,128)S(1)}) custom-call(s32[8]{0:T(128)S(1)} %copy-done.14, s32[8]{0:T(128)S(1)} %copy-done.15, f32[1488,128]{1,0:T(8,128)S(1)} %copy-done.3, f32[1488,128]{1,0:T(8,128)S(1)} %get-tuple-element.41._.zonal_ref, ...), custom_call_target="tpu_custom_call" | custom-call | bytes 7380000 | tf_op jit(solution)/shard_map/pallas_call | solution.py:616
  44.0 1.6 %collective-permute-start.15 = (f32[360,128]{1,0:T(8,128)S(1)}, f32[360,128]{1,0:T(8,128)S(1)}, u32[]{:S(2)}, u32[]{:S(2)}) collective-permute-start(f32[360,128]{1,0:T(8,128)S(1)} %get-tuple-element.53), channel_id=1, source_target_pairs={{0,3},{1,2},{2,1},{3,0},{4,7},{5,6},{6,5},{7,4},{8,11},{9,10},{10,... | collective-permute-start | bytes 552968 | tf_op jit(solution)/shard_map/ppermute | solution.py:543
  46.4 3.3 %collective-permute-done.12.refs_6_ = f32[360,128]{1,0:T(8,128)S(1)} collective-permute-done((f32[360,128]{1,0:T(8,128)S(1)}, f32[360,128]{1,0:T(8,128)S(1)}, u32[]{:S(2)}, u32[]{:S(2)}) %collective-permute-start.12) | collective-permute-done | bytes 184352 | tf_op jit(solution)/shard_map/ppermute | solution.py:543
  49.6 1.9 %shard_map.160._ = f32[8,360,256]{2,1,0:T(8,128)} custom-call(f32[360,128]{1,0:T(8,128)S(1)} %get-tuple-element.35.refs_0_, f32[360,128]{1,0:T(8,128)S(1)} %collective-permute-done.4.refs_1_, f32[360,128]{1,0:T(8,128)S(1)} %collective-permute-done.5.refs_2_, f32[360,128]{1,0:T(8,128)S(1)} %collective-permute-done.6.refs_3_, ...), custom_call_target="tpu_custom_call" | custom-call | bytes 7380000 | tf_op jit(solution)/shard_map/pallas_call | solution.py:624
  51.6 1.4 %collective-permute-done.14.refs_1_ = f32[360,128]{1,0:T(8,128)S(1)} collective-permute-done((f32[360,128]{1,0:T(8,128)S(1)}, f32[360,128]{1,0:T(8,128)S(1)}, u32[]{:S(2)}, u32[]{:S(2)}) %collective-permute-start.14) | collective-permute-done | bytes 184352 | tf_op jit(solution)/shard_map/ppermute | solution.py:543
  53.0 4.1 %collective-permute-done.15.refs_2_ = f32[360,128]{1,0:T(8,128)S(1)} collective-permute-done((f32[360,128]{1,0:T(8,128)S(1)}, f32[360,128]{1,0:T(8,128)S(1)}, u32[]{:S(2)}, u32[]{:S(2)}) %collective-permute-start.15) | collective-permute-done | bytes 184352 | tf_op jit(solution)/shard_map/ppermute | solution.py:543
  57.1 1.4 %shard_map.162 = f32[8,360,256]{2,1,0:T(8,128)} custom-call(f32[8,360,256]{2,1,0:T(8,128)} %shard_map.160._, f32[8,360,128]{2,1,0:T(8,128)S(1)} %get-tuple-element.49.tile_ref, f32[360,128]{1,0:T(8,128)S(1)} %get-tuple-element.51.refs_0_, f32[360,128]{1,0:T(8,128)S(1)} %collective-permute-done.14.refs_1_, ...), custom_call_target="tpu_custom_call", output_to_operand_aliasing={{}: (0, {})} | custom-call | bytes 7380000 | tf_op jit(solution)/shard_map/pallas_call | solution.py:631
  (51 shorter events, 4.3 us)
Async XLA Ops:
  1.8 24.1 %copy-start.12 = (bf16[360,384]{1,0:T(8,128)(2,1)S(1)}, bf16[360,384]{1,0:T(8,128)(2,1)}, u32[]{:S(2)}) copy-start(bf16[360,384]{1,0:T(8,128)(2,1)} %constant.33.clone.refs_7_.refs_11_) | copy-start | bytes 829444
  1.8 24.1 %copy-start.13 = (bf16[360,384]{1,0:T(8,128)(2,1)S(1)}, bf16[360,384]{1,0:T(8,128)(2,1)}, u32[]{:S(2)}) copy-start(bf16[360,384]{1,0:T(8,128)(2,1)} %constant.32.clone.refs_6_.refs_10_) | copy-start | bytes 829444
  3.1 7.7 %collective-permute-start.1 = (f32[552,128]{1,0:T(8,128)S(1)}, f32[552,128]{1,0:T(8,128)S(1)}, u32[]{:S(2)}, u32[]{:S(2)}) collective-permute-start(f32[552,128]{1,0:T(8,128)S(1)} %get-tuple-element.32), channel_id=1, source_target_pairs={{0,2},{1,3},{2,0},{3,1},{4,6},{5,7},{6,4},{7,5},{8,10},{9,11},{10,... | collective-permute-start | bytes 847880 | tf_op jit(solution)/shard_map/ppermute | solution.py:543
  4.4 14.4 %collective-permute-start.2 = (f32[552,128]{1,0:T(8,128)S(1)}, f32[552,128]{1,0:T(8,128)S(1)}, u32[]{:S(2)}, u32[]{:S(2)}) collective-permute-start(f32[552,128]{1,0:T(8,128)S(1)} %get-tuple-element.33), channel_id=1, source_target_pairs={{0,3},{1,2},{2,1},{3,0},{4,7},{5,6},{6,5},{7,4},{8,11},{9,10},{10,... | collective-permute-start | bytes 847880 | tf_op jit(solution)/shard_map/ppermute | solution.py:543
  5.5 20.5 %copy-start.7 = (bf16[384,360]{1,0:T(8,128)(2,1)S(1)}, bf16[384,360]{1,0:T(8,128)(2,1)}, u32[]{:S(2)}) copy-start(bf16[384,360]{1,0:T(8,128)(2,1)} %constant.28.clone.refs_2_.refs_6_) | copy-start | bytes 829444
  5.5 20.5 %copy-start.8 = (bf16[384,360]{1,0:T(8,128)(2,1)S(1)}, bf16[384,360]{1,0:T(8,128)(2,1)}, u32[]{:S(2)}) copy-start(bf16[384,360]{1,0:T(8,128)(2,1)} %constant.27.clone.refs_1_.refs_5_) | copy-start | bytes 829444
  5.5 20.5 %copy-start.9 = (bf16[384,360]{1,0:T(8,128)(2,1)S(1)}, bf16[384,360]{1,0:T(8,128)(2,1)}, u32[]{:S(2)}) copy-start(bf16[384,360]{1,0:T(8,128)(2,1)} %constant.26.clone.refs_0_.refs_4_) | copy-start | bytes 829444
  5.5 20.5 %copy-start.10 = (bf16[360,384]{1,0:T(8,128)(2,1)S(1)}, bf16[360,384]{1,0:T(8,128)(2,1)}, u32[]{:S(2)}) copy-start(bf16[360,384]{1,0:T(8,128)(2,1)} %constant.35.clone.refs_9_.refs_13_) | copy-start | bytes 829444
  5.5 20.5 %copy-start.11 = (bf16[360,384]{1,0:T(8,128)(2,1)S(1)}, bf16[360,384]{1,0:T(8,128)(2,1)}, u32[]{:S(2)}) copy-start(bf16[360,384]{1,0:T(8,128)(2,1)} %constant.34.clone.refs_8_.refs_12_) | copy-start | bytes 829444
  5.5 13.3 %collective-permute-start.3 = (f32[552,128]{1,0:T(8,128)S(1)}, f32[552,128]{1,0:T(8,128)S(1)}, u32[]{:S(2)}, u32[]{:S(2)}) collective-permute-start(f32[552,128]{1,0:T(8,128)S(1)} %get-tuple-element.34), channel_id=1, source_target_pairs={{0,1},{1,0},{2,3},{3,2},{4,5},{5,4},{6,7},{7,6},{8,9},{9,8},{10,11... | collective-permute-start | bytes 847880 | tf_op jit(solution)/shard_map/ppermute | solution.py:543
  7.1 18.8 %collective-permute-start = (f32[632,128]{1,0:T(8,128)S(1)}, f32[632,128]{1,0:T(8,128)S(1)}, u32[]{:S(2)}, u32[]{:S(2)}) collective-permute-start(f32[632,128]{1,0:T(8,128)S(1)} %get-tuple-element.30), channel_id=1, source_target_pairs={{0,1},{1,0},{2,3},{3,2},{4,5},{5,4},{6,7},{7,6},{8,9},{9,8},{10,11... | collective-permute-start | bytes 970760 | tf_op jit(solution)/shard_map/ppermute | solution.py:543
  7.7 28.1 %collective-permute-start.9 = (f32[632,128]{1,0:T(8,128)S(1)}, f32[632,128]{1,0:T(8,128)S(1)}, u32[]{:S(2)}, u32[]{:S(2)}) collective-permute-start(f32[632,128]{1,0:T(8,128)S(1)} %get-tuple-element.43), channel_id=1, source_target_pairs={{0,2},{1,3},{2,0},{3,1},{4,6},{5,7},{6,4},{7,5},{8,10},{9,11},{10,... | collective-permute-start | bytes 970760 | tf_op jit(solution)/shard_map/ppermute | solution.py:543
  10.8 25.0 %collective-permute-start.10 = (f32[632,128]{1,0:T(8,128)S(1)}, f32[632,128]{1,0:T(8,128)S(1)}, u32[]{:S(2)}, u32[]{:S(2)}) collective-permute-start(f32[632,128]{1,0:T(8,128)S(1)} %get-tuple-element.44), channel_id=1, source_target_pairs={{0,3},{1,2},{2,1},{3,0},{4,7},{5,6},{6,5},{7,4},{8,11},{9,10},{10,... | collective-permute-start | bytes 970760 | tf_op jit(solution)/shard_map/ppermute | solution.py:543
  19.5 10.6 %collective-permute-start.7 = (f32[376,128]{1,0:T(8,128)S(1)}, f32[376,128]{1,0:T(8,128)S(1)}, u32[]{:S(2)}, u32[]{:S(2)}) collective-permute-start(f32[376,128]{1,0:T(8,128)S(1)} %get-tuple-element.39), channel_id=1, source_target_pairs={{0,4},{4,8},{8,12},{12,16},{16,20},{20,24},{24,28},{1,5},{5,9},{9,... | collective-permute-start | bytes 577544 | tf_op jit(solution)/shard_map/ppermute | solution.py:591
  22.7 10.6 %collective-permute-start.8 = (f32[376,128]{1,0:T(8,128)S(1)}, f32[376,128]{1,0:T(8,128)S(1)}, u32[]{:S(2)}, u32[]{:S(2)}) collective-permute-start(f32[376,128]{1,0:T(8,128)S(1)} %get-tuple-element.40), channel_id=1, source_target_pairs={{4,0},{8,4},{12,8},{16,12},{20,16},{24,20},{28,24},{5,1},{9,5},{13... | collective-permute-start | bytes 577544 | tf_op jit(solution)/shard_map/ppermute | solution.py:592
  28.8 14.6 %collective-permute-start.4 = (f32[360,128]{1,0:T(8,128)S(1)}, f32[360,128]{1,0:T(8,128)S(1)}, u32[]{:S(2)}, u32[]{:S(2)}) collective-permute-start(f32[360,128]{1,0:T(8,128)S(1)} %get-tuple-element.36), channel_id=1, source_target_pairs={{0,2},{1,3},{2,0},{3,1},{4,6},{5,7},{6,4},{7,5},{8,10},{9,11},{10,... | collective-permute-start | bytes 552968 | tf_op jit(solution)/shard_map/ppermute | solution.py:543
  30.1 13.5 %collective-permute-start.5 = (f32[360,128]{1,0:T(8,128)S(1)}, f32[360,128]{1,0:T(8,128)S(1)}, u32[]{:S(2)}, u32[]{:S(2)}) collective-permute-start(f32[360,128]{1,0:T(8,128)S(1)} %get-tuple-element.37), channel_id=1, source_target_pairs={{0,3},{1,2},{2,1},{3,0},{4,7},{5,6},{6,5},{7,4},{8,11},{9,10},{10,... | collective-permute-start | bytes 552968 | tf_op jit(solution)/shard_map/ppermute | solution.py:543
  33.2 10.8 %collective-permute-start.6 = (f32[360,128]{1,0:T(8,128)S(1)}, f32[360,128]{1,0:T(8,128)S(1)}, u32[]{:S(2)}, u32[]{:S(2)}) collective-permute-start(f32[360,128]{1,0:T(8,128)S(1)} %get-tuple-element.38), channel_id=1, source_target_pairs={{0,1},{1,0},{2,3},{3,2},{4,5},{5,4},{6,7},{7,6},{8,9},{9,8},{10,11... | collective-permute-start | bytes 552968 | tf_op jit(solution)/shard_map/ppermute | solution.py:543
  38.8 6.9 %collective-permute-start.11 = (f32[360,128]{1,0:T(8,128)S(1)}, f32[360,128]{1,0:T(8,128)S(1)}, u32[]{:S(2)}, u32[]{:S(2)}) collective-permute-start(f32[360,128]{1,0:T(8,128)S(1)} %get-tuple-element.46), channel_id=1, source_target_pairs={{0,2},{1,3},{2,0},{3,1},{4,6},{5,7},{6,4},{7,5},{8,10},{9,11},{10,... | collective-permute-start | bytes 552968 | tf_op jit(solution)/shard_map/ppermute | solution.py:543
  39.2 10.4 %collective-permute-start.12 = (f32[360,128]{1,0:T(8,128)S(1)}, f32[360,128]{1,0:T(8,128)S(1)}, u32[]{:S(2)}, u32[]{:S(2)}) collective-permute-start(f32[360,128]{1,0:T(8,128)S(1)} %get-tuple-element.47), channel_id=1, source_target_pairs={{0,3},{1,2},{2,1},{3,0},{4,7},{5,6},{6,5},{7,4},{8,11},{9,10},{10,... | collective-permute-start | bytes 552968 | tf_op jit(solution)/shard_map/ppermute | solution.py:543
  43.4 6.2 %collective-permute-start.13 = (f32[360,128]{1,0:T(8,128)S(1)}, f32[360,128]{1,0:T(8,128)S(1)}, u32[]{:S(2)}, u32[]{:S(2)}) collective-permute-start(f32[360,128]{1,0:T(8,128)S(1)} %get-tuple-element.48), channel_id=1, source_target_pairs={{0,1},{1,0},{2,3},{3,2},{4,5},{5,4},{6,7},{7,6},{8,9},{9,8},{10,11... | collective-permute-start | bytes 552968 | tf_op jit(solution)/shard_map/ppermute | solution.py:543
  43.7 9.3 %collective-permute-start.14 = (f32[360,128]{1,0:T(8,128)S(1)}, f32[360,128]{1,0:T(8,128)S(1)}, u32[]{:S(2)}, u32[]{:S(2)}) collective-permute-start(f32[360,128]{1,0:T(8,128)S(1)} %get-tuple-element.52), channel_id=1, source_target_pairs={{0,2},{1,3},{2,0},{3,1},{4,6},{5,7},{6,4},{7,5},{8,10},{9,11},{10,... | collective-permute-start | bytes 552968 | tf_op jit(solution)/shard_map/ppermute | solution.py:543
  44.0 13.0 %collective-permute-start.15 = (f32[360,128]{1,0:T(8,128)S(1)}, f32[360,128]{1,0:T(8,128)S(1)}, u32[]{:S(2)}, u32[]{:S(2)}) collective-permute-start(f32[360,128]{1,0:T(8,128)S(1)} %get-tuple-element.53), channel_id=1, source_target_pairs={{0,3},{1,2},{2,1},{3,0},{4,7},{5,6},{6,5},{7,4},{8,11},{9,10},{10,... | collective-permute-start | bytes 552968 | tf_op jit(solution)/shard_map/ppermute | solution.py:543
  45.7 11.4 %collective-permute-start.16 = (f32[360,128]{1,0:T(8,128)S(1)}, f32[360,128]{1,0:T(8,128)S(1)}, u32[]{:S(2)}, u32[]{:S(2)}) collective-permute-start(f32[360,128]{1,0:T(8,128)S(1)} %get-tuple-element.54), channel_id=1, source_target_pairs={{0,1},{1,0},{2,3},{3,2},{4,5},{5,4},{6,7},{7,6},{8,9},{9,8},{10,11... | collective-permute-start | bytes 552968 | tf_op jit(solution)/shard_map/ppermute | solution.py:543
  (9 other events, 149.7 us)

commit v4 on v3

--- a/solution.py
+++ b/solution.py
@@ -229,7 +229,7 @@
     return round_up(-(-width * 3 // 4), 8)
 
 
-def press_kernel(part, wind_ref, tile_ref, *refs):
+def press_kernel(part, wind_ref, tile_ref, _, *refs):
     packs, vert_ref = refs[:4], refs[4]
     rows, width, _ = tile_ref.shape
     levels = LANES // 2
@@ -292,7 +292,7 @@
     south_ref[2 * lines :] = jnp.full((8, LANES), cut_value(flag_ref, cut_ref, 0, nlon), F32)
 
 
-def edge_spec_kernel(bounds, part, skip, flag_ref, cut_ref, mode_ref, south_ref, north_ref, *refs):
+def edge_spec_kernel(bounds, part, skip, flag_ref, cut_ref, mode_ref, south_ref, north_ref, _, *refs):
     blocks, forward, spec_ref = natural(refs[:4]), refs[4:10], refs[10]
     lines = blocks[0].shape[0] - skip
     width = skip - 8
@@ -319,7 +319,7 @@
         spec_ref[low:high] = value * damp[low:high]
 
 
-def merid_spec_kernel(bounds, part, flag_ref, cut_ref, mode_ref, edge_ref, _, *refs):
+def merid_spec_kernel(bounds, part, flag_ref, cut_ref, mode_ref, edge_ref, *refs):
     blocks, forward, inverse, outs, spec_ref = natural(refs[:4]), refs[4:10], refs[10:16], refs[16:20], refs[20]
     rows = flag_ref.shape[0]
     width = outs[0].shape[0]
@@ -577,9 +577,9 @@
     *packs, vert = call(
         functools.partial(press_kernel, part),
         [f32(*second)] * 4 + [f32(*full)],
-        [low_tile, high_tile],
+        [low_tile, high_tile, ANY],
         [whole(second)] * 4 + [whole(full)],
-    )(state, state)
+    )(state, state, first_circle[1])
     second_circle = exchange(packs)
 
     to_north, to_south = call(
@@ -601,16 +601,16 @@
     edge_spec = call(
         functools.partial(edge_spec_kernel, bounds, part, skip),
         f32(*spectrum),
-        [SMEM] * 2 + [whole(mode.shape)] + [whole(rims)] * 2 + [whole(first)] * 4 + table_specs[:6],
+        [SMEM] * 2 + [whole(mode.shape)] + [whole(rims)] * 2 + [ANY] + [whole(first)] * 4 + table_specs[:6],
         whole(spectrum),
-    )(filter_flag, cutoff, mode, from_south, from_north, *first_circle, *forward)
+    )(filter_flag, cutoff, mode, from_south, from_north, zonal_spec, *first_circle, *forward)
 
     *merid_parts, merid_spec = call(
         functools.partial(merid_spec_kernel, bounds, part),
         [f32(*block)] * 4 + [f32(*spectrum)],
-        [SMEM] * 2 + [whole(mode.shape), whole(spectrum), ANY] + [whole(second)] * 4 + table_specs,
+        [SMEM] * 2 + [whole(mode.shape), whole(spectrum)] + [whole(second)] * 4 + table_specs,
         [whole(block)] * 4 + [whole(spectrum)],
-    )(filter_flag, cutoff, mode, edge_spec, zonal_spec, *second_circle, *forward, *inverse)
+    )(filter_flag, cutoff, mode, edge_spec, *second_circle, *forward, *inverse)
     merid_back = exchange(merid_parts)
 
     press_parts = call(

time: 58.8 us -> 58 us (0.986)
  starting transfers between devices: 21.5 us -> 20.4 us
    ppermute x15, starting transfers between devices: 15.2 us -> 14.1 us  [exchange(): lax.ppermute(blocks[step], 'lon', pairs[step])]
  transfers between devices with their start and end apart: 17 -> 17, of which waited for: 6 -> 6; matrix products, arithmetic and copies ran while one was open for 0% -> 0% of each run, Pallas kernels for 25% -> 26%
where the time goes in v4:
time: 58 us; the launch traced here: 57.6 us
  starting transfers between devices  20.4 us (35%)
  Pallas kernels  17.4 us (30%)
  waiting for transfers between devices  17.4 us (30%)
  local copies, waits for them, and re-layouts  1.91 us (3%)
    ppermute x15, waiting for transfers between devices, exchange(): lax.ppermute(blocks[step], 'lon', pairs[step])  15 us
    ppermute x15, starting transfers between devices, exchange(): lax.ppermute(blocks[step], 'lon', pairs[step])  14.1 us
    ppermute x1, starting transfers between devices, packed_body(): lax.ppermute(to_south, 'lat', [(i + 1, i) for i in range(bands - 1)])  3.24 us
    ppermute x1, starting transfers between devices, packed_body(): lax.ppermute(to_north, 'lat', [(i, i + 1) for i in range(bands - 1)])  3.12 us
    pallas_call x1, Pallas kernels, packed_body(): call(functools.partial(merid_spec_kernel, bounds, part), [f32(*block)] *...  3 us
    pallas_call x1, Pallas kernels, packed_body(): call(functools.partial(press_back_kernel, bounds, part), [f32(*block)] *...  2.81 us
    pallas_call x1, Pallas kernels, packed_body(): call(functools.partial(zonal_spec_kernel, bounds, part), [f32(*block)] *...  2.77 us
    ppermute x1, waiting for transfers between devices, packed_body(): lax.ppermute(to_south, 'lat', [(i + 1, i) for i in range(bands - 1)])  2.43 us
  transfers between devices with their start and end apart: 17, of which 6 were waited for; matrix products, arithmetic and copies ran while one was open for 0% of the time, Pallas kernels for 26%

profile of v4, /device:TPU:17, one launch (start us, length us, event | category | flops | bytes accessed | tf_op | source)
XLA Modules:
  0.0 57.6 jit_solution(8710864798394630494)
XLA Ops:
  0.0 1.8 %copy-done = f32[8,360,256]{2,1,0:T(8,128)S(1)} copy-done((f32[8,360,256]{2,1,0:T(8,128)S(1)}, f32[8,360,256]{2,1,0:T(8,128)}, u32[]{:S(2)}) %copy-start) | copy-done | bytes 2949144
  1.8 1.2 %shard_map.154 = (f32[552,128]{1,0:T(8,128)S(1)}, f32[552,128]{1,0:T(8,128)S(1)}, f32[552,128]{1,0:T(8,128)S(1)}, f32[552,128]{1,0:T(8,128)S(1)}) custom-call(f32[8,360,256]{2,1,0:T(8,128)S(1)} %copy-done, f32[8,360,256]{2,1,0:T(8,128)S(1)} %copy-done), custom_call_target="tpu_custom_call" | custom-call | bytes 7380000 | tf_op jit(solution)/shard_map/pallas_call | solution.py:569
  3.1 1.3 %collective-permute-start = (f32[552,128]{1,0:T(8,128)S(1)}, f32[552,128]{1,0:T(8,128)S(1)}, u32[]{:S(2)}, u32[]{:S(2)}) collective-permute-start(f32[552,128]{1,0:T(8,128)S(1)} %get-tuple-element.30), channel_id=1, source_target_pairs={{0,2},{1,3},{2,0},{3,1},{4,6},{5,7},{6,4},{7,5},{8,10},{9,11},{10,... | collective-permute-start | bytes 847880 | tf_op jit(solution)/shard_map/ppermute | solution.py:543
  4.4 1.1 %collective-permute-start.2 = (f32[552,128]{1,0:T(8,128)S(1)}, f32[552,128]{1,0:T(8,128)S(1)}, u32[]{:S(2)}, u32[]{:S(2)}) collective-permute-start(f32[552,128]{1,0:T(8,128)S(1)} %get-tuple-element.33), channel_id=1, source_target_pairs={{0,3},{1,2},{2,1},{3,0},{4,7},{5,6},{6,5},{7,4},{8,11},{9,10},{10,... | collective-permute-start | bytes 847880 | tf_op jit(solution)/shard_map/ppermute | solution.py:543
  5.6 5.2 %collective-permute-done._.q2.refs_1_ = f32[552,128]{1,0:T(8,128)S(1)} collective-permute-done((f32[552,128]{1,0:T(8,128)S(1)}, f32[552,128]{1,0:T(8,128)S(1)}, u32[]{:S(2)}, u32[]{:S(2)}) %collective-permute-start) | collective-permute-done | bytes 282656 | tf_op jit(solution)/shard_map/ppermute | solution.py:543
  10.8 1.5 %shard_map.155 = (f32[632,128]{1,0:T(8,128)S(1)}, f32[632,128]{1,0:T(8,128)S(1)}, f32[632,128]{1,0:T(8,128)S(1)}, f32[632,128]{1,0:T(8,128)S(1)}, f32[8,360,128]{2,1,0:T(8,128)S(1)}) custom-call(f32[8,360,256]{2,1,0:T(8,128)S(1)} %copy-done, f32[8,360,256]{2,1,0:T(8,128)S(1)} %copy-done, f32[552,128]{1,0:T(8,128)S(1)} %collective-permute-done._.q2.refs_1_), custom_call_target="tpu_custom_call" | custom-call | bytes 7380000 | tf_op jit(solution)/shard_map/pallas_call | solution.py:577
  12.3 2.8 %collective-permute-start.1 = (f32[632,128]{1,0:T(8,128)S(1)}, f32[632,128]{1,0:T(8,128)S(1)}, u32[]{:S(2)}, u32[]{:S(2)}) collective-permute-start(f32[632,128]{1,0:T(8,128)S(1)} %get-tuple-element.31), channel_id=1, source_target_pairs={{0,1},{1,0},{2,3},{3,2},{4,5},{5,4},{6,7},{7,6},{8,9},{9,8},{10,11... | collective-permute-start | bytes 970760 | tf_op jit(solution)/shard_map/ppermute | solution.py:543
  15.0 1.3 %collective-permute-start.9 = (f32[632,128]{1,0:T(8,128)S(1)}, f32[632,128]{1,0:T(8,128)S(1)}, u32[]{:S(2)}, u32[]{:S(2)}) collective-permute-start(f32[632,128]{1,0:T(8,128)S(1)} %get-tuple-element.43), channel_id=1, source_target_pairs={{0,2},{1,3},{2,0},{3,1},{4,6},{5,7},{6,4},{7,5},{8,10},{9,11},{10,... | collective-permute-start | bytes 970760 | tf_op jit(solution)/shard_map/ppermute | solution.py:543
  16.7 1.1 %collective-permute-done.2.q3.refs_2_ = f32[552,128]{1,0:T(8,128)S(1)} collective-permute-done((f32[552,128]{1,0:T(8,128)S(1)}, f32[552,128]{1,0:T(8,128)S(1)}, u32[]{:S(2)}, u32[]{:S(2)}) %collective-permute-start.2) | collective-permute-done | bytes 282656 | tf_op jit(solution)/shard_map/ppermute | solution.py:543
  18.5 3.1 %collective-permute-start.7 = (f32[376,128]{1,0:T(8,128)S(1)}, f32[376,128]{1,0:T(8,128)S(1)}, u32[]{:S(2)}, u32[]{:S(2)}) collective-permute-start(f32[376,128]{1,0:T(8,128)S(1)} %get-tuple-element.39), channel_id=1, source_target_pairs={{0,4},{4,8},{8,12},{12,16},{16,20},{20,24},{24,28},{1,5},{5,9},{9,... | collective-permute-start | bytes 577544 | tf_op jit(solution)/shard_map/ppermute | solution.py:591
  21.6 3.2 %collective-permute-start.8 = (f32[376,128]{1,0:T(8,128)S(1)}, f32[376,128]{1,0:T(8,128)S(1)}, u32[]{:S(2)}, u32[]{:S(2)}) collective-permute-start(f32[376,128]{1,0:T(8,128)S(1)} %get-tuple-element.40), channel_id=1, source_target_pairs={{4,0},{8,4},{12,8},{16,12},{20,16},{24,20},{28,24},{5,1},{9,5},{13... | collective-permute-start | bytes 577544 | tf_op jit(solution)/shard_map/ppermute | solution.py:592
  25.0 2.8 %shard_map.156 = (f32[360,128]{1,0:T(8,128)S(1)}, f32[360,128]{1,0:T(8,128)S(1)}, f32[360,128]{1,0:T(8,128)S(1)}, f32[360,128]{1,0:T(8,128)S(1)}, f32[1488,128]{1,0:T(8,128)S(1)}) custom-call(s32[8]{0:T(128)S(1)} %copy-done.14, s32[8]{0:T(128)S(1)} %copy-done.15, f32[1488,128]{1,0:T(8,128)S(1)} %copy-done.3, ...), custom_call_target="tpu_custom_call" | custom-call | bytes 7380000 | tf_op jit(solution)/shard_map/pallas_call | solution.py:594
  27.8 1.3 %collective-permute-start.4 = (f32[360,128]{1,0:T(8,128)S(1)}, f32[360,128]{1,0:T(8,128)S(1)}, u32[]{:S(2)}, u32[]{:S(2)}) collective-permute-start(f32[360,128]{1,0:T(8,128)S(1)} %get-tuple-element.36), channel_id=1, source_target_pairs={{0,2},{1,3},{2,0},{3,1},{4,6},{5,7},{6,4},{7,5},{8,10},{9,11},{10,... | collective-permute-start | bytes 552968 | tf_op jit(solution)/shard_map/ppermute | solution.py:543
  29.8 2.4 %collective-permute-done.8.north_ref = f32[376,128]{1,0:T(8,128)S(1)} collective-permute-done((f32[376,128]{1,0:T(8,128)S(1)}, f32[376,128]{1,0:T(8,128)S(1)}, u32[]{:S(2)}, u32[]{:S(2)}) %collective-permute-start.8) | collective-permute-done | bytes 192544 | tf_op jit(solution)/shard_map/ppermute | solution.py:592
  32.7 2.1 %shard_map.158.edge_ref = f32[1488,128]{1,0:T(8,128)S(1)} custom-call(s32[8]{0:T(128)S(1)} %copy-done.14, s32[8]{0:T(128)S(1)} %copy-done.15, f32[1488,128]{1,0:T(8,128)S(1)} %copy-done.3, f32[376,128]{1,0:T(8,128)S(1)} %collective-permute-done.7.south_ref, f32[376,128]{1,0:T(8,128)S(1)} %collective-permute-done.8.north_ref, ...), custom_call_target="tpu_custom_call" | custom-call | bytes 7380000 | tf_op jit(solution)/shard_map/pallas_call | solution.py:601
  34.8 3.0 %shard_map.159 = (f32[360,128]{1,0:T(8,128)S(1)}, f32[360,128]{1,0:T(8,128)S(1)}, f32[360,128]{1,0:T(8,128)S(1)}, f32[360,128]{1,0:T(8,128)S(1)}, f32[1488,128]{1,0:T(8,128)S(1)}) custom-call(s32[8]{0:T(128)S(1)} %copy-done.14, s32[8]{0:T(128)S(1)} %copy-done.15, f32[1488,128]{1,0:T(8,128)S(1)} %copy-done.3, f32[1488,128]{1,0:T(8,128)S(1)} %shard_map.158.edge_ref, ...), custom_call_target="tpu_custom_call" | custom-call | bytes 7380000 | tf_op jit(solution)/shard_map/pallas_call | solution.py:608
  37.8 1.2 %collective-permute-start.11 = (f32[360,128]{1,0:T(8,128)S(1)}, f32[360,128]{1,0:T(8,128)S(1)}, u32[]{:S(2)}, u32[]{:S(2)}) collective-permute-start(f32[360,128]{1,0:T(8,128)S(1)} %get-tuple-element.46), channel_id=1, source_target_pairs={{0,2},{1,3},{2,0},{3,1},{4,6},{5,7},{6,4},{7,5},{8,10},{9,11},{10,... | collective-permute-start | bytes 552968 | tf_op jit(solution)/shard_map/ppermute | solution.py:543
  39.5 2.8 %shard_map.161 = (f32[360,128]{1,0:T(8,128)S(1)}, f32[360,128]{1,0:T(8,128)S(1)}, f32[360,128]{1,0:T(8,128)S(1)}, f32[360,128]{1,0:T(8,128)S(1)}) custom-call(s32[8]{0:T(128)S(1)} %copy-done.14, s32[8]{0:T(128)S(1)} %copy-done.15, f32[1488,128]{1,0:T(8,128)S(1)} %copy-done.3, f32[1488,128]{1,0:T(8,128)S(1)} %get-tuple-element.41._.zonal_ref, ...), custom_call_target="tpu_custom_call" | custom-call | bytes 7380000 | tf_op jit(solution)/shard_map/pallas_call | solution.py:616
  42.6 1.1 %collective-permute-start.14 = (f32[360,128]{1,0:T(8,128)S(1)}, f32[360,128]{1,0:T(8,128)S(1)}, u32[]{:S(2)}, u32[]{:S(2)}) collective-permute-start(f32[360,128]{1,0:T(8,128)S(1)} %get-tuple-element.52), channel_id=1, source_target_pairs={{0,2},{1,3},{2,0},{3,1},{4,6},{5,7},{6,4},{7,5},{8,10},{9,11},{10,... | collective-permute-start | bytes 552968 | tf_op jit(solution)/shard_map/ppermute | solution.py:543
  45.3 3.3 %collective-permute-done.12.refs_6_ = f32[360,128]{1,0:T(8,128)S(1)} collective-permute-done((f32[360,128]{1,0:T(8,128)S(1)}, f32[360,128]{1,0:T(8,128)S(1)}, u32[]{:S(2)}, u32[]{:S(2)}) %collective-permute-start.12) | collective-permute-done | bytes 184352 | tf_op jit(solution)/shard_map/ppermute | solution.py:543
  48.6 1.9 %shard_map.160._ = f32[8,360,256]{2,1,0:T(8,128)} custom-call(f32[360,128]{1,0:T(8,128)S(1)} %get-tuple-element.35.refs_0_, f32[360,128]{1,0:T(8,128)S(1)} %collective-permute-done.4.refs_1_, f32[360,128]{1,0:T(8,128)S(1)} %collective-permute-done.5.refs_2_, f32[360,128]{1,0:T(8,128)S(1)} %collective-permute-done.6.refs_3_, ...), custom_call_target="tpu_custom_call" | custom-call | bytes 7380000 | tf_op jit(solution)/shard_map/pallas_call | solution.py:624
  50.5 1.4 %collective-permute-done.14.refs_1_ = f32[360,128]{1,0:T(8,128)S(1)} collective-permute-done((f32[360,128]{1,0:T(8,128)S(1)}, f32[360,128]{1,0:T(8,128)S(1)}, u32[]{:S(2)}, u32[]{:S(2)}) %collective-permute-start.14) | collective-permute-done | bytes 184352 | tf_op jit(solution)/shard_map/ppermute | solution.py:543
  51.9 4.1 %collective-permute-done.15.refs_2_ = f32[360,128]{1,0:T(8,128)S(1)} collective-permute-done((f32[360,128]{1,0:T(8,128)S(1)}, f32[360,128]{1,0:T(8,128)S(1)}, u32[]{:S(2)}, u32[]{:S(2)}) %collective-permute-start.15) | collective-permute-done | bytes 184352 | tf_op jit(solution)/shard_map/ppermute | solution.py:543
  56.0 1.4 %shard_map.162 = f32[8,360,256]{2,1,0:T(8,128)} custom-call(f32[8,360,256]{2,1,0:T(8,128)} %shard_map.160._, f32[8,360,128]{2,1,0:T(8,128)S(1)} %get-tuple-element.49.tile_ref, f32[360,128]{1,0:T(8,128)S(1)} %get-tuple-element.51.refs_0_, f32[360,128]{1,0:T(8,128)S(1)} %collective-permute-done.14.refs_1_, ...), custom_call_target="tpu_custom_call", output_to_operand_aliasing={{}: (0, {})} | custom-call | bytes 7380000 | tf_op jit(solution)/shard_map/pallas_call | solution.py:631
  (51 shorter events, 4.9 us)
Async XLA Ops:
  1.8 23.1 %copy-start.13 = (bf16[360,384]{1,0:T(8,128)(2,1)S(1)}, bf16[360,384]{1,0:T(8,128)(2,1)}, u32[]{:S(2)}) copy-start(bf16[360,384]{1,0:T(8,128)(2,1)} %constant.32.clone.refs_6_.refs_10_) | copy-start | bytes 829444
  3.1 7.7 %collective-permute-start = (f32[552,128]{1,0:T(8,128)S(1)}, f32[552,128]{1,0:T(8,128)S(1)}, u32[]{:S(2)}, u32[]{:S(2)}) collective-permute-start(f32[552,128]{1,0:T(8,128)S(1)} %get-tuple-element.30), channel_id=1, source_target_pairs={{0,2},{1,3},{2,0},{3,1},{4,6},{5,7},{6,4},{7,5},{8,10},{9,11},{10,... | collective-permute-start | bytes 847880 | tf_op jit(solution)/shard_map/ppermute | solution.py:543
  4.4 13.4 %collective-permute-start.2 = (f32[552,128]{1,0:T(8,128)S(1)}, f32[552,128]{1,0:T(8,128)S(1)}, u32[]{:S(2)}, u32[]{:S(2)}) collective-permute-start(f32[552,128]{1,0:T(8,128)S(1)} %get-tuple-element.33), channel_id=1, source_target_pairs={{0,3},{1,2},{2,1},{3,0},{4,7},{5,6},{6,5},{7,4},{8,11},{9,10},{10,... | collective-permute-start | bytes 847880 | tf_op jit(solution)/shard_map/ppermute | solution.py:543
  5.4 19.5 %copy-start.7 = (bf16[384,360]{1,0:T(8,128)(2,1)S(1)}, bf16[384,360]{1,0:T(8,128)(2,1)}, u32[]{:S(2)}) copy-start(bf16[384,360]{1,0:T(8,128)(2,1)} %constant.28.clone.refs_2_.refs_6_) | copy-start | bytes 829444
  5.5 19.5 %copy-start.8 = (bf16[384,360]{1,0:T(8,128)(2,1)S(1)}, bf16[384,360]{1,0:T(8,128)(2,1)}, u32[]{:S(2)}) copy-start(bf16[384,360]{1,0:T(8,128)(2,1)} %constant.27.clone.refs_1_.refs_5_) | copy-start | bytes 829444
  5.5 19.5 %copy-start.9 = (bf16[384,360]{1,0:T(8,128)(2,1)S(1)}, bf16[384,360]{1,0:T(8,128)(2,1)}, u32[]{:S(2)}) copy-start(bf16[384,360]{1,0:T(8,128)(2,1)} %constant.26.clone.refs_0_.refs_4_) | copy-start | bytes 829444
  5.5 19.5 %copy-start.10 = (bf16[360,384]{1,0:T(8,128)(2,1)S(1)}, bf16[360,384]{1,0:T(8,128)(2,1)}, u32[]{:S(2)}) copy-start(bf16[360,384]{1,0:T(8,128)(2,1)} %constant.35.clone.refs_9_.refs_13_) | copy-start | bytes 829444
  5.5 19.5 %copy-start.11 = (bf16[360,384]{1,0:T(8,128)(2,1)S(1)}, bf16[360,384]{1,0:T(8,128)(2,1)}, u32[]{:S(2)}) copy-start(bf16[360,384]{1,0:T(8,128)(2,1)} %constant.34.clone.refs_8_.refs_12_) | copy-start | bytes 829444
  5.5 19.5 %copy-start.12 = (bf16[360,384]{1,0:T(8,128)(2,1)S(1)}, bf16[360,384]{1,0:T(8,128)(2,1)}, u32[]{:S(2)}) copy-start(bf16[360,384]{1,0:T(8,128)(2,1)} %constant.33.clone.refs_7_.refs_11_) | copy-start | bytes 829444
  5.5 12.3 %collective-permute-start.3 = (f32[552,128]{1,0:T(8,128)S(1)}, f32[552,128]{1,0:T(8,128)S(1)}, u32[]{:S(2)}, u32[]{:S(2)}) collective-permute-start(f32[552,128]{1,0:T(8,128)S(1)} %get-tuple-element.34), channel_id=1, source_target_pairs={{0,1},{1,0},{2,3},{3,2},{4,5},{5,4},{6,7},{7,6},{8,9},{9,8},{10,11... | collective-permute-start | bytes 847880 | tf_op jit(solution)/shard_map/ppermute | solution.py:543
  12.3 12.6 %collective-permute-start.1 = (f32[632,128]{1,0:T(8,128)S(1)}, f32[632,128]{1,0:T(8,128)S(1)}, u32[]{:S(2)}, u32[]{:S(2)}) collective-permute-start(f32[632,128]{1,0:T(8,128)S(1)} %get-tuple-element.31), channel_id=1, source_target_pairs={{0,1},{1,0},{2,3},{3,2},{4,5},{5,4},{6,7},{7,6},{8,9},{9,8},{10,11... | collective-permute-start | bytes 970760 | tf_op jit(solution)/shard_map/ppermute | solution.py:543
  15.0 19.7 %collective-permute-start.9 = (f32[632,128]{1,0:T(8,128)S(1)}, f32[632,128]{1,0:T(8,128)S(1)}, u32[]{:S(2)}, u32[]{:S(2)}) collective-permute-start(f32[632,128]{1,0:T(8,128)S(1)} %get-tuple-element.43), channel_id=1, source_target_pairs={{0,2},{1,3},{2,0},{3,1},{4,6},{5,7},{6,4},{7,5},{8,10},{9,11},{10,... | collective-permute-start | bytes 970760 | tf_op jit(solution)/shard_map/ppermute | solution.py:543
  16.3 18.5 %collective-permute-start.10 = (f32[632,128]{1,0:T(8,128)S(1)}, f32[632,128]{1,0:T(8,128)S(1)}, u32[]{:S(2)}, u32[]{:S(2)}) collective-permute-start(f32[632,128]{1,0:T(8,128)S(1)} %get-tuple-element.44), channel_id=1, source_target_pairs={{0,3},{1,2},{2,1},{3,0},{4,7},{5,6},{6,5},{7,4},{8,11},{9,10},{10,... | collective-permute-start | bytes 970760 | tf_op jit(solution)/shard_map/ppermute | solution.py:543
  18.5 10.6 %collective-permute-start.7 = (f32[376,128]{1,0:T(8,128)S(1)}, f32[376,128]{1,0:T(8,128)S(1)}, u32[]{:S(2)}, u32[]{:S(2)}) collective-permute-start(f32[376,128]{1,0:T(8,128)S(1)} %get-tuple-element.39), channel_id=1, source_target_pairs={{0,4},{4,8},{8,12},{12,16},{16,20},{20,24},{24,28},{1,5},{5,9},{9,... | collective-permute-start | bytes 577544 | tf_op jit(solution)/shard_map/ppermute | solution.py:591
  21.6 10.6 %collective-permute-start.8 = (f32[376,128]{1,0:T(8,128)S(1)}, f32[376,128]{1,0:T(8,128)S(1)}, u32[]{:S(2)}, u32[]{:S(2)}) collective-permute-start(f32[376,128]{1,0:T(8,128)S(1)} %get-tuple-element.40), channel_id=1, source_target_pairs={{4,0},{8,4},{12,8},{16,12},{20,16},{24,20},{28,24},{5,1},{9,5},{13... | collective-permute-start | bytes 577544 | tf_op jit(solution)/shard_map/ppermute | solution.py:592
  27.8 14.5 %collective-permute-start.4 = (f32[360,128]{1,0:T(8,128)S(1)}, f32[360,128]{1,0:T(8,128)S(1)}, u32[]{:S(2)}, u32[]{:S(2)}) collective-permute-start(f32[360,128]{1,0:T(8,128)S(1)} %get-tuple-element.36), channel_id=1, source_target_pairs={{0,2},{1,3},{2,0},{3,1},{4,6},{5,7},{6,4},{7,5},{8,10},{9,11},{10,... | collective-permute-start | bytes 552968 | tf_op jit(solution)/shard_map/ppermute | solution.py:543
  29.1 13.5 %collective-permute-start.5 = (f32[360,128]{1,0:T(8,128)S(1)}, f32[360,128]{1,0:T(8,128)S(1)}, u32[]{:S(2)}, u32[]{:S(2)}) collective-permute-start(f32[360,128]{1,0:T(8,128)S(1)} %get-tuple-element.37), channel_id=1, source_target_pairs={{0,3},{1,2},{2,1},{3,0},{4,7},{5,6},{6,5},{7,4},{8,11},{9,10},{10,... | collective-permute-start | bytes 552968 | tf_op jit(solution)/shard_map/ppermute | solution.py:543
  32.2 11.5 %collective-permute-start.6 = (f32[360,128]{1,0:T(8,128)S(1)}, f32[360,128]{1,0:T(8,128)S(1)}, u32[]{:S(2)}, u32[]{:S(2)}) collective-permute-start(f32[360,128]{1,0:T(8,128)S(1)} %get-tuple-element.38), channel_id=1, source_target_pairs={{0,1},{1,0},{2,3},{3,2},{4,5},{5,4},{6,7},{7,6},{8,9},{9,8},{10,11... | collective-permute-start | bytes 552968 | tf_op jit(solution)/shard_map/ppermute | solution.py:543
  37.8 6.8 %collective-permute-start.11 = (f32[360,128]{1,0:T(8,128)S(1)}, f32[360,128]{1,0:T(8,128)S(1)}, u32[]{:S(2)}, u32[]{:S(2)}) collective-permute-start(f32[360,128]{1,0:T(8,128)S(1)} %get-tuple-element.46), channel_id=1, source_target_pairs={{0,2},{1,3},{2,0},{3,1},{4,6},{5,7},{6,4},{7,5},{8,10},{9,11},{10,... | collective-permute-start | bytes 552968 | tf_op jit(solution)/shard_map/ppermute | solution.py:543
  38.9 9.7 %collective-permute-start.12 = (f32[360,128]{1,0:T(8,128)S(1)}, f32[360,128]{1,0:T(8,128)S(1)}, u32[]{:S(2)}, u32[]{:S(2)}) collective-permute-start(f32[360,128]{1,0:T(8,128)S(1)} %get-tuple-element.47), channel_id=1, source_target_pairs={{0,3},{1,2},{2,1},{3,0},{4,7},{5,6},{6,5},{7,4},{8,11},{9,10},{10,... | collective-permute-start | bytes 552968 | tf_op jit(solution)/shard_map/ppermute | solution.py:543
  42.4 6.2 %collective-permute-start.13 = (f32[360,128]{1,0:T(8,128)S(1)}, f32[360,128]{1,0:T(8,128)S(1)}, u32[]{:S(2)}, u32[]{:S(2)}) collective-permute-start(f32[360,128]{1,0:T(8,128)S(1)} %get-tuple-element.48), channel_id=1, source_target_pairs={{0,1},{1,0},{2,3},{3,2},{4,5},{5,4},{6,7},{7,6},{8,9},{9,8},{10,11... | collective-permute-start | bytes 552968 | tf_op jit(solution)/shard_map/ppermute | solution.py:543
  42.6 9.3 %collective-permute-start.14 = (f32[360,128]{1,0:T(8,128)S(1)}, f32[360,128]{1,0:T(8,128)S(1)}, u32[]{:S(2)}, u32[]{:S(2)}) collective-permute-start(f32[360,128]{1,0:T(8,128)S(1)} %get-tuple-element.52), channel_id=1, source_target_pairs={{0,2},{1,3},{2,0},{3,1},{4,6},{5,7},{6,4},{7,5},{8,10},{9,11},{10,... | collective-permute-start | bytes 552968 | tf_op jit(solution)/shard_map/ppermute | solution.py:543
  43.7 12.3 %collective-permute-start.15 = (f32[360,128]{1,0:T(8,128)S(1)}, f32[360,128]{1,0:T(8,128)S(1)}, u32[]{:S(2)}, u32[]{:S(2)}) collective-permute-start(f32[360,128]{1,0:T(8,128)S(1)} %get-tuple-element.53), channel_id=1, source_target_pairs={{0,3},{1,2},{2,1},{3,0},{4,7},{5,6},{6,5},{7,4},{8,11},{9,10},{10,... | collective-permute-start | bytes 552968 | tf_op jit(solution)/shard_map/ppermute | solution.py:543
  44.6 11.5 %collective-permute-start.16 = (f32[360,128]{1,0:T(8,128)S(1)}, f32[360,128]{1,0:T(8,128)S(1)}, u32[]{:S(2)}, u32[]{:S(2)}) collective-permute-start(f32[360,128]{1,0:T(8,128)S(1)} %get-tuple-element.54), channel_id=1, source_target_pairs={{0,1},{1,0},{2,3},{3,2},{4,5},{5,4},{6,7},{7,6},{8,9},{9,8},{10,11... | collective-permute-start | bytes 552968 | tf_op jit(solution)/shard_map/ppermute | solution.py:543
  (9 other events, 115.8 us)

commit v5 on v4

--- a/solution.py
+++ b/solution.py
@@ -178,7 +178,6 @@
 def zonal_kernel(part, wind_ref, tile_ref, *refs):
     packs, zonal_ref = refs[:4], refs[4]
     rows, width, _ = tile_ref.shape
-    last = rows - 1
     levels = LANES // 2
     nlat = rows * lax.axis_size("lat")
     me = lax.axis_index("lon")
@@ -208,17 +207,23 @@
     masks8 = group_masks(8, part)
     put(packs, width, partner_order(transpose_groups(sides, masks8, part, range(4, 8)), me))
 
+def edge_kernel(part, *refs):
+    (wind_first, wind_last), (tile_first, tile_last), packs = refs[:2], refs[2:4], refs[4:]
+    _, width, _ = tile_first.shape
+    me = lax.axis_index("lon")
+    half = 0.5 * WIND_COEF
     head = rim_lines(width)
-
-    def pack_rim(start):
+    masks = group_masks(8, part)
+
+    def pack(start):
         tiles = []
         for begin in (start, jnp.minimum(start + head, width - 8)):
             lines = pl.ds(pl.multiple_of(begin, 8), 8)
-            for row in (0, last):
-                tiles += [merid_row(wind_ref, tile_ref, row, lines), tile_ref[row, lines]]
-        put(packs, width + 8 + start, partner_order(transpose_groups(tiles, masks8, part, range(4, 8)), me))
-
-    each_chunk(head, 8, pack_rim)
+            tiles += [wind_first[0, lines] - half * tile_first[1, lines], tile_first[0, lines]]
+            tiles += [wind_last[1, lines] + half * tile_last[0, lines], tile_last[1, lines]]
+        put(packs, start, partner_order(transpose_groups(tiles, masks, part, range(4, 8)), me))
+
+    each_chunk(head, 8, pack)
 
 
 def rim_lines(width):
@@ -278,11 +283,11 @@
 
 
 def rim_kernel(part, skip, flag_ref, cut_ref, *refs):
-    blocks, north_ref, south_ref = natural(refs[:4]), refs[4], refs[5]
-    lines = blocks[0].shape[0] - skip
+    blocks, north_ref, south_ref = natural(refs[:4]), refs[-2], refs[-1]
+    lines = blocks[0].shape[0]
     first = lane_ids((lines, LANES)) // part % 4 < 2
     for half in range(2):
-        one, two = blocks[2 * half][skip:], blocks[2 * half + 1][skip:]
+        one, two = blocks[2 * half][...], blocks[2 * half + 1][...]
         where = slice(half * lines, half * lines + lines)
         south_ref[where] = jnp.where(first, one, turn_groups(two, 2, part))
         north_ref[where] = jnp.where(first, turn_groups(two, -2, part), one)
@@ -294,14 +299,14 @@
 
 def edge_spec_kernel(bounds, part, skip, flag_ref, cut_ref, mode_ref, south_ref, north_ref, _, *refs):
     blocks, forward, spec_ref = natural(refs[:4]), refs[4:10], refs[10]
-    lines = blocks[0].shape[0] - skip
+    lines = blocks[0].shape[0]
     width = skip - 8
     half = 0.5 * WIND_COEF
     item = lane_ids((lines, LANES)) // part % 4
     fields = []
     for quarter, block in enumerate(blocks):
         where = slice(quarter // 2 * lines, quarter // 2 * lines + lines)
-        own, south, north = block[skip:], south_ref[where], north_ref[where]
+        own, south, north = block[...], south_ref[where], north_ref[where]
         at = 0 if quarter % 2 else 2
         merid_s, press_s = turn_groups(south, 1 - at, part), turn_groups(south, -1 - at, part)
         merid_n, press_n = turn_groups(north, 1 + at, part), turn_groups(north, at - 1, part)
@@ -538,9 +543,12 @@
     return jax.ShapeDtypeStruct(shape, F32)
 
 
+def send(block, step):
+    return lax.ppermute(block, "lon", [(i, i ^ step) for i in range(4)])
+
+
 def exchange(blocks):
-    pairs = [[(i, i ^ step) for i in range(4)] for step in range(4)]
-    return [blocks[0]] + [lax.ppermute(blocks[step], "lon", pairs[step]) for step in (2, 3, 1)]
+    return [blocks[0]] + [send(blocks[step], step) for step in (2, 3, 1)]
 
 
 def packed_body(state, filter_flag, cutoff):
@@ -560,50 +568,62 @@
     table_specs = [whole(t.shape) for t in forward] + [whole(t.shape) for t in inverse]
     block, spectrum, full = (width, LANES), (at, LANES), (rows, width, LANES)
     skip = width + 8
-    first = (skip + rim_lines(width), LANES)
     second = (fold_lines(width) + width, LANES)
     rims = (2 * rim_lines(width) + 8, LANES)
     low_tile, high_tile = tile_of(state.shape, 0), tile_of(state.shape, 1)
 
-    first_circle = exchange(
-        call(
-            functools.partial(zonal_kernel, part),
-            [f32(*first)] * 4,
-            [low_tile, high_tile],
-            [whole(first)] * 4,
-            scratch_shapes=[pltpu.VMEM(full, F32)],
-        )(state, state)
-    )
+    edges = (rim_lines(width), LANES)
+    sided = (skip, LANES)
+
+    def two_rows(row, index):
+        return pl.BlockSpec((2, width, LANES), lambda step: (row, 0, index))
+
+    edge_packs = call(
+        functools.partial(edge_kernel, part),
+        [f32(*edges)] * 4,
+        [two_rows(0, 0), two_rows(rows // 2 - 1, 0), two_rows(0, 1), two_rows(rows // 2 - 1, 1)],
+        [whole(edges)] * 4,
+    )(state, state, state, state)
+    zonal_packs = call(
+        functools.partial(zonal_kernel, part),
+        [f32(*sided)] * 4,
+        [low_tile, high_tile],
+        [whole(sided)] * 4,
+        scratch_shapes=[pltpu.VMEM(full, F32)],
+    )(state, state)
+    edge_circle = exchange(edge_packs)
+    first_circle = exchange(zonal_packs)
     *packs, vert = call(
         functools.partial(press_kernel, part),
         [f32(*second)] * 4 + [f32(*full)],
         [low_tile, high_tile, ANY],
         [whole(second)] * 4 + [whole(full)],
-    )(state, state, first_circle[1])
+    )(state, state, edge_circle[1])
     second_circle = exchange(packs)
 
+    edge_specs = [whole(edges)] * 4
     to_north, to_south = call(
         functools.partial(rim_kernel, part, skip),
         [f32(*rims)] * 2,
-        [SMEM] * 2 + [whole(first)] * 4,
+        [SMEM] * 2 + edge_specs + [ANY],
         [whole(rims)] * 2,
-    )(filter_flag, cutoff, *first_circle)
+    )(filter_flag, cutoff, *edge_circle, vert)
     from_south = lax.ppermute(to_north, "lat", [(i, i + 1) for i in range(bands - 1)])
     from_north = lax.ppermute(to_south, "lat", [(i + 1, i) for i in range(bands - 1)])
 
     *zonal_parts, zonal_spec = call(
         functools.partial(zonal_spec_kernel, bounds, part),
         [f32(*block)] * 4 + [f32(*spectrum)],
-        [SMEM] * 2 + [whole(mode.shape), ANY] + [whole(first)] * 4 + table_specs,
+        [SMEM] * 2 + [whole(mode.shape), ANY] + [whole(sided)] * 4 + table_specs,
         [whole(block)] * 4 + [whole(spectrum)],
     )(filter_flag, cutoff, mode, second_circle[3], *first_circle, *forward, *inverse)
     zonal_back = exchange(zonal_parts)
     edge_spec = call(
         functools.partial(edge_spec_kernel, bounds, part, skip),
         f32(*spectrum),
-        [SMEM] * 2 + [whole(mode.shape)] + [whole(rims)] * 2 + [ANY] + [whole(first)] * 4 + table_specs[:6],
+        [SMEM] * 2 + [whole(mode.shape)] + [whole(rims)] * 2 + [ANY] + edge_specs + table_specs[:6],
         whole(spectrum),
-    )(filter_flag, cutoff, mode, from_south, from_north, zonal_spec, *first_circle, *forward)
+    )(filter_flag, cutoff, mode, from_south, from_north, zonal_spec, *edge_circle, *forward)
 
     *merid_parts, merid_spec = call(
         functools.partial(merid_spec_kernel, bounds, part),

time: 58 us -> 57.5 us (level)
  waiting for transfers between devices: 17.4 us -> 13.9 us
  starting transfers between devices: 20.4 us -> 23.2 us
    ppermute x15 -> x18, waiting for transfers between devices: 15 us -> 11.7 us  [send(): return lax.ppermute(block, 'lon', [(i, i ^ step) for i in range(4)])]
    ppermute x15 -> x18, starting transfers between devices: 14.1 us -> 16.8 us  [send(): return lax.ppermute(block, 'lon', [(i, i ^ step) for i in range(4)])]
    pallas_call x1 -> x2, Pallas kernels: 1.23 us -> 1.25 us  [the longest x1 1 us: packed_body(): call(functools.partial(zonal_kernel, part), [f32(*sided)] * 4, [low_tile,...]
  transfers between devices with their start and end apart: 17 -> 20, of which waited for: 6 -> 6; matrix products, arithmetic and copies ran while one was open for 0% -> 0% of each run, Pallas kernels for 26% -> 26%
where the time goes in v5:
time: 57.5 us; the launch traced here: 56.8 us
  starting transfers between devices  23.2 us (40%)
  Pallas kernels  17.3 us (30%)
  waiting for transfers between devices  13.9 us (24%)
  local copies, waits for them, and re-layouts  1.92 us (3%)
    ppermute x18, starting transfers between devices, send(): return lax.ppermute(block, 'lon', [(i, i ^ step) for i in range(4)])  16.8 us
    ppermute x18, waiting for transfers between devices, send(): return lax.ppermute(block, 'lon', [(i, i ^ step) for i in range(4)])  11.7 us
    ppermute x1, starting transfers between devices, packed_body(): lax.ppermute(to_south, 'lat', [(i + 1, i) for i in range(bands - 1)])  3.25 us
    ppermute x1, starting transfers between devices, packed_body(): lax.ppermute(to_north, 'lat', [(i, i + 1) for i in range(bands - 1)])  3.11 us
    pallas_call x1, Pallas kernels, packed_body(): call(functools.partial(merid_spec_kernel, bounds, part), [f32(*block)] *...  3.01 us
    pallas_call x1, Pallas kernels, packed_body(): call(functools.partial(press_back_kernel, bounds, part), [f32(*block)] *...  2.82 us
    pallas_call x1, Pallas kernels, packed_body(): call(functools.partial(zonal_spec_kernel, bounds, part), [f32(*block)] *...  2.76 us
    ppermute x1, waiting for transfers between devices, packed_body(): lax.ppermute(to_south, 'lat', [(i + 1, i) for i in range(bands - 1)])  2.18 us
  transfers between devices with their start and end apart: 20, of which 6 were waited for; matrix products, arithmetic and copies ran while one was open for 0% of the time, Pallas kernels for 26%

profile of v5, /device:TPU:17, one launch (start us, length us, event | category | flops | bytes accessed | tf_op | source)
XLA Modules:
  0.0 56.8 jit_solution(10576978497125033627)
XLA Ops:
  0.0 1.8 %copy-done = f32[8,360,256]{2,1,0:T(8,128)S(1)} copy-done((f32[8,360,256]{2,1,0:T(8,128)S(1)}, f32[8,360,256]{2,1,0:T(8,128)}, u32[]{:S(2)}) %copy-start) | copy-done | bytes 2949144
  1.8 1.0 %shard_map.156 = (f32[368,128]{1,0:T(8,128)S(1)}, f32[368,128]{1,0:T(8,128)S(1)}, f32[368,128]{1,0:T(8,128)S(1)}, f32[368,128]{1,0:T(8,128)S(1)}) custom-call(f32[8,360,256]{2,1,0:T(8,128)S(1)} %copy-done, f32[8,360,256]{2,1,0:T(8,128)S(1)} %copy-done), custom_call_target="tpu_custom_call" | custom-call | bytes 7380000 | tf_op jit(solution)/shard_map/pallas_call | solution.py:587
  2.8 1.3 %collective-permute-start.2 = (f32[368,128]{1,0:T(8,128)S(1)}, f32[368,128]{1,0:T(8,128)S(1)}, u32[]{:S(2)}, u32[]{:S(2)}) collective-permute-start(f32[368,128]{1,0:T(8,128)S(1)} %get-tuple-element.37), channel_id=1, source_target_pairs={{0,2},{1,3},{2,0},{3,1},{4,6},{5,7},{6,4},{7,5},{8,10},{9,11},{10,... | collective-permute-start | bytes 565256 | tf_op jit(solution)/shard_map/ppermute | solution.py:547
  4.7 2.4 %collective-permute-start.8 = (f32[184,128]{1,0:T(8,128)S(1)}, f32[184,128]{1,0:T(8,128)S(1)}, u32[]{:S(2)}, u32[]{:S(2)}) collective-permute-start(f32[184,128]{1,0:T(8,128)S(1)} %get-tuple-element.45), channel_id=1, source_target_pairs={{0,3},{1,2},{2,1},{3,0},{4,7},{5,6},{6,5},{7,4},{8,11},{9,10},{10,... | collective-permute-start | bytes 282632 | tf_op jit(solution)/shard_map/ppermute | solution.py:547
  7.7 2.8 %collective-permute-done._.refs_1_ = f32[184,128]{1,0:T(8,128)S(1)} collective-permute-done((f32[184,128]{1,0:T(8,128)S(1)}, f32[184,128]{1,0:T(8,128)S(1)}, u32[]{:S(2)}, u32[]{:S(2)}) %collective-permute-start) | collective-permute-done | bytes 94240 | tf_op jit(solution)/shard_map/ppermute | solution.py:547
  10.5 2.7 %collective-permute-start.4 = (f32[368,128]{1,0:T(8,128)S(1)}, f32[368,128]{1,0:T(8,128)S(1)}, u32[]{:S(2)}, u32[]{:S(2)}) collective-permute-start(f32[368,128]{1,0:T(8,128)S(1)} %get-tuple-element.39), channel_id=1, source_target_pairs={{0,1},{1,0},{2,3},{3,2},{4,5},{5,4},{6,7},{7,6},{8,9},{9,8},{10,11... | collective-permute-start | bytes 565256 | tf_op jit(solution)/shard_map/ppermute | solution.py:547
  13.3 1.4 %shard_map.155 = (f32[632,128]{1,0:T(8,128)S(1)}, f32[632,128]{1,0:T(8,128)S(1)}, f32[632,128]{1,0:T(8,128)S(1)}, f32[632,128]{1,0:T(8,128)S(1)}, f32[8,360,128]{2,1,0:T(8,128)S(1)}) custom-call(f32[8,360,256]{2,1,0:T(8,128)S(1)} %copy-done, f32[8,360,256]{2,1,0:T(8,128)S(1)} %copy-done, f32[184,128]{1,0:T(8,128)S(1)} %collective-permute-done._.refs_1_), custom_call_target="tpu_custom_call" | custom-call | bytes 7380000 | tf_op jit(solution)/shard_map/pallas_call | solution.py:596
  14.9 1.3 %collective-permute-start.12 = (f32[632,128]{1,0:T(8,128)S(1)}, f32[632,128]{1,0:T(8,128)S(1)}, u32[]{:S(2)}, u32[]{:S(2)}) collective-permute-start(f32[632,128]{1,0:T(8,128)S(1)} %get-tuple-element.52), channel_id=1, source_target_pairs={{0,2},{1,3},{2,0},{3,1},{4,6},{5,7},{6,4},{7,5},{8,10},{9,11},{10,... | collective-permute-start | bytes 970760 | tf_op jit(solution)/shard_map/ppermute | solution.py:547
  17.7 3.1 %collective-permute-start.10 = (f32[376,128]{1,0:T(8,128)S(1)}, f32[376,128]{1,0:T(8,128)S(1)}, u32[]{:S(2)}, u32[]{:S(2)}) collective-permute-start(f32[376,128]{1,0:T(8,128)S(1)} %get-tuple-element.48), channel_id=1, source_target_pairs={{0,4},{4,8},{8,12},{12,16},{16,20},{20,24},{24,28},{1,5},{5,9},{9,... | collective-permute-start | bytes 577544 | tf_op jit(solution)/shard_map/ppermute | solution.py:611
  20.9 3.2 %collective-permute-start.11 = (f32[376,128]{1,0:T(8,128)S(1)}, f32[376,128]{1,0:T(8,128)S(1)}, u32[]{:S(2)}, u32[]{:S(2)}) collective-permute-start(f32[376,128]{1,0:T(8,128)S(1)} %get-tuple-element.49), channel_id=1, source_target_pairs={{4,0},{8,4},{12,8},{16,12},{20,16},{24,20},{28,24},{5,1},{9,5},{13... | collective-permute-start | bytes 577544 | tf_op jit(solution)/shard_map/ppermute | solution.py:612
  24.3 2.8 %shard_map.157 = (f32[360,128]{1,0:T(8,128)S(1)}, f32[360,128]{1,0:T(8,128)S(1)}, f32[360,128]{1,0:T(8,128)S(1)}, f32[360,128]{1,0:T(8,128)S(1)}, f32[1488,128]{1,0:T(8,128)S(1)}) custom-call(s32[8]{0:T(128)S(1)} %copy-done.14, s32[8]{0:T(128)S(1)} %copy-done.15, f32[1488,128]{1,0:T(8,128)S(1)} %copy-done.3, ...), custom_call_target="tpu_custom_call" | custom-call | bytes 7380000 | tf_op jit(solution)/shard_map/pallas_call | solution.py:614
  27.0 1.4 %collective-permute-start.5 = (f32[360,128]{1,0:T(8,128)S(1)}, f32[360,128]{1,0:T(8,128)S(1)}, u32[]{:S(2)}, u32[]{:S(2)}) collective-permute-start(f32[360,128]{1,0:T(8,128)S(1)} %get-tuple-element.41), channel_id=1, source_target_pairs={{0,2},{1,3},{2,0},{3,1},{4,6},{5,7},{6,4},{7,5},{8,10},{9,11},{10,... | collective-permute-start | bytes 552968 | tf_op jit(solution)/shard_map/ppermute | solution.py:547
  28.4 0.8 %collective-permute-start.6 = (f32[360,128]{1,0:T(8,128)S(1)}, f32[360,128]{1,0:T(8,128)S(1)}, u32[]{:S(2)}, u32[]{:S(2)}) collective-permute-start(f32[360,128]{1,0:T(8,128)S(1)} %get-tuple-element.42), channel_id=1, source_target_pairs={{0,3},{1,2},{2,1},{3,0},{4,7},{5,6},{6,5},{7,4},{8,11},{9,10},{10,... | collective-permute-start | bytes 552968 | tf_op jit(solution)/shard_map/ppermute | solution.py:547
  29.2 2.2 %collective-permute-done.11.north_ref = f32[376,128]{1,0:T(8,128)S(1)} collective-permute-done((f32[376,128]{1,0:T(8,128)S(1)}, f32[376,128]{1,0:T(8,128)S(1)}, u32[]{:S(2)}, u32[]{:S(2)}) %collective-permute-start.11) | collective-permute-done | bytes 192544 | tf_op jit(solution)/shard_map/ppermute | solution.py:612
  31.9 2.1 %shard_map.159.edge_ref = f32[1488,128]{1,0:T(8,128)S(1)} custom-call(s32[8]{0:T(128)S(1)} %copy-done.14, s32[8]{0:T(128)S(1)} %copy-done.15, f32[1488,128]{1,0:T(8,128)S(1)} %copy-done.3, f32[376,128]{1,0:T(8,128)S(1)} %collective-permute-done.10.south_ref, f32[376,128]{1,0:T(8,128)S(1)} %collective-permute-done.11.north_ref, ...), custom_call_target="tpu_custom_call" | custom-call | bytes 7380000 | tf_op jit(solution)/shard_map/pallas_call | solution.py:621
  34.0 3.0 %shard_map.160 = (f32[360,128]{1,0:T(8,128)S(1)}, f32[360,128]{1,0:T(8,128)S(1)}, f32[360,128]{1,0:T(8,128)S(1)}, f32[360,128]{1,0:T(8,128)S(1)}, f32[1488,128]{1,0:T(8,128)S(1)}) custom-call(s32[8]{0:T(128)S(1)} %copy-done.14, s32[8]{0:T(128)S(1)} %copy-done.15, f32[1488,128]{1,0:T(8,128)S(1)} %copy-done.3, f32[1488,128]{1,0:T(8,128)S(1)} %shard_map.159.edge_ref, ...), custom_call_target="tpu_custom_call" | custom-call | bytes 7380000 | tf_op jit(solution)/shard_map/pallas_call | solution.py:628
  37.0 1.4 %collective-permute-start.14 = (f32[360,128]{1,0:T(8,128)S(1)}, f32[360,128]{1,0:T(8,128)S(1)}, u32[]{:S(2)}, u32[]{:S(2)}) collective-permute-start(f32[360,128]{1,0:T(8,128)S(1)} %get-tuple-element.55), channel_id=1, source_target_pairs={{0,2},{1,3},{2,0},{3,1},{4,6},{5,7},{6,4},{7,5},{8,10},{9,11},{10,... | collective-permute-start | bytes 552968 | tf_op jit(solution)/shard_map/ppermute | solution.py:547
  38.7 2.8 %shard_map.162 = (f32[360,128]{1,0:T(8,128)S(1)}, f32[360,128]{1,0:T(8,128)S(1)}, f32[360,128]{1,0:T(8,128)S(1)}, f32[360,128]{1,0:T(8,128)S(1)}) custom-call(s32[8]{0:T(128)S(1)} %copy-done.14, s32[8]{0:T(128)S(1)} %copy-done.15, f32[1488,128]{1,0:T(8,128)S(1)} %copy-done.3, f32[1488,128]{1,0:T(8,128)S(1)} %get-tuple-element.50._.zonal_ref, ...), custom_call_target="tpu_custom_call" | custom-call | bytes 7380000 | tf_op jit(solution)/shard_map/pallas_call | solution.py:636
  41.8 1.3 %collective-permute-start.17 = (f32[360,128]{1,0:T(8,128)S(1)}, f32[360,128]{1,0:T(8,128)S(1)}, u32[]{:S(2)}, u32[]{:S(2)}) collective-permute-start(f32[360,128]{1,0:T(8,128)S(1)} %get-tuple-element.60), channel_id=1, source_target_pairs={{0,2},{1,3},{2,0},{3,1},{4,6},{5,7},{6,4},{7,5},{8,10},{9,11},{10,... | collective-permute-start | bytes 552968 | tf_op jit(solution)/shard_map/ppermute | solution.py:547
  44.5 3.3 %collective-permute-done.15.refs_6_ = f32[360,128]{1,0:T(8,128)S(1)} collective-permute-done((f32[360,128]{1,0:T(8,128)S(1)}, f32[360,128]{1,0:T(8,128)S(1)}, u32[]{:S(2)}, u32[]{:S(2)}) %collective-permute-start.15) | collective-permute-done | bytes 184352 | tf_op jit(solution)/shard_map/ppermute | solution.py:547
  47.8 1.9 %shard_map.161._ = f32[8,360,256]{2,1,0:T(8,128)} custom-call(f32[360,128]{1,0:T(8,128)S(1)} %get-tuple-element.40.refs_0_, f32[360,128]{1,0:T(8,128)S(1)} %collective-permute-done.5.refs_1_, f32[360,128]{1,0:T(8,128)S(1)} %collective-permute-done.6.refs_2_, f32[360,128]{1,0:T(8,128)S(1)} %collective-permute-done.7.refs_3_, ...), custom_call_target="tpu_custom_call" | custom-call | bytes 7380000 | tf_op jit(solution)/shard_map/pallas_call | solution.py:644
  49.7 1.4 %collective-permute-done.17.refs_1_ = f32[360,128]{1,0:T(8,128)S(1)} collective-permute-done((f32[360,128]{1,0:T(8,128)S(1)}, f32[360,128]{1,0:T(8,128)S(1)}, u32[]{:S(2)}, u32[]{:S(2)}) %collective-permute-start.17) | collective-permute-done | bytes 184352 | tf_op jit(solution)/shard_map/ppermute | solution.py:547
  51.1 4.1 %collective-permute-done.18.refs_2_ = f32[360,128]{1,0:T(8,128)S(1)} collective-permute-done((f32[360,128]{1,0:T(8,128)S(1)}, f32[360,128]{1,0:T(8,128)S(1)}, u32[]{:S(2)}, u32[]{:S(2)}) %collective-permute-start.18) | collective-permute-done | bytes 184352 | tf_op jit(solution)/shard_map/ppermute | solution.py:547
  55.3 1.4 %shard_map.163 = f32[8,360,256]{2,1,0:T(8,128)} custom-call(f32[8,360,256]{2,1,0:T(8,128)} %shard_map.161._, f32[8,360,128]{2,1,0:T(8,128)S(1)} %get-tuple-element.47.refs_4_.tile_ref, f32[360,128]{1,0:T(8,128)S(1)} %get-tuple-element.59.refs_0_, f32[360,128]{1,0:T(8,128)S(1)} %collective-permute-done.17.refs_1_, ...), custom_call_target="tpu_custom_call", output_to_operand_aliasing={{}: (0, {})} | custom-call | bytes 7380000 | tf_op jit(solution)/shard_map/pallas_call | solution.py:651
  (58 shorter events, 5.4 us)
Async XLA Ops:
  2.8 13.4 %collective-permute-start.2 = (f32[368,128]{1,0:T(8,128)S(1)}, f32[368,128]{1,0:T(8,128)S(1)}, u32[]{:S(2)}, u32[]{:S(2)}) collective-permute-start(f32[368,128]{1,0:T(8,128)S(1)} %get-tuple-element.37), channel_id=1, source_target_pairs={{0,2},{1,3},{2,0},{3,1},{4,6},{5,7},{6,4},{7,5},{8,10},{9,11},{10,... | collective-permute-start | bytes 565256 | tf_op jit(solution)/shard_map/ppermute | solution.py:547
  4.4 6.1 %collective-permute-start = (f32[184,128]{1,0:T(8,128)S(1)}, f32[184,128]{1,0:T(8,128)S(1)}, u32[]{:S(2)}, u32[]{:S(2)}) collective-permute-start(f32[184,128]{1,0:T(8,128)S(1)} %get-tuple-element.34), channel_id=1, source_target_pairs={{0,2},{1,3},{2,0},{3,1},{4,6},{5,7},{6,4},{7,5},{8,10},{9,11},{10,... | collective-permute-start | bytes 282632 | tf_op jit(solution)/shard_map/ppermute | solution.py:547
  4.7 10.1 %collective-permute-start.8 = (f32[184,128]{1,0:T(8,128)S(1)}, f32[184,128]{1,0:T(8,128)S(1)}, u32[]{:S(2)}, u32[]{:S(2)}) collective-permute-start(f32[184,128]{1,0:T(8,128)S(1)} %get-tuple-element.45), channel_id=1, source_target_pairs={{0,3},{1,2},{2,1},{3,0},{4,7},{5,6},{6,5},{7,4},{8,11},{9,10},{10,... | collective-permute-start | bytes 282632 | tf_op jit(solution)/shard_map/ppermute | solution.py:547
  7.1 7.8 %collective-permute-start.9 = (f32[184,128]{1,0:T(8,128)S(1)}, f32[184,128]{1,0:T(8,128)S(1)}, u32[]{:S(2)}, u32[]{:S(2)}) collective-permute-start(f32[184,128]{1,0:T(8,128)S(1)} %get-tuple-element.46), channel_id=1, source_target_pairs={{0,1},{1,0},{2,3},{3,2},{4,5},{5,4},{6,7},{7,6},{8,9},{9,8},{10,11... | collective-permute-start | bytes 282632 | tf_op jit(solution)/shard_map/ppermute | solution.py:547
  7.1 10.6 %collective-permute-start.3 = (f32[368,128]{1,0:T(8,128)S(1)}, f32[368,128]{1,0:T(8,128)S(1)}, u32[]{:S(2)}, u32[]{:S(2)}) collective-permute-start(f32[368,128]{1,0:T(8,128)S(1)} %get-tuple-element.38), channel_id=1, source_target_pairs={{0,3},{1,2},{2,1},{3,0},{4,7},{5,6},{6,5},{7,4},{8,11},{9,10},{10,... | collective-permute-start | bytes 565256 | tf_op jit(solution)/shard_map/ppermute | solution.py:547
  10.5 10.3 %collective-permute-start.4 = (f32[368,128]{1,0:T(8,128)S(1)}, f32[368,128]{1,0:T(8,128)S(1)}, u32[]{:S(2)}, u32[]{:S(2)}) collective-permute-start(f32[368,128]{1,0:T(8,128)S(1)} %get-tuple-element.39), channel_id=1, source_target_pairs={{0,1},{1,0},{2,3},{3,2},{4,5},{5,4},{6,7},{7,6},{8,9},{9,8},{10,11... | collective-permute-start | bytes 565256 | tf_op jit(solution)/shard_map/ppermute | solution.py:547
  13.2 10.9 %copy-start.6 = (bf16[384,360]{1,0:T(8,128)(2,1)S(1)}, bf16[384,360]{1,0:T(8,128)(2,1)}, u32[]{:S(2)}) copy-start(bf16[384,360]{1,0:T(8,128)(2,1)} %constant.29.clone.refs_3_.refs_7_) | copy-start | bytes 829444
  13.2 10.9 %copy-start.7 = (bf16[384,360]{1,0:T(8,128)(2,1)S(1)}, bf16[384,360]{1,0:T(8,128)(2,1)}, u32[]{:S(2)}) copy-start(bf16[384,360]{1,0:T(8,128)(2,1)} %constant.28.clone.refs_2_.refs_6_) | copy-start | bytes 829444
  13.2 10.9 %copy-start.8 = (bf16[384,360]{1,0:T(8,128)(2,1)S(1)}, bf16[384,360]{1,0:T(8,128)(2,1)}, u32[]{:S(2)}) copy-start(bf16[384,360]{1,0:T(8,128)(2,1)} %constant.27.clone.refs_1_.refs_5_) | copy-start | bytes 829444
  13.2 10.9 %copy-start.9 = (bf16[384,360]{1,0:T(8,128)(2,1)S(1)}, bf16[384,360]{1,0:T(8,128)(2,1)}, u32[]{:S(2)}) copy-start(bf16[384,360]{1,0:T(8,128)(2,1)} %constant.26.clone.refs_0_.refs_4_) | copy-start | bytes 829444
  14.8 9.3 %collective-permute-start.1 = (f32[632,128]{1,0:T(8,128)S(1)}, f32[632,128]{1,0:T(8,128)S(1)}, u32[]{:S(2)}, u32[]{:S(2)}) collective-permute-start(f32[632,128]{1,0:T(8,128)S(1)} %get-tuple-element.35), channel_id=1, source_target_pairs={{0,1},{1,0},{2,3},{3,2},{4,5},{5,4},{6,7},{7,6},{8,9},{9,8},{10,11... | collective-permute-start | bytes 970760 | tf_op jit(solution)/shard_map/ppermute | solution.py:547
  14.9 19.0 %collective-permute-start.12 = (f32[632,128]{1,0:T(8,128)S(1)}, f32[632,128]{1,0:T(8,128)S(1)}, u32[]{:S(2)}, u32[]{:S(2)}) collective-permute-start(f32[632,128]{1,0:T(8,128)S(1)} %get-tuple-element.52), channel_id=1, source_target_pairs={{0,2},{1,3},{2,0},{3,1},{4,6},{5,7},{6,4},{7,5},{8,10},{9,11},{10,... | collective-permute-start | bytes 970760 | tf_op jit(solution)/shard_map/ppermute | solution.py:547
  16.2 17.7 %collective-permute-start.13 = (f32[632,128]{1,0:T(8,128)S(1)}, f32[632,128]{1,0:T(8,128)S(1)}, u32[]{:S(2)}, u32[]{:S(2)}) collective-permute-start(f32[632,128]{1,0:T(8,128)S(1)} %get-tuple-element.53), channel_id=1, source_target_pairs={{0,3},{1,2},{2,1},{3,0},{4,7},{5,6},{6,5},{7,4},{8,11},{9,10},{10,... | collective-permute-start | bytes 970760 | tf_op jit(solution)/shard_map/ppermute | solution.py:547
  17.7 10.7 %collective-permute-start.10 = (f32[376,128]{1,0:T(8,128)S(1)}, f32[376,128]{1,0:T(8,128)S(1)}, u32[]{:S(2)}, u32[]{:S(2)}) collective-permute-start(f32[376,128]{1,0:T(8,128)S(1)} %get-tuple-element.48), channel_id=1, source_target_pairs={{0,4},{4,8},{8,12},{12,16},{16,20},{20,24},{24,28},{1,5},{5,9},{9,... | collective-permute-start | bytes 577544 | tf_op jit(solution)/shard_map/ppermute | solution.py:611
  20.9 10.6 %collective-permute-start.11 = (f32[376,128]{1,0:T(8,128)S(1)}, f32[376,128]{1,0:T(8,128)S(1)}, u32[]{:S(2)}, u32[]{:S(2)}) collective-permute-start(f32[376,128]{1,0:T(8,128)S(1)} %get-tuple-element.49), channel_id=1, source_target_pairs={{4,0},{8,4},{12,8},{16,12},{20,16},{24,20},{28,24},{5,1},{9,5},{13... | collective-permute-start | bytes 577544 | tf_op jit(solution)/shard_map/ppermute | solution.py:612
  27.0 14.5 %collective-permute-start.5 = (f32[360,128]{1,0:T(8,128)S(1)}, f32[360,128]{1,0:T(8,128)S(1)}, u32[]{:S(2)}, u32[]{:S(2)}) collective-permute-start(f32[360,128]{1,0:T(8,128)S(1)} %get-tuple-element.41), channel_id=1, source_target_pairs={{0,2},{1,3},{2,0},{3,1},{4,6},{5,7},{6,4},{7,5},{8,10},{9,11},{10,... | collective-permute-start | bytes 552968 | tf_op jit(solution)/shard_map/ppermute | solution.py:547
  28.4 13.4 %collective-permute-start.6 = (f32[360,128]{1,0:T(8,128)S(1)}, f32[360,128]{1,0:T(8,128)S(1)}, u32[]{:S(2)}, u32[]{:S(2)}) collective-permute-start(f32[360,128]{1,0:T(8,128)S(1)} %get-tuple-element.42), channel_id=1, source_target_pairs={{0,3},{1,2},{2,1},{3,0},{4,7},{5,6},{6,5},{7,4},{8,11},{9,10},{10,... | collective-permute-start | bytes 552968 | tf_op jit(solution)/shard_map/ppermute | solution.py:547
  31.4 11.7 %collective-permute-start.7 = (f32[360,128]{1,0:T(8,128)S(1)}, f32[360,128]{1,0:T(8,128)S(1)}, u32[]{:S(2)}, u32[]{:S(2)}) collective-permute-start(f32[360,128]{1,0:T(8,128)S(1)} %get-tuple-element.43), channel_id=1, source_target_pairs={{0,1},{1,0},{2,3},{3,2},{4,5},{5,4},{6,7},{7,6},{8,9},{9,8},{10,11... | collective-permute-start | bytes 552968 | tf_op jit(solution)/shard_map/ppermute | solution.py:547
  37.0 6.8 %collective-permute-start.14 = (f32[360,128]{1,0:T(8,128)S(1)}, f32[360,128]{1,0:T(8,128)S(1)}, u32[]{:S(2)}, u32[]{:S(2)}) collective-permute-start(f32[360,128]{1,0:T(8,128)S(1)} %get-tuple-element.55), channel_id=1, source_target_pairs={{0,2},{1,3},{2,0},{3,1},{4,6},{5,7},{6,4},{7,5},{8,10},{9,11},{10,... | collective-permute-start | bytes 552968 | tf_op jit(solution)/shard_map/ppermute | solution.py:547
  38.3 9.5 %collective-permute-start.15 = (f32[360,128]{1,0:T(8,128)S(1)}, f32[360,128]{1,0:T(8,128)S(1)}, u32[]{:S(2)}, u32[]{:S(2)}) collective-permute-start(f32[360,128]{1,0:T(8,128)S(1)} %get-tuple-element.56), channel_id=1, source_target_pairs={{0,3},{1,2},{2,1},{3,0},{4,7},{5,6},{6,5},{7,4},{8,11},{9,10},{10,... | collective-permute-start | bytes 552968 | tf_op jit(solution)/shard_map/ppermute | solution.py:547
  41.6 6.2 %collective-permute-start.16 = (f32[360,128]{1,0:T(8,128)S(1)}, f32[360,128]{1,0:T(8,128)S(1)}, u32[]{:S(2)}, u32[]{:S(2)}) collective-permute-start(f32[360,128]{1,0:T(8,128)S(1)} %get-tuple-element.57), channel_id=1, source_target_pairs={{0,1},{1,0},{2,3},{3,2},{4,5},{5,4},{6,7},{7,6},{8,9},{9,8},{10,11... | collective-permute-start | bytes 552968 | tf_op jit(solution)/shard_map/ppermute | solution.py:547
  41.8 9.3 %collective-permute-start.17 = (f32[360,128]{1,0:T(8,128)S(1)}, f32[360,128]{1,0:T(8,128)S(1)}, u32[]{:S(2)}, u32[]{:S(2)}) collective-permute-start(f32[360,128]{1,0:T(8,128)S(1)} %get-tuple-element.60), channel_id=1, source_target_pairs={{0,2},{1,3},{2,0},{3,1},{4,6},{5,7},{6,4},{7,5},{8,10},{9,11},{10,... | collective-permute-start | bytes 552968 | tf_op jit(solution)/shard_map/ppermute | solution.py:547
  43.1 12.2 %collective-permute-start.18 = (f32[360,128]{1,0:T(8,128)S(1)}, f32[360,128]{1,0:T(8,128)S(1)}, u32[]{:S(2)}, u32[]{:S(2)}) collective-permute-start(f32[360,128]{1,0:T(8,128)S(1)} %get-tuple-element.61), channel_id=1, source_target_pairs={{0,3},{1,2},{2,1},{3,0},{4,7},{5,6},{6,5},{7,4},{8,11},{9,10},{10,... | collective-permute-start | bytes 552968 | tf_op jit(solution)/shard_map/ppermute | solution.py:547
  43.8 11.5 %collective-permute-start.19 = (f32[360,128]{1,0:T(8,128)S(1)}, f32[360,128]{1,0:T(8,128)S(1)}, u32[]{:S(2)}, u32[]{:S(2)}) collective-permute-start(f32[360,128]{1,0:T(8,128)S(1)} %get-tuple-element.62), channel_id=1, source_target_pairs={{0,1},{1,0},{2,3},{3,2},{4,5},{5,4},{6,7},{7,6},{8,9},{9,8},{10,11... | collective-permute-start | bytes 552968 | tf_op jit(solution)/shard_map/ppermute | solution.py:547
  (12 other events, 110.3 us)

commit v6 on v5

--- a/solution.py
+++ b/solution.py
@@ -534,7 +534,7 @@
         in_specs=in_specs,
         out_specs=out_specs,
         compiler_params=pltpu.CompilerParams(vmem_limit_bytes=VMEM_BYTES),
-        cost_estimate=pl.CostEstimate(flops=0, bytes_accessed=int(cost * 3.69e6), transcendentals=0),
+        cost_estimate=pl.CostEstimate(flops=int(cost * 1.15e9), bytes_accessed=int(cost * 3.69e6), transcendentals=0),
         **more,
     )
 
@@ -607,6 +607,7 @@
         [f32(*rims)] * 2,
         [SMEM] * 2 + edge_specs + [ANY],
         [whole(rims)] * 2,
+        cost=8,
     )(filter_flag, cutoff, *edge_circle, vert)
     from_south = lax.ppermute(to_north, "lat", [(i, i + 1) for i in range(bands - 1)])
     from_north = lax.ppermute(to_south, "lat", [(i + 1, i) for i in range(bands - 1)])

time: 57.5 us -> 57.1 us (level)
  transfers between devices with their start and end apart: 20 -> 20, of which waited for: 6 -> 6; matrix products, arithmetic and copies ran while one was open for 0% -> 0% of each run, Pallas kernels for 26% -> 28%
where the time goes in v6:
time: 57.1 us; the launch traced here: 56.1 us
  starting transfers between devices  22.9 us (40%)
  Pallas kernels  17.4 us (30%)
  waiting for transfers between devices  13.4 us (23%)
  local copies, waits for them, and re-layouts  1.92 us (3%)
    ppermute x18, starting transfers between devices, send(): return lax.ppermute(block, 'lon', [(i, i ^ step) for i in range(4)])  16.6 us
    ppermute x18, waiting for transfers between devices, send(): return lax.ppermute(block, 'lon', [(i, i ^ step) for i in range(4)])  11.4 us
    ppermute x1, starting transfers between devices, packed_body(): lax.ppermute(to_south, 'lat', [(i + 1, i) for i in range(bands - 1)])  3.24 us
    ppermute x1, starting transfers between devices, packed_body(): lax.ppermute(to_north, 'lat', [(i, i + 1) for i in range(bands - 1)])  3.11 us
    pallas_call x1, Pallas kernels, packed_body(): call(functools.partial(merid_spec_kernel, bounds, part), [f32(*block)] *...  3.01 us
    pallas_call x1, Pallas kernels, packed_body(): call(functools.partial(press_back_kernel, bounds, part), [f32(*block)] *...  2.84 us
    pallas_call x1, Pallas kernels, packed_body(): call(functools.partial(zonal_spec_kernel, bounds, part), [f32(*block)] *...  2.77 us
    pallas_call x1, Pallas kernels, packed_body(): call(functools.partial(edge_spec_kernel, bounds, part, skip), f32(*spectr...  2.05 us
  transfers between devices with their start and end apart: 20, of which 6 were waited for; matrix products, arithmetic and copies ran while one was open for 0% of the time, Pallas kernels for 28%

profile of v6, /device:TPU:17, one launch (start us, length us, event | category | flops | bytes accessed | tf_op | source)
XLA Modules:
  0.0 56.1 jit_solution(17916746635500594094)
XLA Ops:
  0.0 1.8 %copy-done = f32[8,360,256]{2,1,0:T(8,128)S(1)} copy-done((f32[8,360,256]{2,1,0:T(8,128)S(1)}, f32[8,360,256]{2,1,0:T(8,128)}, u32[]{:S(2)}) %copy-start) | copy-done | bytes 2949144
  2.1 1.3 %collective-permute-start = (f32[184,128]{1,0:T(8,128)S(1)}, f32[184,128]{1,0:T(8,128)S(1)}, u32[]{:S(2)}, u32[]{:S(2)}) collective-permute-start(f32[184,128]{1,0:T(8,128)S(1)} %get-tuple-element.34), channel_id=1, source_target_pairs={{0,2},{1,3},{2,0},{3,1},{4,6},{5,7},{6,4},{7,5},{8,10},{9,11},{10,... | collective-permute-start | bytes 282632 | tf_op jit(solution)/shard_map/ppermute | solution.py:547
  3.4 1.1 %collective-permute-start.8 = (f32[184,128]{1,0:T(8,128)S(1)}, f32[184,128]{1,0:T(8,128)S(1)}, u32[]{:S(2)}, u32[]{:S(2)}) collective-permute-start(f32[184,128]{1,0:T(8,128)S(1)} %get-tuple-element.45), channel_id=1, source_target_pairs={{0,3},{1,2},{2,1},{3,0},{4,7},{5,6},{6,5},{7,4},{8,11},{9,10},{10,... | collective-permute-start | bytes 282632 | tf_op jit(solution)/shard_map/ppermute | solution.py:547
  4.5 1.0 %shard_map.156 = (f32[368,128]{1,0:T(8,128)S(1)}, f32[368,128]{1,0:T(8,128)S(1)}, f32[368,128]{1,0:T(8,128)S(1)}, f32[368,128]{1,0:T(8,128)S(1)}) custom-call(f32[8,360,256]{2,1,0:T(8,128)S(1)} %copy-done, f32[8,360,256]{2,1,0:T(8,128)S(1)} %copy-done), custom_call_target="tpu_custom_call" | custom-call | flops 2300000000 | bytes 7380000 | tf_op jit(solution)/shard_map/pallas_call | solution.py:587
  5.5 1.3 %collective-permute-start.2 = (f32[368,128]{1,0:T(8,128)S(1)}, f32[368,128]{1,0:T(8,128)S(1)}, u32[]{:S(2)}, u32[]{:S(2)}) collective-permute-start(f32[368,128]{1,0:T(8,128)S(1)} %get-tuple-element.37), channel_id=1, source_target_pairs={{0,2},{1,3},{2,0},{3,1},{4,6},{5,7},{6,4},{7,5},{8,10},{9,11},{10,... | collective-permute-start | bytes 565256 | tf_op jit(solution)/shard_map/ppermute | solution.py:547
  7.7 1.5 %shard_map.155 = (f32[632,128]{1,0:T(8,128)S(1)}, f32[632,128]{1,0:T(8,128)S(1)}, f32[632,128]{1,0:T(8,128)S(1)}, f32[632,128]{1,0:T(8,128)S(1)}, f32[8,360,128]{2,1,0:T(8,128)S(1)}) custom-call(f32[8,360,256]{2,1,0:T(8,128)S(1)} %copy-done, f32[8,360,256]{2,1,0:T(8,128)S(1)} %copy-done, f32[184,128]{1,0:T(8,128)S(1)} %collective-permute-done._.refs_1_), custom_call_target="tpu_custom_call" | custom-call | flops 2300000000 | bytes 7380000 | tf_op jit(solution)/shard_map/pallas_call | solution.py:596
  9.8 1.5 %collective-permute-start.12 = (f32[632,128]{1,0:T(8,128)S(1)}, f32[632,128]{1,0:T(8,128)S(1)}, u32[]{:S(2)}, u32[]{:S(2)}) collective-permute-start(f32[632,128]{1,0:T(8,128)S(1)} %get-tuple-element.52), channel_id=1, source_target_pairs={{0,2},{1,3},{2,0},{3,1},{4,6},{5,7},{6,4},{7,5},{8,10},{9,11},{10,... | collective-permute-start | bytes 970760 | tf_op jit(solution)/shard_map/ppermute | solution.py:547
  12.8 2.4 %collective-permute-start.13 = (f32[632,128]{1,0:T(8,128)S(1)}, f32[632,128]{1,0:T(8,128)S(1)}, u32[]{:S(2)}, u32[]{:S(2)}) collective-permute-start(f32[632,128]{1,0:T(8,128)S(1)} %get-tuple-element.53), channel_id=1, source_target_pairs={{0,3},{1,2},{2,1},{3,0},{4,7},{5,6},{6,5},{7,4},{8,11},{9,10},{10,... | collective-permute-start | bytes 970760 | tf_op jit(solution)/shard_map/ppermute | solution.py:547
  15.2 1.9 %collective-permute-done.3.q3 = f32[368,128]{1,0:T(8,128)S(1)} collective-permute-done((f32[368,128]{1,0:T(8,128)S(1)}, f32[368,128]{1,0:T(8,128)S(1)}, u32[]{:S(2)}, u32[]{:S(2)}) %collective-permute-start.3) | collective-permute-done | bytes 188448 | tf_op jit(solution)/shard_map/ppermute | solution.py:547
  17.1 3.1 %collective-permute-start.10 = (f32[376,128]{1,0:T(8,128)S(1)}, f32[376,128]{1,0:T(8,128)S(1)}, u32[]{:S(2)}, u32[]{:S(2)}) collective-permute-start(f32[376,128]{1,0:T(8,128)S(1)} %get-tuple-element.48), channel_id=1, source_target_pairs={{0,4},{4,8},{8,12},{12,16},{16,20},{20,24},{24,28},{1,5},{5,9},{9,... | collective-permute-start | bytes 577544 | tf_op jit(solution)/shard_map/ppermute | solution.py:612
  20.2 3.2 %collective-permute-start.11 = (f32[376,128]{1,0:T(8,128)S(1)}, f32[376,128]{1,0:T(8,128)S(1)}, u32[]{:S(2)}, u32[]{:S(2)}) collective-permute-start(f32[376,128]{1,0:T(8,128)S(1)} %get-tuple-element.49), channel_id=1, source_target_pairs={{4,0},{8,4},{12,8},{16,12},{20,16},{24,20},{28,24},{5,1},{9,5},{13... | collective-permute-start | bytes 577544 | tf_op jit(solution)/shard_map/ppermute | solution.py:613
  23.6 2.8 %shard_map.157 = (f32[360,128]{1,0:T(8,128)S(1)}, f32[360,128]{1,0:T(8,128)S(1)}, f32[360,128]{1,0:T(8,128)S(1)}, f32[360,128]{1,0:T(8,128)S(1)}, f32[1488,128]{1,0:T(8,128)S(1)}) custom-call(s32[8]{0:T(128)S(1)} %copy-done.14, s32[8]{0:T(128)S(1)} %copy-done.15, f32[1488,128]{1,0:T(8,128)S(1)} %copy-done.5, ...), custom_call_target="tpu_custom_call" | custom-call | flops 2300000000 | bytes 7380000 | tf_op jit(solution)/shard_map/pallas_call | solution.py:615
  26.4 1.6 %collective-permute-start.5 = (f32[360,128]{1,0:T(8,128)S(1)}, f32[360,128]{1,0:T(8,128)S(1)}, u32[]{:S(2)}, u32[]{:S(2)}) collective-permute-start(f32[360,128]{1,0:T(8,128)S(1)} %get-tuple-element.41), channel_id=1, source_target_pairs={{0,2},{1,3},{2,0},{3,1},{4,6},{5,7},{6,4},{7,5},{8,10},{9,11},{10,... | collective-permute-start | bytes 552968 | tf_op jit(solution)/shard_map/ppermute | solution.py:547
  28.8 1.9 %collective-permute-done.11.north_ref = f32[376,128]{1,0:T(8,128)S(1)} collective-permute-done((f32[376,128]{1,0:T(8,128)S(1)}, f32[376,128]{1,0:T(8,128)S(1)}, u32[]{:S(2)}, u32[]{:S(2)}) %collective-permute-start.11) | collective-permute-done | bytes 192544 | tf_op jit(solution)/shard_map/ppermute | solution.py:613
  31.2 2.1 %shard_map.159.edge_ref = f32[1488,128]{1,0:T(8,128)S(1)} custom-call(s32[8]{0:T(128)S(1)} %copy-done.14, s32[8]{0:T(128)S(1)} %copy-done.15, f32[1488,128]{1,0:T(8,128)S(1)} %copy-done.5, f32[376,128]{1,0:T(8,128)S(1)} %collective-permute-done.10.south_ref, f32[376,128]{1,0:T(8,128)S(1)} %collective-permute-done.11.north_ref, ...), custom_call_target="tpu_custom_call" | custom-call | flops 2300000000 | bytes 7380000 | tf_op jit(solution)/shard_map/pallas_call | solution.py:622
  33.3 3.0 %shard_map.160 = (f32[360,128]{1,0:T(8,128)S(1)}, f32[360,128]{1,0:T(8,128)S(1)}, f32[360,128]{1,0:T(8,128)S(1)}, f32[360,128]{1,0:T(8,128)S(1)}, f32[1488,128]{1,0:T(8,128)S(1)}) custom-call(s32[8]{0:T(128)S(1)} %copy-done.14, s32[8]{0:T(128)S(1)} %copy-done.15, f32[1488,128]{1,0:T(8,128)S(1)} %copy-done.5, f32[1488,128]{1,0:T(8,128)S(1)} %shard_map.159.edge_ref, ...), custom_call_target="tpu_custom_call" | custom-call | flops 2300000000 | bytes 7380000 | tf_op jit(solution)/shard_map/pallas_call | solution.py:629
  36.3 1.5 %collective-permute-start.14 = (f32[360,128]{1,0:T(8,128)S(1)}, f32[360,128]{1,0:T(8,128)S(1)}, u32[]{:S(2)}, u32[]{:S(2)}) collective-permute-start(f32[360,128]{1,0:T(8,128)S(1)} %get-tuple-element.55), channel_id=1, source_target_pairs={{0,2},{1,3},{2,0},{3,1},{4,6},{5,7},{6,4},{7,5},{8,10},{9,11},{10,... | collective-permute-start | bytes 552968 | tf_op jit(solution)/shard_map/ppermute | solution.py:547
  38.3 2.8 %shard_map.162 = (f32[360,128]{1,0:T(8,128)S(1)}, f32[360,128]{1,0:T(8,128)S(1)}, f32[360,128]{1,0:T(8,128)S(1)}, f32[360,128]{1,0:T(8,128)S(1)}) custom-call(s32[8]{0:T(128)S(1)} %copy-done.14, s32[8]{0:T(128)S(1)} %copy-done.15, f32[1488,128]{1,0:T(8,128)S(1)} %copy-done.5, f32[1488,128]{1,0:T(8,128)S(1)} %get-tuple-element.50._.zonal_ref, ...), custom_call_target="tpu_custom_call" | custom-call | flops 2300000000 | bytes 7380000 | tf_op jit(solution)/shard_map/pallas_call | solution.py:637
  41.1 1.5 %collective-permute-start.17 = (f32[360,128]{1,0:T(8,128)S(1)}, f32[360,128]{1,0:T(8,128)S(1)}, u32[]{:S(2)}, u32[]{:S(2)}) collective-permute-start(f32[360,128]{1,0:T(8,128)S(1)} %get-tuple-element.60), channel_id=1, source_target_pairs={{0,2},{1,3},{2,0},{3,1},{4,6},{5,7},{6,4},{7,5},{8,10},{9,11},{10,... | collective-permute-start | bytes 552968 | tf_op jit(solution)/shard_map/ppermute | solution.py:547
  43.8 3.3 %collective-permute-done.15.refs_6_ = f32[360,128]{1,0:T(8,128)S(1)} collective-permute-done((f32[360,128]{1,0:T(8,128)S(1)}, f32[360,128]{1,0:T(8,128)S(1)}, u32[]{:S(2)}, u32[]{:S(2)}) %collective-permute-start.15) | collective-permute-done | bytes 184352 | tf_op jit(solution)/shard_map/ppermute | solution.py:547
  47.1 1.9 %shard_map.161._ = f32[8,360,256]{2,1,0:T(8,128)} custom-call(f32[360,128]{1,0:T(8,128)S(1)} %get-tuple-element.40.refs_0_, f32[360,128]{1,0:T(8,128)S(1)} %collective-permute-done.5.refs_1_, f32[360,128]{1,0:T(8,128)S(1)} %collective-permute-done.6.refs_2_, f32[360,128]{1,0:T(8,128)S(1)} %collective-permute-done.7.refs_3_, ...), custom_call_target="tpu_custom_call" | custom-call | flops 2300000000 | bytes 7380000 | tf_op jit(solution)/shard_map/pallas_call | solution.py:645
  49.0 1.5 %collective-permute-done.17.refs_1_ = f32[360,128]{1,0:T(8,128)S(1)} collective-permute-done((f32[360,128]{1,0:T(8,128)S(1)}, f32[360,128]{1,0:T(8,128)S(1)}, u32[]{:S(2)}, u32[]{:S(2)}) %collective-permute-start.17) | collective-permute-done | bytes 184352 | tf_op jit(solution)/shard_map/ppermute | solution.py:547
  50.5 4.1 %collective-permute-done.18.refs_2_ = f32[360,128]{1,0:T(8,128)S(1)} collective-permute-done((f32[360,128]{1,0:T(8,128)S(1)}, f32[360,128]{1,0:T(8,128)S(1)}, u32[]{:S(2)}, u32[]{:S(2)}) %collective-permute-start.18) | collective-permute-done | bytes 184352 | tf_op jit(solution)/shard_map/ppermute | solution.py:547
  54.6 1.4 %shard_map.163 = f32[8,360,256]{2,1,0:T(8,128)} custom-call(f32[8,360,256]{2,1,0:T(8,128)} %shard_map.161._, f32[8,360,128]{2,1,0:T(8,128)S(1)} %get-tuple-element.47.refs_4_.tile_ref, f32[360,128]{1,0:T(8,128)S(1)} %get-tuple-element.59.refs_0_, f32[360,128]{1,0:T(8,128)S(1)} %collective-permute-done.17.refs_1_, ...), custom_call_target="tpu_custom_call", output_to_operand_aliasing={{}: (0, {})} | custom-call | flops 2300000000 | bytes 7380000 | tf_op jit(solution)/shard_map/pallas_call | solution.py:652
  (58 shorter events, 6.2 us)
Async XLA Ops:
  2.1 5.6 %collective-permute-start = (f32[184,128]{1,0:T(8,128)S(1)}, f32[184,128]{1,0:T(8,128)S(1)}, u32[]{:S(2)}, u32[]{:S(2)}) collective-permute-start(f32[184,128]{1,0:T(8,128)S(1)} %get-tuple-element.34), channel_id=1, source_target_pairs={{0,2},{1,3},{2,0},{3,1},{4,6},{5,7},{6,4},{7,5},{8,10},{9,11},{10,... | collective-permute-start | bytes 282632 | tf_op jit(solution)/shard_map/ppermute | solution.py:547
  3.4 5.8 %collective-permute-start.8 = (f32[184,128]{1,0:T(8,128)S(1)}, f32[184,128]{1,0:T(8,128)S(1)}, u32[]{:S(2)}, u32[]{:S(2)}) collective-permute-start(f32[184,128]{1,0:T(8,128)S(1)} %get-tuple-element.45), channel_id=1, source_target_pairs={{0,3},{1,2},{2,1},{3,0},{4,7},{5,6},{6,5},{7,4},{8,11},{9,10},{10,... | collective-permute-start | bytes 282632 | tf_op jit(solution)/shard_map/ppermute | solution.py:547
  4.5 5.3 %collective-permute-start.9 = (f32[184,128]{1,0:T(8,128)S(1)}, f32[184,128]{1,0:T(8,128)S(1)}, u32[]{:S(2)}, u32[]{:S(2)}) collective-permute-start(f32[184,128]{1,0:T(8,128)S(1)} %get-tuple-element.46), channel_id=1, source_target_pairs={{0,1},{1,0},{2,3},{3,2},{4,5},{5,4},{6,7},{7,6},{8,9},{9,8},{10,11... | collective-permute-start | bytes 282632 | tf_op jit(solution)/shard_map/ppermute | solution.py:547
  5.5 7.3 %collective-permute-start.2 = (f32[368,128]{1,0:T(8,128)S(1)}, f32[368,128]{1,0:T(8,128)S(1)}, u32[]{:S(2)}, u32[]{:S(2)}) collective-permute-start(f32[368,128]{1,0:T(8,128)S(1)} %get-tuple-element.37), channel_id=1, source_target_pairs={{0,2},{1,3},{2,0},{3,1},{4,6},{5,7},{6,4},{7,5},{8,10},{9,11},{10,... | collective-permute-start | bytes 565256 | tf_op jit(solution)/shard_map/ppermute | solution.py:547
  6.8 10.3 %collective-permute-start.3 = (f32[368,128]{1,0:T(8,128)S(1)}, f32[368,128]{1,0:T(8,128)S(1)}, u32[]{:S(2)}, u32[]{:S(2)}) collective-permute-start(f32[368,128]{1,0:T(8,128)S(1)} %get-tuple-element.38), channel_id=1, source_target_pairs={{0,3},{1,2},{2,1},{3,0},{4,7},{5,6},{6,5},{7,4},{8,11},{9,10},{10,... | collective-permute-start | bytes 565256 | tf_op jit(solution)/shard_map/ppermute | solution.py:547
  7.7 12.5 %collective-permute-start.4 = (f32[368,128]{1,0:T(8,128)S(1)}, f32[368,128]{1,0:T(8,128)S(1)}, u32[]{:S(2)}, u32[]{:S(2)}) collective-permute-start(f32[368,128]{1,0:T(8,128)S(1)} %get-tuple-element.39), channel_id=1, source_target_pairs={{0,1},{1,0},{2,3},{3,2},{4,5},{5,4},{6,7},{7,6},{8,9},{9,8},{10,11... | collective-permute-start | bytes 565256 | tf_op jit(solution)/shard_map/ppermute | solution.py:547
  9.2 14.3 %collective-permute-start.1 = (f32[632,128]{1,0:T(8,128)S(1)}, f32[632,128]{1,0:T(8,128)S(1)}, u32[]{:S(2)}, u32[]{:S(2)}) collective-permute-start(f32[632,128]{1,0:T(8,128)S(1)} %get-tuple-element.35), channel_id=1, source_target_pairs={{0,1},{1,0},{2,3},{3,2},{4,5},{5,4},{6,7},{7,6},{8,9},{9,8},{10,11... | collective-permute-start | bytes 970760 | tf_op jit(solution)/shard_map/ppermute | solution.py:547
  9.8 23.5 %collective-permute-start.12 = (f32[632,128]{1,0:T(8,128)S(1)}, f32[632,128]{1,0:T(8,128)S(1)}, u32[]{:S(2)}, u32[]{:S(2)}) collective-permute-start(f32[632,128]{1,0:T(8,128)S(1)} %get-tuple-element.52), channel_id=1, source_target_pairs={{0,2},{1,3},{2,0},{3,1},{4,6},{5,7},{6,4},{7,5},{8,10},{9,11},{10,... | collective-permute-start | bytes 970760 | tf_op jit(solution)/shard_map/ppermute | solution.py:547
  11.3 12.2 %copy-start.2 = (bf16[720,720]{1,0:T(8,128)(2,1)S(1)}, bf16[720,720]{1,0:T(8,128)(2,1)}, u32[]{:S(2)}) copy-start(bf16[720,720]{1,0:T(8,128)(2,1)} %constant.30.clone.refs_4_.refs_8_) | copy-start | bytes 3110404
  11.3 12.2 %copy-start.3 = (bf16[720,720]{1,0:T(8,128)(2,1)S(1)}, bf16[720,720]{1,0:T(8,128)(2,1)}, u32[]{:S(2)}) copy-start(bf16[720,720]{1,0:T(8,128)(2,1)} %constant.37.clone.refs_11_.refs_15_) | copy-start | bytes 3110404
  11.3 12.2 %copy-start.4 = (bf16[720,720]{1,0:T(8,128)(2,1)S(1)}, bf16[720,720]{1,0:T(8,128)(2,1)}, u32[]{:S(2)}) copy-start(bf16[720,720]{1,0:T(8,128)(2,1)} %constant.36.clone.refs_10_.refs_14_) | copy-start | bytes 3110404
  11.3 12.2 %copy-start.5 = (f32[1488,128]{1,0:T(8,128)S(1)}, f32[1488,128]{1,0:T(8,128)}, u32[]{:S(2)}) copy-start(f32[1488,128]{1,0:T(8,128)} %constant.38.clone.mode_ref) | copy-start | bytes 2285572
  12.8 20.5 %collective-permute-start.13 = (f32[632,128]{1,0:T(8,128)S(1)}, f32[632,128]{1,0:T(8,128)S(1)}, u32[]{:S(2)}, u32[]{:S(2)}) collective-permute-start(f32[632,128]{1,0:T(8,128)S(1)} %get-tuple-element.53), channel_id=1, source_target_pairs={{0,3},{1,2},{2,1},{3,0},{4,7},{5,6},{6,5},{7,4},{8,11},{9,10},{10,... | collective-permute-start | bytes 970760 | tf_op jit(solution)/shard_map/ppermute | solution.py:547
  17.1 10.9 %collective-permute-start.10 = (f32[376,128]{1,0:T(8,128)S(1)}, f32[376,128]{1,0:T(8,128)S(1)}, u32[]{:S(2)}, u32[]{:S(2)}) collective-permute-start(f32[376,128]{1,0:T(8,128)S(1)} %get-tuple-element.48), channel_id=1, source_target_pairs={{0,4},{4,8},{8,12},{12,16},{16,20},{20,24},{24,28},{1,5},{5,9},{9,... | collective-permute-start | bytes 577544 | tf_op jit(solution)/shard_map/ppermute | solution.py:612
  20.2 10.5 %collective-permute-start.11 = (f32[376,128]{1,0:T(8,128)S(1)}, f32[376,128]{1,0:T(8,128)S(1)}, u32[]{:S(2)}, u32[]{:S(2)}) collective-permute-start(f32[376,128]{1,0:T(8,128)S(1)} %get-tuple-element.49), channel_id=1, source_target_pairs={{4,0},{8,4},{12,8},{16,12},{20,16},{24,20},{28,24},{5,1},{9,5},{13... | collective-permute-start | bytes 577544 | tf_op jit(solution)/shard_map/ppermute | solution.py:613
  26.4 11.7 %collective-permute-start.5 = (f32[360,128]{1,0:T(8,128)S(1)}, f32[360,128]{1,0:T(8,128)S(1)}, u32[]{:S(2)}, u32[]{:S(2)}) collective-permute-start(f32[360,128]{1,0:T(8,128)S(1)} %get-tuple-element.41), channel_id=1, source_target_pairs={{0,2},{1,3},{2,0},{3,1},{4,6},{5,7},{6,4},{7,5},{8,10},{9,11},{10,... | collective-permute-start | bytes 552968 | tf_op jit(solution)/shard_map/ppermute | solution.py:547
  28.0 13.1 %collective-permute-start.6 = (f32[360,128]{1,0:T(8,128)S(1)}, f32[360,128]{1,0:T(8,128)S(1)}, u32[]{:S(2)}, u32[]{:S(2)}) collective-permute-start(f32[360,128]{1,0:T(8,128)S(1)} %get-tuple-element.42), channel_id=1, source_target_pairs={{0,3},{1,2},{2,1},{3,0},{4,7},{5,6},{6,5},{7,4},{8,11},{9,10},{10,... | collective-permute-start | bytes 552968 | tf_op jit(solution)/shard_map/ppermute | solution.py:547
  30.7 11.9 %collective-permute-start.7 = (f32[360,128]{1,0:T(8,128)S(1)}, f32[360,128]{1,0:T(8,128)S(1)}, u32[]{:S(2)}, u32[]{:S(2)}) collective-permute-start(f32[360,128]{1,0:T(8,128)S(1)} %get-tuple-element.43), channel_id=1, source_target_pairs={{0,1},{1,0},{2,3},{3,2},{4,5},{5,4},{6,7},{7,6},{8,9},{9,8},{10,11... | collective-permute-start | bytes 552968 | tf_op jit(solution)/shard_map/ppermute | solution.py:547
  36.3 6.8 %collective-permute-start.14 = (f32[360,128]{1,0:T(8,128)S(1)}, f32[360,128]{1,0:T(8,128)S(1)}, u32[]{:S(2)}, u32[]{:S(2)}) collective-permute-start(f32[360,128]{1,0:T(8,128)S(1)} %get-tuple-element.55), channel_id=1, source_target_pairs={{0,2},{1,3},{2,0},{3,1},{4,6},{5,7},{6,4},{7,5},{8,10},{9,11},{10,... | collective-permute-start | bytes 552968 | tf_op jit(solution)/shard_map/ppermute | solution.py:547
  37.8 9.3 %collective-permute-start.15 = (f32[360,128]{1,0:T(8,128)S(1)}, f32[360,128]{1,0:T(8,128)S(1)}, u32[]{:S(2)}, u32[]{:S(2)}) collective-permute-start(f32[360,128]{1,0:T(8,128)S(1)} %get-tuple-element.56), channel_id=1, source_target_pairs={{0,3},{1,2},{2,1},{3,0},{4,7},{5,6},{6,5},{7,4},{8,11},{9,10},{10,... | collective-permute-start | bytes 552968 | tf_op jit(solution)/shard_map/ppermute | solution.py:547
  38.0 9.1 %collective-permute-start.16 = (f32[360,128]{1,0:T(8,128)S(1)}, f32[360,128]{1,0:T(8,128)S(1)}, u32[]{:S(2)}, u32[]{:S(2)}) collective-permute-start(f32[360,128]{1,0:T(8,128)S(1)} %get-tuple-element.57), channel_id=1, source_target_pairs={{0,1},{1,0},{2,3},{3,2},{4,5},{5,4},{6,7},{7,6},{8,9},{9,8},{10,11... | collective-permute-start | bytes 552968 | tf_op jit(solution)/shard_map/ppermute | solution.py:547
  41.1 9.4 %collective-permute-start.17 = (f32[360,128]{1,0:T(8,128)S(1)}, f32[360,128]{1,0:T(8,128)S(1)}, u32[]{:S(2)}, u32[]{:S(2)}) collective-permute-start(f32[360,128]{1,0:T(8,128)S(1)} %get-tuple-element.60), channel_id=1, source_target_pairs={{0,2},{1,3},{2,0},{3,1},{4,6},{5,7},{6,4},{7,5},{8,10},{9,11},{10,... | collective-permute-start | bytes 552968 | tf_op jit(solution)/shard_map/ppermute | solution.py:547
  42.6 12.0 %collective-permute-start.18 = (f32[360,128]{1,0:T(8,128)S(1)}, f32[360,128]{1,0:T(8,128)S(1)}, u32[]{:S(2)}, u32[]{:S(2)}) collective-permute-start(f32[360,128]{1,0:T(8,128)S(1)} %get-tuple-element.61), channel_id=1, source_target_pairs={{0,3},{1,2},{2,1},{3,0},{4,7},{5,6},{6,5},{7,4},{8,11},{9,10},{10,... | collective-permute-start | bytes 552968 | tf_op jit(solution)/shard_map/ppermute | solution.py:547
  43.1 11.5 %collective-permute-start.19 = (f32[360,128]{1,0:T(8,128)S(1)}, f32[360,128]{1,0:T(8,128)S(1)}, u32[]{:S(2)}, u32[]{:S(2)}) collective-permute-start(f32[360,128]{1,0:T(8,128)S(1)} %get-tuple-element.62), channel_id=1, source_target_pairs={{0,1},{1,0},{2,3},{3,2},{4,5},{5,4},{6,7},{7,6},{8,9},{9,8},{10,11... | collective-permute-start | bytes 552968 | tf_op jit(solution)/shard_map/ppermute | solution.py:547
  (12 other events, 118.6 us)

commit v7 on v6

--- a/solution.py
+++ b/solution.py
@@ -199,16 +199,10 @@
         put(packs, start, partner_order(blocks, me))
 
     each_chunk(width, size, pack)
-    line = lax.broadcasted_iota(jnp.int32, (8, LANES), 0)
-    sides = []
-    for row in range(rows):
-        side = jnp.where(line == 0, tile_ref[row, 0:8], 0.0)
-        sides.append(jnp.where(line == 7, tile_ref[row, width - 8 : width], side))
-    masks8 = group_masks(8, part)
-    put(packs, width, partner_order(transpose_groups(sides, masks8, part, range(4, 8)), me))
+
 
 def edge_kernel(part, *refs):
-    (wind_first, wind_last), (tile_first, tile_last), packs = refs[:2], refs[2:4], refs[4:]
+    (wind_first, wind_last), (tile_first, tile_last), (begin_ref, end_ref), packs = refs[:2], refs[2:4], refs[4:6], refs[6:]
     _, width, _ = tile_first.shape
     me = lax.axis_index("lon")
     half = 0.5 * WIND_COEF
@@ -221,9 +215,18 @@
             lines = pl.ds(pl.multiple_of(begin, 8), 8)
             tiles += [wind_first[0, lines] - half * tile_first[1, lines], tile_first[0, lines]]
             tiles += [wind_last[1, lines] + half * tile_last[0, lines], tile_last[1, lines]]
+        return tiles
+
+    def send_out(start, tiles):
         put(packs, start, partner_order(transpose_groups(tiles, masks, part, range(4, 8)), me))
 
-    each_chunk(head, 8, pack)
+    each_chunk(head - 8, 8, lambda start: send_out(start, pack(start)))
+    line = lax.broadcasted_iota(jnp.int32, (8, LANES), 0)
+    ends = []
+    for row in range(4):
+        inner = jnp.where(line == 1, pltpu.roll(begin_ref[row + 4], 1, 0), pltpu.roll(end_ref[row + 4], 7, 0))
+        ends.append(jnp.where(line == 0, begin_ref[row], jnp.where(line == 7, end_ref[row], inner)))
+    send_out(head - 8, pack(head - 8)[:4] + ends)
 
 
 def rim_lines(width):
@@ -419,7 +422,7 @@
     return jnp.minimum(1.0, ratio * ratio)
 
 
-def zonal_spec_kernel(bounds, part, flag_ref, cut_ref, mode_ref, _, q0, q2, q3, q1, *refs):
+def zonal_spec_kernel(bounds, part, flag_ref, cut_ref, mode_ref, _, e0, e2, e3, e1, q0, q2, q3, q1, *refs):
     forward, inverse, outs, spec_ref = refs[:6], refs[6:12], refs[12:16], refs[16]
     rows = flag_ref.shape[0]
     width = outs[0].shape[0]
@@ -427,7 +430,13 @@
     quarters = (q0, q1, q2, q3)
     scale = WIND_COEF / (2.0 * lane_cosine(0, rows, part))
     line = lax.broadcasted_iota(jnp.int32, (8, LANES), 0)
-    sides = partner_order([q[width : width + 8] for q in quarters], me)
+    low = lane_ids((8, LANES)) < LANES // 2
+    sides = []
+    for edge in (e0, e1, e2, e3):
+        value = edge[edge.shape[0] - 8 :]
+        inner = jnp.where(line == 0, pltpu.roll(value, 7, 0), pltpu.roll(value, 1, 0))
+        sides.append(jnp.where(low, turn_groups(value, -4, part), inner))
+    sides = partner_order(sides, me)
     starts = [jnp.where(line == 0, scale * pltpu.roll(sides[(q + 3) % 4], 1, 0), 0.0) for q in range(4)]
     ends = [jnp.where(line == 7, scale * pltpu.roll(sides[(q + 1) % 4], 7, 0), 0.0) for q in range(4)]
     starts, ends = partner_order(starts, me), partner_order(ends, me)
@@ -573,22 +582,24 @@
     low_tile, high_tile = tile_of(state.shape, 0), tile_of(state.shape, 1)
 
     edges = (rim_lines(width), LANES)
-    sided = (skip, LANES)
 
     def two_rows(row, index):
         return pl.BlockSpec((2, width, LANES), lambda step: (row, 0, index))
+
+    def end_lines(index):
+        return pl.BlockSpec((rows, 8, LANES), lambda step: (0, index, 1))
 
     edge_packs = call(
         functools.partial(edge_kernel, part),
         [f32(*edges)] * 4,
-        [two_rows(0, 0), two_rows(rows // 2 - 1, 0), two_rows(0, 1), two_rows(rows // 2 - 1, 1)],
+        [two_rows(0, 0), two_rows(rows // 2 - 1, 0), two_rows(0, 1), two_rows(rows // 2 - 1, 1)] + [end_lines(0), end_lines(width // 8 - 1)],
         [whole(edges)] * 4,
-    )(state, state, state, state)
+    )(*[state] * 6)
     zonal_packs = call(
         functools.partial(zonal_kernel, part),
-        [f32(*sided)] * 4,
+        [f32(*block)] * 4,
         [low_tile, high_tile],
-        [whole(sided)] * 4,
+        [whole(block)] * 4,
         scratch_shapes=[pltpu.VMEM(full, F32)],
     )(state, state)
     edge_circle = exchange(edge_packs)
@@ -615,9 +626,9 @@
     *zonal_parts, zonal_spec = call(
         functools.partial(zonal_spec_kernel, bounds, part),
         [f32(*block)] * 4 + [f32(*spectrum)],
-        [SMEM] * 2 + [whole(mode.shape), ANY] + [whole(sided)] * 4 + table_specs,
+        [SMEM] * 2 + [whole(mode.shape), ANY] + [whole(edges)] * 4 + [whole(block)] * 4 + table_specs,
         [whole(block)] * 4 + [whole(spectrum)],
-    )(filter_flag, cutoff, mode, second_circle[3], *first_circle, *forward, *inverse)
+    )(filter_flag, cutoff, mode, second_circle[3], *edge_circle, *first_circle, *forward, *inverse)
     zonal_back = exchange(zonal_parts)
     edge_spec = call(
         functools.partial(edge_spec_kernel, bounds, part, skip),
@@ -767,7 +778,7 @@
 def body(state, filter_flag, cutoff):
     rows, width, depth = state.shape
     levels = depth // 4
-    lanes_fit = rows == 8 and 2 * levels == LANES and width % 8 == 0
+    lanes_fit = rows == 8 and 2 * levels == LANES and width % 16 == 8
     if lax.axis_size("lon") == 4 and lanes_fit:
         return packed_body(state, filter_flag, cutoff)
     return plain_body(state, filter_flag, cutoff)

time: 57.1 us -> 56.9 us (level)
  no operation moved by 1% of the time
where the time goes in v7:
time: 56.9 us; the launch traced here: 56 us
  starting transfers between devices  22.9 us (40%)
  Pallas kernels  17.5 us (31%)
  waiting for transfers between devices  13.2 us (23%)
  local copies, waits for them, and re-layouts  1.92 us (3%)
    ppermute x18, starting transfers between devices, send(): return lax.ppermute(block, 'lon', [(i, i ^ step) for i in range(4)])  16.5 us
    ppermute x18, waiting for transfers between devices, send(): return lax.ppermute(block, 'lon', [(i, i ^ step) for i in range(4)])  11.3 us
    ppermute x1, starting transfers between devices, packed_body(): lax.ppermute(to_south, 'lat', [(i + 1, i) for i in range(bands - 1)])  3.24 us
    ppermute x1, starting transfers between devices, packed_body(): lax.ppermute(to_north, 'lat', [(i, i + 1) for i in range(bands - 1)])  3.11 us
    pallas_call x1, Pallas kernels, packed_body(): call(functools.partial(merid_spec_kernel, bounds, part), [f32(*block)] *...  3.03 us
    pallas_call x1, Pallas kernels, packed_body(): call(functools.partial(press_back_kernel, bounds, part), [f32(*block)] *...  2.85 us
    pallas_call x1, Pallas kernels, packed_body(): call(functools.partial(zonal_spec_kernel, bounds, part), [f32(*block)] *...  2.79 us
    pallas_call x1, Pallas kernels, packed_body(): call(functools.partial(edge_spec_kernel, bounds, part, skip), f32(*spectr...  2.06 us
  transfers between devices with their start and end apart: 20, of which 6 were waited for; matrix products, arithmetic and copies ran while one was open for 0% of the time, Pallas kernels for 28%

profile of v7, /device:TPU:17, one launch (start us, length us, event | category | flops | bytes accessed | tf_op | source)
XLA Modules:
  0.0 56.0 jit_solution(5766841456542751582)
XLA Ops:
  0.0 1.8 %copy-done = f32[8,360,256]{2,1,0:T(8,128)S(1)} copy-done((f32[8,360,256]{2,1,0:T(8,128)S(1)}, f32[8,360,256]{2,1,0:T(8,128)}, u32[]{:S(2)}) %copy-start) | copy-done | bytes 2949144
  2.1 1.3 %collective-permute-start = (f32[184,128]{1,0:T(8,128)S(1)}, f32[184,128]{1,0:T(8,128)S(1)}, u32[]{:S(2)}, u32[]{:S(2)}) collective-permute-start(f32[184,128]{1,0:T(8,128)S(1)} %get-tuple-element.34), channel_id=1, source_target_pairs={{0,2},{1,3},{2,0},{3,1},{4,6},{5,7},{6,4},{7,5},{8,10},{9,11},{10,... | collective-permute-start | bytes 282632 | tf_op jit(solution)/shard_map/ppermute | solution.py:556
  3.4 1.1 %collective-permute-start.2 = (f32[184,128]{1,0:T(8,128)S(1)}, f32[184,128]{1,0:T(8,128)S(1)}, u32[]{:S(2)}, u32[]{:S(2)}) collective-permute-start(f32[184,128]{1,0:T(8,128)S(1)} %get-tuple-element.37), channel_id=1, source_target_pairs={{0,3},{1,2},{2,1},{3,0},{4,7},{5,6},{6,5},{7,4},{8,11},{9,10},{10,... | collective-permute-start | bytes 282632 | tf_op jit(solution)/shard_map/ppermute | solution.py:556
  4.5 1.0 %shard_map.156 = (f32[360,128]{1,0:T(8,128)S(1)}, f32[360,128]{1,0:T(8,128)S(1)}, f32[360,128]{1,0:T(8,128)S(1)}, f32[360,128]{1,0:T(8,128)S(1)}) custom-call(f32[8,360,256]{2,1,0:T(8,128)S(1)} %copy-done, f32[8,360,256]{2,1,0:T(8,128)S(1)} %copy-done), custom_call_target="tpu_custom_call" | custom-call | flops 2300000000 | bytes 7380000 | tf_op jit(solution)/shard_map/pallas_call | solution.py:598
  5.5 1.3 %collective-permute-start.4 = (f32[360,128]{1,0:T(8,128)S(1)}, f32[360,128]{1,0:T(8,128)S(1)}, u32[]{:S(2)}, u32[]{:S(2)}) collective-permute-start(f32[360,128]{1,0:T(8,128)S(1)} %get-tuple-element.40), channel_id=1, source_target_pairs={{0,2},{1,3},{2,0},{3,1},{4,6},{5,7},{6,4},{7,5},{8,10},{9,11},{10,... | collective-permute-start | bytes 552968 | tf_op jit(solution)/shard_map/ppermute | solution.py:556
  7.7 1.5 %shard_map.155 = (f32[632,128]{1,0:T(8,128)S(1)}, f32[632,128]{1,0:T(8,128)S(1)}, f32[632,128]{1,0:T(8,128)S(1)}, f32[632,128]{1,0:T(8,128)S(1)}, f32[8,360,128]{2,1,0:T(8,128)S(1)}) custom-call(f32[8,360,256]{2,1,0:T(8,128)S(1)} %copy-done, f32[8,360,256]{2,1,0:T(8,128)S(1)} %copy-done, f32[184,128]{1,0:T(8,128)S(1)} %collective-permute-done._.e2.refs_1_), custom_call_target="tpu_custom_call" | custom-call | flops 2300000000 | bytes 7380000 | tf_op jit(solution)/shard_map/pallas_call | solution.py:607
  9.8 1.5 %collective-permute-start.12 = (f32[632,128]{1,0:T(8,128)S(1)}, f32[632,128]{1,0:T(8,128)S(1)}, u32[]{:S(2)}, u32[]{:S(2)}) collective-permute-start(f32[632,128]{1,0:T(8,128)S(1)} %get-tuple-element.52), channel_id=1, source_target_pairs={{0,2},{1,3},{2,0},{3,1},{4,6},{5,7},{6,4},{7,5},{8,10},{9,11},{10,... | collective-permute-start | bytes 970760 | tf_op jit(solution)/shard_map/ppermute | solution.py:556
  12.7 2.4 %collective-permute-start.13 = (f32[632,128]{1,0:T(8,128)S(1)}, f32[632,128]{1,0:T(8,128)S(1)}, u32[]{:S(2)}, u32[]{:S(2)}) collective-permute-start(f32[632,128]{1,0:T(8,128)S(1)} %get-tuple-element.53), channel_id=1, source_target_pairs={{0,3},{1,2},{2,1},{3,0},{4,7},{5,6},{6,5},{7,4},{8,11},{9,10},{10,... | collective-permute-start | bytes 970760 | tf_op jit(solution)/shard_map/ppermute | solution.py:556
  15.1 1.8 %collective-permute-done.5.q3 = f32[360,128]{1,0:T(8,128)S(1)} collective-permute-done((f32[360,128]{1,0:T(8,128)S(1)}, f32[360,128]{1,0:T(8,128)S(1)}, u32[]{:S(2)}, u32[]{:S(2)}) %collective-permute-start.5) | collective-permute-done | bytes 184352 | tf_op jit(solution)/shard_map/ppermute | solution.py:556
  16.9 3.1 %collective-permute-start.10 = (f32[376,128]{1,0:T(8,128)S(1)}, f32[376,128]{1,0:T(8,128)S(1)}, u32[]{:S(2)}, u32[]{:S(2)}) collective-permute-start(f32[376,128]{1,0:T(8,128)S(1)} %get-tuple-element.48), channel_id=1, source_target_pairs={{0,4},{4,8},{8,12},{12,16},{16,20},{20,24},{24,28},{1,5},{5,9},{9,... | collective-permute-start | bytes 577544 | tf_op jit(solution)/shard_map/ppermute | solution.py:623
  20.0 3.2 %collective-permute-start.11 = (f32[376,128]{1,0:T(8,128)S(1)}, f32[376,128]{1,0:T(8,128)S(1)}, u32[]{:S(2)}, u32[]{:S(2)}) collective-permute-start(f32[376,128]{1,0:T(8,128)S(1)} %get-tuple-element.49), channel_id=1, source_target_pairs={{4,0},{8,4},{12,8},{16,12},{20,16},{24,20},{28,24},{5,1},{9,5},{13... | collective-permute-start | bytes 577544 | tf_op jit(solution)/shard_map/ppermute | solution.py:624
  23.4 2.8 %shard_map.157 = (f32[360,128]{1,0:T(8,128)S(1)}, f32[360,128]{1,0:T(8,128)S(1)}, f32[360,128]{1,0:T(8,128)S(1)}, f32[360,128]{1,0:T(8,128)S(1)}, f32[1488,128]{1,0:T(8,128)S(1)}) custom-call(s32[8]{0:T(128)S(1)} %copy-done.14, s32[8]{0:T(128)S(1)} %copy-done.15, f32[1488,128]{1,0:T(8,128)S(1)} %copy-done.5, ...), custom_call_target="tpu_custom_call" | custom-call | flops 2300000000 | bytes 7380000 | tf_op jit(solution)/shard_map/pallas_call | solution.py:626
  26.2 1.6 %collective-permute-start.7 = (f32[360,128]{1,0:T(8,128)S(1)}, f32[360,128]{1,0:T(8,128)S(1)}, u32[]{:S(2)}, u32[]{:S(2)}) collective-permute-start(f32[360,128]{1,0:T(8,128)S(1)} %get-tuple-element.44), channel_id=1, source_target_pairs={{0,2},{1,3},{2,0},{3,1},{4,6},{5,7},{6,4},{7,5},{8,10},{9,11},{10,... | collective-permute-start | bytes 552968 | tf_op jit(solution)/shard_map/ppermute | solution.py:556
  28.7 1.9 %collective-permute-done.11.north_ref = f32[376,128]{1,0:T(8,128)S(1)} collective-permute-done((f32[376,128]{1,0:T(8,128)S(1)}, f32[376,128]{1,0:T(8,128)S(1)}, u32[]{:S(2)}, u32[]{:S(2)}) %collective-permute-start.11) | collective-permute-done | bytes 192544 | tf_op jit(solution)/shard_map/ppermute | solution.py:624
  31.0 2.1 %shard_map.159.edge_ref = f32[1488,128]{1,0:T(8,128)S(1)} custom-call(s32[8]{0:T(128)S(1)} %copy-done.14, s32[8]{0:T(128)S(1)} %copy-done.15, f32[1488,128]{1,0:T(8,128)S(1)} %copy-done.5, f32[376,128]{1,0:T(8,128)S(1)} %collective-permute-done.10.south_ref, f32[376,128]{1,0:T(8,128)S(1)} %collective-permute-done.11.north_ref, ...), custom_call_target="tpu_custom_call" | custom-call | flops 2300000000 | bytes 7380000 | tf_op jit(solution)/shard_map/pallas_call | solution.py:633
  33.1 3.0 %shard_map.160 = (f32[360,128]{1,0:T(8,128)S(1)}, f32[360,128]{1,0:T(8,128)S(1)}, f32[360,128]{1,0:T(8,128)S(1)}, f32[360,128]{1,0:T(8,128)S(1)}, f32[1488,128]{1,0:T(8,128)S(1)}) custom-call(s32[8]{0:T(128)S(1)} %copy-done.14, s32[8]{0:T(128)S(1)} %copy-done.15, f32[1488,128]{1,0:T(8,128)S(1)} %copy-done.5, f32[1488,128]{1,0:T(8,128)S(1)} %shard_map.159.edge_ref, ...), custom_call_target="tpu_custom_call" | custom-call | flops 2300000000 | bytes 7380000 | tf_op jit(solution)/shard_map/pallas_call | solution.py:640
  36.2 1.5 %collective-permute-start.14 = (f32[360,128]{1,0:T(8,128)S(1)}, f32[360,128]{1,0:T(8,128)S(1)}, u32[]{:S(2)}, u32[]{:S(2)}) collective-permute-start(f32[360,128]{1,0:T(8,128)S(1)} %get-tuple-element.55), channel_id=1, source_target_pairs={{0,2},{1,3},{2,0},{3,1},{4,6},{5,7},{6,4},{7,5},{8,10},{9,11},{10,... | collective-permute-start | bytes 552968 | tf_op jit(solution)/shard_map/ppermute | solution.py:556
  38.1 2.8 %shard_map.162 = (f32[360,128]{1,0:T(8,128)S(1)}, f32[360,128]{1,0:T(8,128)S(1)}, f32[360,128]{1,0:T(8,128)S(1)}, f32[360,128]{1,0:T(8,128)S(1)}) custom-call(s32[8]{0:T(128)S(1)} %copy-done.14, s32[8]{0:T(128)S(1)} %copy-done.15, f32[1488,128]{1,0:T(8,128)S(1)} %copy-done.5, f32[1488,128]{1,0:T(8,128)S(1)} %get-tuple-element.50._.zonal_ref, ...), custom_call_target="tpu_custom_call" | custom-call | flops 2300000000 | bytes 7380000 | tf_op jit(solution)/shard_map/pallas_call | solution.py:648
  41.0 1.5 %collective-permute-start.17 = (f32[360,128]{1,0:T(8,128)S(1)}, f32[360,128]{1,0:T(8,128)S(1)}, u32[]{:S(2)}, u32[]{:S(2)}) collective-permute-start(f32[360,128]{1,0:T(8,128)S(1)} %get-tuple-element.60), channel_id=1, source_target_pairs={{0,2},{1,3},{2,0},{3,1},{4,6},{5,7},{6,4},{7,5},{8,10},{9,11},{10,... | collective-permute-start | bytes 552968 | tf_op jit(solution)/shard_map/ppermute | solution.py:556
  43.7 3.3 %collective-permute-done.15.refs_6_ = f32[360,128]{1,0:T(8,128)S(1)} collective-permute-done((f32[360,128]{1,0:T(8,128)S(1)}, f32[360,128]{1,0:T(8,128)S(1)}, u32[]{:S(2)}, u32[]{:S(2)}) %collective-permute-start.15) | collective-permute-done | bytes 184352 | tf_op jit(solution)/shard_map/ppermute | solution.py:556
  46.9 1.9 %shard_map.161._ = f32[8,360,256]{2,1,0:T(8,128)} custom-call(f32[360,128]{1,0:T(8,128)S(1)} %get-tuple-element.43.refs_0_, f32[360,128]{1,0:T(8,128)S(1)} %collective-permute-done.7.refs_1_, f32[360,128]{1,0:T(8,128)S(1)} %collective-permute-done.8.refs_2_, f32[360,128]{1,0:T(8,128)S(1)} %collective-permute-done.9.refs_3_, ...), custom_call_target="tpu_custom_call" | custom-call | flops 2300000000 | bytes 7380000 | tf_op jit(solution)/shard_map/pallas_call | solution.py:656
  48.9 1.5 %collective-permute-done.17.refs_1_ = f32[360,128]{1,0:T(8,128)S(1)} collective-permute-done((f32[360,128]{1,0:T(8,128)S(1)}, f32[360,128]{1,0:T(8,128)S(1)}, u32[]{:S(2)}, u32[]{:S(2)}) %collective-permute-start.17) | collective-permute-done | bytes 184352 | tf_op jit(solution)/shard_map/ppermute | solution.py:556
  50.4 4.1 %collective-permute-done.18.refs_2_ = f32[360,128]{1,0:T(8,128)S(1)} collective-permute-done((f32[360,128]{1,0:T(8,128)S(1)}, f32[360,128]{1,0:T(8,128)S(1)}, u32[]{:S(2)}, u32[]{:S(2)}) %collective-permute-start.18) | collective-permute-done | bytes 184352 | tf_op jit(solution)/shard_map/ppermute | solution.py:556
  54.4 1.4 %shard_map.163 = f32[8,360,256]{2,1,0:T(8,128)} custom-call(f32[8,360,256]{2,1,0:T(8,128)} %shard_map.161._, f32[8,360,128]{2,1,0:T(8,128)S(1)} %get-tuple-element.47.refs_4_.tile_ref, f32[360,128]{1,0:T(8,128)S(1)} %get-tuple-element.59.refs_0_, f32[360,128]{1,0:T(8,128)S(1)} %collective-permute-done.17.refs_1_, ...), custom_call_target="tpu_custom_call", output_to_operand_aliasing={{}: (0, {})} | custom-call | flops 2300000000 | bytes 7380000 | tf_op jit(solution)/shard_map/pallas_call | solution.py:663
  (58 shorter events, 6.1 us)
Async XLA Ops:
  2.1 5.6 %collective-permute-start = (f32[184,128]{1,0:T(8,128)S(1)}, f32[184,128]{1,0:T(8,128)S(1)}, u32[]{:S(2)}, u32[]{:S(2)}) collective-permute-start(f32[184,128]{1,0:T(8,128)S(1)} %get-tuple-element.34), channel_id=1, source_target_pairs={{0,2},{1,3},{2,0},{3,1},{4,6},{5,7},{6,4},{7,5},{8,10},{9,11},{10,... | collective-permute-start | bytes 282632 | tf_op jit(solution)/shard_map/ppermute | solution.py:556
  3.4 5.8 %collective-permute-start.2 = (f32[184,128]{1,0:T(8,128)S(1)}, f32[184,128]{1,0:T(8,128)S(1)}, u32[]{:S(2)}, u32[]{:S(2)}) collective-permute-start(f32[184,128]{1,0:T(8,128)S(1)} %get-tuple-element.37), channel_id=1, source_target_pairs={{0,3},{1,2},{2,1},{3,0},{4,7},{5,6},{6,5},{7,4},{8,11},{9,10},{10,... | collective-permute-start | bytes 282632 | tf_op jit(solution)/shard_map/ppermute | solution.py:556
  4.5 5.3 %collective-permute-start.3 = (f32[184,128]{1,0:T(8,128)S(1)}, f32[184,128]{1,0:T(8,128)S(1)}, u32[]{:S(2)}, u32[]{:S(2)}) collective-permute-start(f32[184,128]{1,0:T(8,128)S(1)} %get-tuple-element.38), channel_id=1, source_target_pairs={{0,1},{1,0},{2,3},{3,2},{4,5},{5,4},{6,7},{7,6},{8,9},{9,8},{10,11... | collective-permute-start | bytes 282632 | tf_op jit(solution)/shard_map/ppermute | solution.py:556
  5.5 7.3 %collective-permute-start.4 = (f32[360,128]{1,0:T(8,128)S(1)}, f32[360,128]{1,0:T(8,128)S(1)}, u32[]{:S(2)}, u32[]{:S(2)}) collective-permute-start(f32[360,128]{1,0:T(8,128)S(1)} %get-tuple-element.40), channel_id=1, source_target_pairs={{0,2},{1,3},{2,0},{3,1},{4,6},{5,7},{6,4},{7,5},{8,10},{9,11},{10,... | collective-permute-start | bytes 552968 | tf_op jit(solution)/shard_map/ppermute | solution.py:556
  6.8 10.1 %collective-permute-start.5 = (f32[360,128]{1,0:T(8,128)S(1)}, f32[360,128]{1,0:T(8,128)S(1)}, u32[]{:S(2)}, u32[]{:S(2)}) collective-permute-start(f32[360,128]{1,0:T(8,128)S(1)} %get-tuple-element.41), channel_id=1, source_target_pairs={{0,3},{1,2},{2,1},{3,0},{4,7},{5,6},{6,5},{7,4},{8,11},{9,10},{10,... | collective-permute-start | bytes 552968 | tf_op jit(solution)/shard_map/ppermute | solution.py:556
  7.7 12.3 %collective-permute-start.6 = (f32[360,128]{1,0:T(8,128)S(1)}, f32[360,128]{1,0:T(8,128)S(1)}, u32[]{:S(2)}, u32[]{:S(2)}) collective-permute-start(f32[360,128]{1,0:T(8,128)S(1)} %get-tuple-element.42), channel_id=1, source_target_pairs={{0,1},{1,0},{2,3},{3,2},{4,5},{5,4},{6,7},{7,6},{8,9},{9,8},{10,11... | collective-permute-start | bytes 552968 | tf_op jit(solution)/shard_map/ppermute | solution.py:556
  9.2 14.1 %collective-permute-start.1 = (f32[632,128]{1,0:T(8,128)S(1)}, f32[632,128]{1,0:T(8,128)S(1)}, u32[]{:S(2)}, u32[]{:S(2)}) collective-permute-start(f32[632,128]{1,0:T(8,128)S(1)} %get-tuple-element.35), channel_id=1, source_target_pairs={{0,1},{1,0},{2,3},{3,2},{4,5},{5,4},{6,7},{7,6},{8,9},{9,8},{10,11... | collective-permute-start | bytes 970760 | tf_op jit(solution)/shard_map/ppermute | solution.py:556
  9.8 23.3 %collective-permute-start.12 = (f32[632,128]{1,0:T(8,128)S(1)}, f32[632,128]{1,0:T(8,128)S(1)}, u32[]{:S(2)}, u32[]{:S(2)}) collective-permute-start(f32[632,128]{1,0:T(8,128)S(1)} %get-tuple-element.52), channel_id=1, source_target_pairs={{0,2},{1,3},{2,0},{3,1},{4,6},{5,7},{6,4},{7,5},{8,10},{9,11},{10,... | collective-permute-start | bytes 970760 | tf_op jit(solution)/shard_map/ppermute | solution.py:556
  11.2 12.0 %copy-start.2 = (bf16[720,720]{1,0:T(8,128)(2,1)S(1)}, bf16[720,720]{1,0:T(8,128)(2,1)}, u32[]{:S(2)}) copy-start(bf16[720,720]{1,0:T(8,128)(2,1)} %constant.30.clone.refs_4_.refs_8_) | copy-start | bytes 3110404
  11.3 12.0 %copy-start.3 = (bf16[720,720]{1,0:T(8,128)(2,1)S(1)}, bf16[720,720]{1,0:T(8,128)(2,1)}, u32[]{:S(2)}) copy-start(bf16[720,720]{1,0:T(8,128)(2,1)} %constant.37.clone.refs_11_.refs_15_) | copy-start | bytes 3110404
  11.3 12.0 %copy-start.4 = (bf16[720,720]{1,0:T(8,128)(2,1)S(1)}, bf16[720,720]{1,0:T(8,128)(2,1)}, u32[]{:S(2)}) copy-start(bf16[720,720]{1,0:T(8,128)(2,1)} %constant.36.clone.refs_10_.refs_14_) | copy-start | bytes 3110404
  11.3 12.0 %copy-start.5 = (f32[1488,128]{1,0:T(8,128)S(1)}, f32[1488,128]{1,0:T(8,128)}, u32[]{:S(2)}) copy-start(f32[1488,128]{1,0:T(8,128)} %constant.38.clone.mode_ref) | copy-start | bytes 2285572
  12.7 20.4 %collective-permute-start.13 = (f32[632,128]{1,0:T(8,128)S(1)}, f32[632,128]{1,0:T(8,128)S(1)}, u32[]{:S(2)}, u32[]{:S(2)}) collective-permute-start(f32[632,128]{1,0:T(8,128)S(1)} %get-tuple-element.53), channel_id=1, source_target_pairs={{0,3},{1,2},{2,1},{3,0},{4,7},{5,6},{6,5},{7,4},{8,11},{9,10},{10,... | collective-permute-start | bytes 970760 | tf_op jit(solution)/shard_map/ppermute | solution.py:556
  16.9 11.0 %collective-permute-start.10 = (f32[376,128]{1,0:T(8,128)S(1)}, f32[376,128]{1,0:T(8,128)S(1)}, u32[]{:S(2)}, u32[]{:S(2)}) collective-permute-start(f32[376,128]{1,0:T(8,128)S(1)} %get-tuple-element.48), channel_id=1, source_target_pairs={{0,4},{4,8},{8,12},{12,16},{16,20},{20,24},{24,28},{1,5},{5,9},{9,... | collective-permute-start | bytes 577544 | tf_op jit(solution)/shard_map/ppermute | solution.py:623
  20.0 10.5 %collective-permute-start.11 = (f32[376,128]{1,0:T(8,128)S(1)}, f32[376,128]{1,0:T(8,128)S(1)}, u32[]{:S(2)}, u32[]{:S(2)}) collective-permute-start(f32[376,128]{1,0:T(8,128)S(1)} %get-tuple-element.49), channel_id=1, source_target_pairs={{4,0},{8,4},{12,8},{16,12},{20,16},{24,20},{28,24},{5,1},{9,5},{13... | collective-permute-start | bytes 577544 | tf_op jit(solution)/shard_map/ppermute | solution.py:624
  26.2 11.7 %collective-permute-start.7 = (f32[360,128]{1,0:T(8,128)S(1)}, f32[360,128]{1,0:T(8,128)S(1)}, u32[]{:S(2)}, u32[]{:S(2)}) collective-permute-start(f32[360,128]{1,0:T(8,128)S(1)} %get-tuple-element.44), channel_id=1, source_target_pairs={{0,2},{1,3},{2,0},{3,1},{4,6},{5,7},{6,4},{7,5},{8,10},{9,11},{10,... | collective-permute-start | bytes 552968 | tf_op jit(solution)/shard_map/ppermute | solution.py:556
  27.8 13.1 %collective-permute-start.8 = (f32[360,128]{1,0:T(8,128)S(1)}, f32[360,128]{1,0:T(8,128)S(1)}, u32[]{:S(2)}, u32[]{:S(2)}) collective-permute-start(f32[360,128]{1,0:T(8,128)S(1)} %get-tuple-element.45), channel_id=1, source_target_pairs={{0,3},{1,2},{2,1},{3,0},{4,7},{5,6},{6,5},{7,4},{8,11},{9,10},{10,... | collective-permute-start | bytes 552968 | tf_op jit(solution)/shard_map/ppermute | solution.py:556
  30.5 11.9 %collective-permute-start.9 = (f32[360,128]{1,0:T(8,128)S(1)}, f32[360,128]{1,0:T(8,128)S(1)}, u32[]{:S(2)}, u32[]{:S(2)}) collective-permute-start(f32[360,128]{1,0:T(8,128)S(1)} %get-tuple-element.46), channel_id=1, source_target_pairs={{0,1},{1,0},{2,3},{3,2},{4,5},{5,4},{6,7},{7,6},{8,9},{9,8},{10,11... | collective-permute-start | bytes 552968 | tf_op jit(solution)/shard_map/ppermute | solution.py:556
  36.2 6.8 %collective-permute-start.14 = (f32[360,128]{1,0:T(8,128)S(1)}, f32[360,128]{1,0:T(8,128)S(1)}, u32[]{:S(2)}, u32[]{:S(2)}) collective-permute-start(f32[360,128]{1,0:T(8,128)S(1)} %get-tuple-element.55), channel_id=1, source_target_pairs={{0,2},{1,3},{2,0},{3,1},{4,6},{5,7},{6,4},{7,5},{8,10},{9,11},{10,... | collective-permute-start | bytes 552968 | tf_op jit(solution)/shard_map/ppermute | solution.py:556
  37.7 9.3 %collective-permute-start.15 = (f32[360,128]{1,0:T(8,128)S(1)}, f32[360,128]{1,0:T(8,128)S(1)}, u32[]{:S(2)}, u32[]{:S(2)}) collective-permute-start(f32[360,128]{1,0:T(8,128)S(1)} %get-tuple-element.56), channel_id=1, source_target_pairs={{0,3},{1,2},{2,1},{3,0},{4,7},{5,6},{6,5},{7,4},{8,11},{9,10},{10,... | collective-permute-start | bytes 552968 | tf_op jit(solution)/shard_map/ppermute | solution.py:556
  37.9 9.1 %collective-permute-start.16 = (f32[360,128]{1,0:T(8,128)S(1)}, f32[360,128]{1,0:T(8,128)S(1)}, u32[]{:S(2)}, u32[]{:S(2)}) collective-permute-start(f32[360,128]{1,0:T(8,128)S(1)} %get-tuple-element.57), channel_id=1, source_target_pairs={{0,1},{1,0},{2,3},{3,2},{4,5},{5,4},{6,7},{7,6},{8,9},{9,8},{10,11... | collective-permute-start | bytes 552968 | tf_op jit(solution)/shard_map/ppermute | solution.py:556
  41.0 9.4 %collective-permute-start.17 = (f32[360,128]{1,0:T(8,128)S(1)}, f32[360,128]{1,0:T(8,128)S(1)}, u32[]{:S(2)}, u32[]{:S(2)}) collective-permute-start(f32[360,128]{1,0:T(8,128)S(1)} %get-tuple-element.60), channel_id=1, source_target_pairs={{0,2},{1,3},{2,0},{3,1},{4,6},{5,7},{6,4},{7,5},{8,10},{9,11},{10,... | collective-permute-start | bytes 552968 | tf_op jit(solution)/shard_map/ppermute | solution.py:556
  42.5 12.0 %collective-permute-start.18 = (f32[360,128]{1,0:T(8,128)S(1)}, f32[360,128]{1,0:T(8,128)S(1)}, u32[]{:S(2)}, u32[]{:S(2)}) collective-permute-start(f32[360,128]{1,0:T(8,128)S(1)} %get-tuple-element.61), channel_id=1, source_target_pairs={{0,3},{1,2},{2,1},{3,0},{4,7},{5,6},{6,5},{7,4},{8,11},{9,10},{10,... | collective-permute-start | bytes 552968 | tf_op jit(solution)/shard_map/ppermute | solution.py:556
  43.0 11.5 %collective-permute-start.19 = (f32[360,128]{1,0:T(8,128)S(1)}, f32[360,128]{1,0:T(8,128)S(1)}, u32[]{:S(2)}, u32[]{:S(2)}) collective-permute-start(f32[360,128]{1,0:T(8,128)S(1)} %get-tuple-element.62), channel_id=1, source_target_pairs={{0,1},{1,0},{2,3},{3,2},{4,5},{5,4},{6,7},{7,6},{8,9},{9,8},{10,11... | collective-permute-start | bytes 552968 | tf_op jit(solution)/shard_map/ppermute | solution.py:556
  (12 other events, 117.2 us)

commit v8 on v7

--- a/solution.py
+++ b/solution.py
@@ -497,6 +497,12 @@
     each_chunk(width, size, unpack)
 
 
+def out_cuts(width):
+    size = chunk_of(width)
+    chunks = width // size
+    return sorted({size * (chunks * part // 15) for part in (0, 6, 10, 13, 15)})
+
+
 def press_out_kernel(part, _, tile_ref, *refs):
     blocks, out_hbm, tile_out, sems = natural(refs[:4]), refs[4], refs[5], refs[6]
     rows, width, _ = tile_ref.shape
@@ -504,10 +510,10 @@
     size = chunk_of(width)
     masks = group_masks(size, part)
     low = lane_ids((size, LANES)) < LANES // 2
-    count = sems.shape[0]
+    cuts = out_cuts(width)
     copies = []
-    for piece in range(count):
-        begin, end = piece * width // count, (piece + 1) * width // count
+    for piece in range(len(cuts) - 1):
+        begin, end = cuts[piece], cuts[piece + 1]
 
         def unpack(start):
             lines = pl.ds(start + begin, size)
@@ -659,7 +665,7 @@
         [whole(block)] * 8,
         low_tile,
     )(*zonal_back, *merid_back)
-    pieces = next(n for n in (3, 5, 1) if width % (n * chunk_of(width)) == 0)
+    pieces = len(out_cuts(width)) - 1
     return call(
         functools.partial(press_out_kernel, part),
         f32(*state.shape),

time: 56.9 us -> 56.9 us (level)
  no operation moved by 1% of the time
where the time goes in v8:
time: 56.9 us; the launch traced here: 56 us
  starting transfers between devices  22.9 us (40%)
  Pallas kernels  17.4 us (31%)
  waiting for transfers between devices  13.2 us (23%)
  local copies, waits for them, and re-layouts  1.92 us (3%)
    ppermute x18, starting transfers between devices, send(): return lax.ppermute(block, 'lon', [(i, i ^ step) for i in range(4)])  16.5 us
    ppermute x18, waiting for transfers between devices, send(): return lax.ppermute(block, 'lon', [(i, i ^ step) for i in range(4)])  11.3 us
    ppermute x1, starting transfers between devices, packed_body(): lax.ppermute(to_south, 'lat', [(i + 1, i) for i in range(bands - 1)])  3.24 us
    ppermute x1, starting transfers between devices, packed_body(): lax.ppermute(to_north, 'lat', [(i, i + 1) for i in range(bands - 1)])  3.11 us
    pallas_call x1, Pallas kernels, packed_body(): call(functools.partial(merid_spec_kernel, bounds, part), [f32(*block)] *...  3.03 us
    pallas_call x1, Pallas kernels, packed_body(): call(functools.partial(press_back_kernel, bounds, part), [f32(*block)] *...  2.85 us
    pallas_call x1, Pallas kernels, packed_body(): call(functools.partial(zonal_spec_kernel, bounds, part), [f32(*block)] *...  2.79 us
    pallas_call x1, Pallas kernels, packed_body(): call(functools.partial(edge_spec_kernel, bounds, part, skip), f32(*spectr...  2.06 us
  transfers between devices with their start and end apart: 20, of which 6 were waited for; matrix products, arithmetic and copies ran while one was open for 0% of the time, Pallas kernels for 28%

profile of v8, /device:TPU:17, one launch (start us, length us, event | category | flops | bytes accessed | tf_op | source)
XLA Modules:
  0.0 56.0 jit_solution(2840807515294003314)
XLA Ops:
  0.0 1.8 %copy-done = f32[8,360,256]{2,1,0:T(8,128)S(1)} copy-done((f32[8,360,256]{2,1,0:T(8,128)S(1)}, f32[8,360,256]{2,1,0:T(8,128)}, u32[]{:S(2)}) %copy-start) | copy-done | bytes 2949144
  2.1 1.3 %collective-permute-start = (f32[184,128]{1,0:T(8,128)S(1)}, f32[184,128]{1,0:T(8,128)S(1)}, u32[]{:S(2)}, u32[]{:S(2)}) collective-permute-start(f32[184,128]{1,0:T(8,128)S(1)} %get-tuple-element.34), channel_id=1, source_target_pairs={{0,2},{1,3},{2,0},{3,1},{4,6},{5,7},{6,4},{7,5},{8,10},{9,11},{10,... | collective-permute-start | bytes 282632 | tf_op jit(solution)/shard_map/ppermute | solution.py:562
  3.4 1.1 %collective-permute-start.2 = (f32[184,128]{1,0:T(8,128)S(1)}, f32[184,128]{1,0:T(8,128)S(1)}, u32[]{:S(2)}, u32[]{:S(2)}) collective-permute-start(f32[184,128]{1,0:T(8,128)S(1)} %get-tuple-element.37), channel_id=1, source_target_pairs={{0,3},{1,2},{2,1},{3,0},{4,7},{5,6},{6,5},{7,4},{8,11},{9,10},{10,... | collective-permute-start | bytes 282632 | tf_op jit(solution)/shard_map/ppermute | solution.py:562
  4.5 1.0 %shard_map.156 = (f32[360,128]{1,0:T(8,128)S(1)}, f32[360,128]{1,0:T(8,128)S(1)}, f32[360,128]{1,0:T(8,128)S(1)}, f32[360,128]{1,0:T(8,128)S(1)}) custom-call(f32[8,360,256]{2,1,0:T(8,128)S(1)} %copy-done, f32[8,360,256]{2,1,0:T(8,128)S(1)} %copy-done), custom_call_target="tpu_custom_call" | custom-call | flops 2300000000 | bytes 7380000 | tf_op jit(solution)/shard_map/pallas_call | solution.py:604
  5.5 1.3 %collective-permute-start.4 = (f32[360,128]{1,0:T(8,128)S(1)}, f32[360,128]{1,0:T(8,128)S(1)}, u32[]{:S(2)}, u32[]{:S(2)}) collective-permute-start(f32[360,128]{1,0:T(8,128)S(1)} %get-tuple-element.40), channel_id=1, source_target_pairs={{0,2},{1,3},{2,0},{3,1},{4,6},{5,7},{6,4},{7,5},{8,10},{9,11},{10,... | collective-permute-start | bytes 552968 | tf_op jit(solution)/shard_map/ppermute | solution.py:562
  7.7 1.5 %shard_map.155 = (f32[632,128]{1,0:T(8,128)S(1)}, f32[632,128]{1,0:T(8,128)S(1)}, f32[632,128]{1,0:T(8,128)S(1)}, f32[632,128]{1,0:T(8,128)S(1)}, f32[8,360,128]{2,1,0:T(8,128)S(1)}) custom-call(f32[8,360,256]{2,1,0:T(8,128)S(1)} %copy-done, f32[8,360,256]{2,1,0:T(8,128)S(1)} %copy-done, f32[184,128]{1,0:T(8,128)S(1)} %collective-permute-done._.e2.refs_1_), custom_call_target="tpu_custom_call" | custom-call | flops 2300000000 | bytes 7380000 | tf_op jit(solution)/shard_map/pallas_call | solution.py:613
  9.8 1.5 %collective-permute-start.12 = (f32[632,128]{1,0:T(8,128)S(1)}, f32[632,128]{1,0:T(8,128)S(1)}, u32[]{:S(2)}, u32[]{:S(2)}) collective-permute-start(f32[632,128]{1,0:T(8,128)S(1)} %get-tuple-element.52), channel_id=1, source_target_pairs={{0,2},{1,3},{2,0},{3,1},{4,6},{5,7},{6,4},{7,5},{8,10},{9,11},{10,... | collective-permute-start | bytes 970760 | tf_op jit(solution)/shard_map/ppermute | solution.py:562
  12.7 2.4 %collective-permute-start.13 = (f32[632,128]{1,0:T(8,128)S(1)}, f32[632,128]{1,0:T(8,128)S(1)}, u32[]{:S(2)}, u32[]{:S(2)}) collective-permute-start(f32[632,128]{1,0:T(8,128)S(1)} %get-tuple-element.53), channel_id=1, source_target_pairs={{0,3},{1,2},{2,1},{3,0},{4,7},{5,6},{6,5},{7,4},{8,11},{9,10},{10,... | collective-permute-start | bytes 970760 | tf_op jit(solution)/shard_map/ppermute | solution.py:562
  15.1 1.8 %collective-permute-done.5.q3 = f32[360,128]{1,0:T(8,128)S(1)} collective-permute-done((f32[360,128]{1,0:T(8,128)S(1)}, f32[360,128]{1,0:T(8,128)S(1)}, u32[]{:S(2)}, u32[]{:S(2)}) %collective-permute-start.5) | collective-permute-done | bytes 184352 | tf_op jit(solution)/shard_map/ppermute | solution.py:562
  16.9 3.1 %collective-permute-start.10 = (f32[376,128]{1,0:T(8,128)S(1)}, f32[376,128]{1,0:T(8,128)S(1)}, u32[]{:S(2)}, u32[]{:S(2)}) collective-permute-start(f32[376,128]{1,0:T(8,128)S(1)} %get-tuple-element.48), channel_id=1, source_target_pairs={{0,4},{4,8},{8,12},{12,16},{16,20},{20,24},{24,28},{1,5},{5,9},{9,... | collective-permute-start | bytes 577544 | tf_op jit(solution)/shard_map/ppermute | solution.py:629
  20.0 3.2 %collective-permute-start.11 = (f32[376,128]{1,0:T(8,128)S(1)}, f32[376,128]{1,0:T(8,128)S(1)}, u32[]{:S(2)}, u32[]{:S(2)}) collective-permute-start(f32[376,128]{1,0:T(8,128)S(1)} %get-tuple-element.49), channel_id=1, source_target_pairs={{4,0},{8,4},{12,8},{16,12},{20,16},{24,20},{28,24},{5,1},{9,5},{13... | collective-permute-start | bytes 577544 | tf_op jit(solution)/shard_map/ppermute | solution.py:630
  23.4 2.8 %shard_map.157 = (f32[360,128]{1,0:T(8,128)S(1)}, f32[360,128]{1,0:T(8,128)S(1)}, f32[360,128]{1,0:T(8,128)S(1)}, f32[360,128]{1,0:T(8,128)S(1)}, f32[1488,128]{1,0:T(8,128)S(1)}) custom-call(s32[8]{0:T(128)S(1)} %copy-done.14, s32[8]{0:T(128)S(1)} %copy-done.15, f32[1488,128]{1,0:T(8,128)S(1)} %copy-done.5, ...), custom_call_target="tpu_custom_call" | custom-call | flops 2300000000 | bytes 7380000 | tf_op jit(solution)/shard_map/pallas_call | solution.py:632
  26.2 1.6 %collective-permute-start.7 = (f32[360,128]{1,0:T(8,128)S(1)}, f32[360,128]{1,0:T(8,128)S(1)}, u32[]{:S(2)}, u32[]{:S(2)}) collective-permute-start(f32[360,128]{1,0:T(8,128)S(1)} %get-tuple-element.44), channel_id=1, source_target_pairs={{0,2},{1,3},{2,0},{3,1},{4,6},{5,7},{6,4},{7,5},{8,10},{9,11},{10,... | collective-permute-start | bytes 552968 | tf_op jit(solution)/shard_map/ppermute | solution.py:562
  28.7 1.9 %collective-permute-done.11.north_ref = f32[376,128]{1,0:T(8,128)S(1)} collective-permute-done((f32[376,128]{1,0:T(8,128)S(1)}, f32[376,128]{1,0:T(8,128)S(1)}, u32[]{:S(2)}, u32[]{:S(2)}) %collective-permute-start.11) | collective-permute-done | bytes 192544 | tf_op jit(solution)/shard_map/ppermute | solution.py:630
  31.0 2.1 %shard_map.159.edge_ref = f32[1488,128]{1,0:T(8,128)S(1)} custom-call(s32[8]{0:T(128)S(1)} %copy-done.14, s32[8]{0:T(128)S(1)} %copy-done.15, f32[1488,128]{1,0:T(8,128)S(1)} %copy-done.5, f32[376,128]{1,0:T(8,128)S(1)} %collective-permute-done.10.south_ref, f32[376,128]{1,0:T(8,128)S(1)} %collective-permute-done.11.north_ref, ...), custom_call_target="tpu_custom_call" | custom-call | flops 2300000000 | bytes 7380000 | tf_op jit(solution)/shard_map/pallas_call | solution.py:639
  33.1 3.0 %shard_map.160 = (f32[360,128]{1,0:T(8,128)S(1)}, f32[360,128]{1,0:T(8,128)S(1)}, f32[360,128]{1,0:T(8,128)S(1)}, f32[360,128]{1,0:T(8,128)S(1)}, f32[1488,128]{1,0:T(8,128)S(1)}) custom-call(s32[8]{0:T(128)S(1)} %copy-done.14, s32[8]{0:T(128)S(1)} %copy-done.15, f32[1488,128]{1,0:T(8,128)S(1)} %copy-done.5, f32[1488,128]{1,0:T(8,128)S(1)} %shard_map.159.edge_ref, ...), custom_call_target="tpu_custom_call" | custom-call | flops 2300000000 | bytes 7380000 | tf_op jit(solution)/shard_map/pallas_call | solution.py:646
  36.2 1.5 %collective-permute-start.14 = (f32[360,128]{1,0:T(8,128)S(1)}, f32[360,128]{1,0:T(8,128)S(1)}, u32[]{:S(2)}, u32[]{:S(2)}) collective-permute-start(f32[360,128]{1,0:T(8,128)S(1)} %get-tuple-element.55), channel_id=1, source_target_pairs={{0,2},{1,3},{2,0},{3,1},{4,6},{5,7},{6,4},{7,5},{8,10},{9,11},{10,... | collective-permute-start | bytes 552968 | tf_op jit(solution)/shard_map/ppermute | solution.py:562
  38.1 2.8 %shard_map.162 = (f32[360,128]{1,0:T(8,128)S(1)}, f32[360,128]{1,0:T(8,128)S(1)}, f32[360,128]{1,0:T(8,128)S(1)}, f32[360,128]{1,0:T(8,128)S(1)}) custom-call(s32[8]{0:T(128)S(1)} %copy-done.14, s32[8]{0:T(128)S(1)} %copy-done.15, f32[1488,128]{1,0:T(8,128)S(1)} %copy-done.5, f32[1488,128]{1,0:T(8,128)S(1)} %get-tuple-element.50._.zonal_ref, ...), custom_call_target="tpu_custom_call" | custom-call | flops 2300000000 | bytes 7380000 | tf_op jit(solution)/shard_map/pallas_call | solution.py:654
  41.0 1.5 %collective-permute-start.17 = (f32[360,128]{1,0:T(8,128)S(1)}, f32[360,128]{1,0:T(8,128)S(1)}, u32[]{:S(2)}, u32[]{:S(2)}) collective-permute-start(f32[360,128]{1,0:T(8,128)S(1)} %get-tuple-element.60), channel_id=1, source_target_pairs={{0,2},{1,3},{2,0},{3,1},{4,6},{5,7},{6,4},{7,5},{8,10},{9,11},{10,... | collective-permute-start | bytes 552968 | tf_op jit(solution)/shard_map/ppermute | solution.py:562
  43.7 3.3 %collective-permute-done.15.refs_6_ = f32[360,128]{1,0:T(8,128)S(1)} collective-permute-done((f32[360,128]{1,0:T(8,128)S(1)}, f32[360,128]{1,0:T(8,128)S(1)}, u32[]{:S(2)}, u32[]{:S(2)}) %collective-permute-start.15) | collective-permute-done | bytes 184352 | tf_op jit(solution)/shard_map/ppermute | solution.py:562
  46.9 1.9 %shard_map.161._ = f32[8,360,256]{2,1,0:T(8,128)} custom-call(f32[360,128]{1,0:T(8,128)S(1)} %get-tuple-element.43.refs_0_, f32[360,128]{1,0:T(8,128)S(1)} %collective-permute-done.7.refs_1_, f32[360,128]{1,0:T(8,128)S(1)} %collective-permute-done.8.refs_2_, f32[360,128]{1,0:T(8,128)S(1)} %collective-permute-done.9.refs_3_, ...), custom_call_target="tpu_custom_call" | custom-call | flops 2300000000 | bytes 7380000 | tf_op jit(solution)/shard_map/pallas_call | solution.py:662
  48.9 1.5 %collective-permute-done.17.refs_1_ = f32[360,128]{1,0:T(8,128)S(1)} collective-permute-done((f32[360,128]{1,0:T(8,128)S(1)}, f32[360,128]{1,0:T(8,128)S(1)}, u32[]{:S(2)}, u32[]{:S(2)}) %collective-permute-start.17) | collective-permute-done | bytes 184352 | tf_op jit(solution)/shard_map/ppermute | solution.py:562
  50.4 4.1 %collective-permute-done.18.refs_2_ = f32[360,128]{1,0:T(8,128)S(1)} collective-permute-done((f32[360,128]{1,0:T(8,128)S(1)}, f32[360,128]{1,0:T(8,128)S(1)}, u32[]{:S(2)}, u32[]{:S(2)}) %collective-permute-start.18) | collective-permute-done | bytes 184352 | tf_op jit(solution)/shard_map/ppermute | solution.py:562
  54.4 1.4 %shard_map.163 = f32[8,360,256]{2,1,0:T(8,128)} custom-call(f32[8,360,256]{2,1,0:T(8,128)} %shard_map.161._, f32[8,360,128]{2,1,0:T(8,128)S(1)} %get-tuple-element.47.refs_4_.tile_ref, f32[360,128]{1,0:T(8,128)S(1)} %get-tuple-element.59.refs_0_, f32[360,128]{1,0:T(8,128)S(1)} %collective-permute-done.17.refs_1_, ...), custom_call_target="tpu_custom_call", output_to_operand_aliasing={{}: (0, {})} | custom-call | flops 2300000000 | bytes 7380000 | tf_op jit(solution)/shard_map/pallas_call | solution.py:669
  (58 shorter events, 6.1 us)
Async XLA Ops:
  2.1 5.6 %collective-permute-start = (f32[184,128]{1,0:T(8,128)S(1)}, f32[184,128]{1,0:T(8,128)S(1)}, u32[]{:S(2)}, u32[]{:S(2)}) collective-permute-start(f32[184,128]{1,0:T(8,128)S(1)} %get-tuple-element.34), channel_id=1, source_target_pairs={{0,2},{1,3},{2,0},{3,1},{4,6},{5,7},{6,4},{7,5},{8,10},{9,11},{10,... | collective-permute-start | bytes 282632 | tf_op jit(solution)/shard_map/ppermute | solution.py:562
  3.4 5.8 %collective-permute-start.2 = (f32[184,128]{1,0:T(8,128)S(1)}, f32[184,128]{1,0:T(8,128)S(1)}, u32[]{:S(2)}, u32[]{:S(2)}) collective-permute-start(f32[184,128]{1,0:T(8,128)S(1)} %get-tuple-element.37), channel_id=1, source_target_pairs={{0,3},{1,2},{2,1},{3,0},{4,7},{5,6},{6,5},{7,4},{8,11},{9,10},{10,... | collective-permute-start | bytes 282632 | tf_op jit(solution)/shard_map/ppermute | solution.py:562
  4.5 5.3 %collective-permute-start.3 = (f32[184,128]{1,0:T(8,128)S(1)}, f32[184,128]{1,0:T(8,128)S(1)}, u32[]{:S(2)}, u32[]{:S(2)}) collective-permute-start(f32[184,128]{1,0:T(8,128)S(1)} %get-tuple-element.38), channel_id=1, source_target_pairs={{0,1},{1,0},{2,3},{3,2},{4,5},{5,4},{6,7},{7,6},{8,9},{9,8},{10,11... | collective-permute-start | bytes 282632 | tf_op jit(solution)/shard_map/ppermute | solution.py:562
  5.5 7.3 %collective-permute-start.4 = (f32[360,128]{1,0:T(8,128)S(1)}, f32[360,128]{1,0:T(8,128)S(1)}, u32[]{:S(2)}, u32[]{:S(2)}) collective-permute-start(f32[360,128]{1,0:T(8,128)S(1)} %get-tuple-element.40), channel_id=1, source_target_pairs={{0,2},{1,3},{2,0},{3,1},{4,6},{5,7},{6,4},{7,5},{8,10},{9,11},{10,... | collective-permute-start | bytes 552968 | tf_op jit(solution)/shard_map/ppermute | solution.py:562
  6.8 10.1 %collective-permute-start.5 = (f32[360,128]{1,0:T(8,128)S(1)}, f32[360,128]{1,0:T(8,128)S(1)}, u32[]{:S(2)}, u32[]{:S(2)}) collective-permute-start(f32[360,128]{1,0:T(8,128)S(1)} %get-tuple-element.41), channel_id=1, source_target_pairs={{0,3},{1,2},{2,1},{3,0},{4,7},{5,6},{6,5},{7,4},{8,11},{9,10},{10,... | collective-permute-start | bytes 552968 | tf_op jit(solution)/shard_map/ppermute | solution.py:562
  7.7 12.3 %collective-permute-start.6 = (f32[360,128]{1,0:T(8,128)S(1)}, f32[360,128]{1,0:T(8,128)S(1)}, u32[]{:S(2)}, u32[]{:S(2)}) collective-permute-start(f32[360,128]{1,0:T(8,128)S(1)} %get-tuple-element.42), channel_id=1, source_target_pairs={{0,1},{1,0},{2,3},{3,2},{4,5},{5,4},{6,7},{7,6},{8,9},{9,8},{10,11... | collective-permute-start | bytes 552968 | tf_op jit(solution)/shard_map/ppermute | solution.py:562
  9.2 14.1 %collective-permute-start.1 = (f32[632,128]{1,0:T(8,128)S(1)}, f32[632,128]{1,0:T(8,128)S(1)}, u32[]{:S(2)}, u32[]{:S(2)}) collective-permute-start(f32[632,128]{1,0:T(8,128)S(1)} %get-tuple-element.35), channel_id=1, source_target_pairs={{0,1},{1,0},{2,3},{3,2},{4,5},{5,4},{6,7},{7,6},{8,9},{9,8},{10,11... | collective-permute-start | bytes 970760 | tf_op jit(solution)/shard_map/ppermute | solution.py:562
  9.8 23.3 %collective-permute-start.12 = (f32[632,128]{1,0:T(8,128)S(1)}, f32[632,128]{1,0:T(8,128)S(1)}, u32[]{:S(2)}, u32[]{:S(2)}) collective-permute-start(f32[632,128]{1,0:T(8,128)S(1)} %get-tuple-element.52), channel_id=1, source_target_pairs={{0,2},{1,3},{2,0},{3,1},{4,6},{5,7},{6,4},{7,5},{8,10},{9,11},{10,... | collective-permute-start | bytes 970760 | tf_op jit(solution)/shard_map/ppermute | solution.py:562
  11.2 12.0 %copy-start.2 = (bf16[720,720]{1,0:T(8,128)(2,1)S(1)}, bf16[720,720]{1,0:T(8,128)(2,1)}, u32[]{:S(2)}) copy-start(bf16[720,720]{1,0:T(8,128)(2,1)} %constant.30.clone.refs_4_.refs_8_) | copy-start | bytes 3110404
  11.3 12.0 %copy-start.3 = (bf16[720,720]{1,0:T(8,128)(2,1)S(1)}, bf16[720,720]{1,0:T(8,128)(2,1)}, u32[]{:S(2)}) copy-start(bf16[720,720]{1,0:T(8,128)(2,1)} %constant.37.clone.refs_11_.refs_15_) | copy-start | bytes 3110404
  11.3 12.0 %copy-start.4 = (bf16[720,720]{1,0:T(8,128)(2,1)S(1)}, bf16[720,720]{1,0:T(8,128)(2,1)}, u32[]{:S(2)}) copy-start(bf16[720,720]{1,0:T(8,128)(2,1)} %constant.36.clone.refs_10_.refs_14_) | copy-start | bytes 3110404
  11.3 12.0 %copy-start.5 = (f32[1488,128]{1,0:T(8,128)S(1)}, f32[1488,128]{1,0:T(8,128)}, u32[]{:S(2)}) copy-start(f32[1488,128]{1,0:T(8,128)} %constant.38.clone.mode_ref) | copy-start | bytes 2285572
  12.7 20.4 %collective-permute-start.13 = (f32[632,128]{1,0:T(8,128)S(1)}, f32[632,128]{1,0:T(8,128)S(1)}, u32[]{:S(2)}, u32[]{:S(2)}) collective-permute-start(f32[632,128]{1,0:T(8,128)S(1)} %get-tuple-element.53), channel_id=1, source_target_pairs={{0,3},{1,2},{2,1},{3,0},{4,7},{5,6},{6,5},{7,4},{8,11},{9,10},{10,... | collective-permute-start | bytes 970760 | tf_op jit(solution)/shard_map/ppermute | solution.py:562
  16.9 11.0 %collective-permute-start.10 = (f32[376,128]{1,0:T(8,128)S(1)}, f32[376,128]{1,0:T(8,128)S(1)}, u32[]{:S(2)}, u32[]{:S(2)}) collective-permute-start(f32[376,128]{1,0:T(8,128)S(1)} %get-tuple-element.48), channel_id=1, source_target_pairs={{0,4},{4,8},{8,12},{12,16},{16,20},{20,24},{24,28},{1,5},{5,9},{9,... | collective-permute-start | bytes 577544 | tf_op jit(solution)/shard_map/ppermute | solution.py:629
  20.0 10.5 %collective-permute-start.11 = (f32[376,128]{1,0:T(8,128)S(1)}, f32[376,128]{1,0:T(8,128)S(1)}, u32[]{:S(2)}, u32[]{:S(2)}) collective-permute-start(f32[376,128]{1,0:T(8,128)S(1)} %get-tuple-element.49), channel_id=1, source_target_pairs={{4,0},{8,4},{12,8},{16,12},{20,16},{24,20},{28,24},{5,1},{9,5},{13... | collective-permute-start | bytes 577544 | tf_op jit(solution)/shard_map/ppermute | solution.py:630
  26.2 11.7 %collective-permute-start.7 = (f32[360,128]{1,0:T(8,128)S(1)}, f32[360,128]{1,0:T(8,128)S(1)}, u32[]{:S(2)}, u32[]{:S(2)}) collective-permute-start(f32[360,128]{1,0:T(8,128)S(1)} %get-tuple-element.44), channel_id=1, source_target_pairs={{0,2},{1,3},{2,0},{3,1},{4,6},{5,7},{6,4},{7,5},{8,10},{9,11},{10,... | collective-permute-start | bytes 552968 | tf_op jit(solution)/shard_map/ppermute | solution.py:562
  27.8 13.1 %collective-permute-start.8 = (f32[360,128]{1,0:T(8,128)S(1)}, f32[360,128]{1,0:T(8,128)S(1)}, u32[]{:S(2)}, u32[]{:S(2)}) collective-permute-start(f32[360,128]{1,0:T(8,128)S(1)} %get-tuple-element.45), channel_id=1, source_target_pairs={{0,3},{1,2},{2,1},{3,0},{4,7},{5,6},{6,5},{7,4},{8,11},{9,10},{10,... | collective-permute-start | bytes 552968 | tf_op jit(solution)/shard_map/ppermute | solution.py:562
  30.5 11.9 %collective-permute-start.9 = (f32[360,128]{1,0:T(8,128)S(1)}, f32[360,128]{1,0:T(8,128)S(1)}, u32[]{:S(2)}, u32[]{:S(2)}) collective-permute-start(f32[360,128]{1,0:T(8,128)S(1)} %get-tuple-element.46), channel_id=1, source_target_pairs={{0,1},{1,0},{2,3},{3,2},{4,5},{5,4},{6,7},{7,6},{8,9},{9,8},{10,11... | collective-permute-start | bytes 552968 | tf_op jit(solution)/shard_map/ppermute | solution.py:562
  36.2 6.8 %collective-permute-start.14 = (f32[360,128]{1,0:T(8,128)S(1)}, f32[360,128]{1,0:T(8,128)S(1)}, u32[]{:S(2)}, u32[]{:S(2)}) collective-permute-start(f32[360,128]{1,0:T(8,128)S(1)} %get-tuple-element.55), channel_id=1, source_target_pairs={{0,2},{1,3},{2,0},{3,1},{4,6},{5,7},{6,4},{7,5},{8,10},{9,11},{10,... | collective-permute-start | bytes 552968 | tf_op jit(solution)/shard_map/ppermute | solution.py:562
  37.7 9.3 %collective-permute-start.15 = (f32[360,128]{1,0:T(8,128)S(1)}, f32[360,128]{1,0:T(8,128)S(1)}, u32[]{:S(2)}, u32[]{:S(2)}) collective-permute-start(f32[360,128]{1,0:T(8,128)S(1)} %get-tuple-element.56), channel_id=1, source_target_pairs={{0,3},{1,2},{2,1},{3,0},{4,7},{5,6},{6,5},{7,4},{8,11},{9,10},{10,... | collective-permute-start | bytes 552968 | tf_op jit(solution)/shard_map/ppermute | solution.py:562
  37.9 9.1 %collective-permute-start.16 = (f32[360,128]{1,0:T(8,128)S(1)}, f32[360,128]{1,0:T(8,128)S(1)}, u32[]{:S(2)}, u32[]{:S(2)}) collective-permute-start(f32[360,128]{1,0:T(8,128)S(1)} %get-tuple-element.57), channel_id=1, source_target_pairs={{0,1},{1,0},{2,3},{3,2},{4,5},{5,4},{6,7},{7,6},{8,9},{9,8},{10,11... | collective-permute-start | bytes 552968 | tf_op jit(solution)/shard_map/ppermute | solution.py:562
  41.0 9.4 %collective-permute-start.17 = (f32[360,128]{1,0:T(8,128)S(1)}, f32[360,128]{1,0:T(8,128)S(1)}, u32[]{:S(2)}, u32[]{:S(2)}) collective-permute-start(f32[360,128]{1,0:T(8,128)S(1)} %get-tuple-element.60), channel_id=1, source_target_pairs={{0,2},{1,3},{2,0},{3,1},{4,6},{5,7},{6,4},{7,5},{8,10},{9,11},{10,... | collective-permute-start | bytes 552968 | tf_op jit(solution)/shard_map/ppermute | solution.py:562
  42.5 12.0 %collective-permute-start.18 = (f32[360,128]{1,0:T(8,128)S(1)}, f32[360,128]{1,0:T(8,128)S(1)}, u32[]{:S(2)}, u32[]{:S(2)}) collective-permute-start(f32[360,128]{1,0:T(8,128)S(1)} %get-tuple-element.61), channel_id=1, source_target_pairs={{0,3},{1,2},{2,1},{3,0},{4,7},{5,6},{6,5},{7,4},{8,11},{9,10},{10,... | collective-permute-start | bytes 552968 | tf_op jit(solution)/shard_map/ppermute | solution.py:562
  43.0 11.5 %collective-permute-start.19 = (f32[360,128]{1,0:T(8,128)S(1)}, f32[360,128]{1,0:T(8,128)S(1)}, u32[]{:S(2)}, u32[]{:S(2)}) collective-permute-start(f32[360,128]{1,0:T(8,128)S(1)} %get-tuple-element.62), channel_id=1, source_target_pairs={{0,1},{1,0},{2,3},{3,2},{4,5},{5,4},{6,7},{7,6},{8,9},{9,8},{10,11... | collective-permute-start | bytes 552968 | tf_op jit(solution)/shard_map/ppermute | solution.py:562
  (12 other events, 117.2 us)
